TPU v7x, 256 devices: a whole 4x4x8 slice. The times are simulated.
256 devices in a mesh: space: 64 (over x, y, z_lo, core), tm: 4 (over z_hi).
Axes of the slice: x: 4, y: 4, z: 8 (z_hi: 4, z_lo: 2; z = z_hi * 2 + z_lo), core: 2. Of those that a mesh axis runs over, the one named last changes fastest.
Arguments:
- snapshots: bfloat16 [2048, 3, 49152], P('tm', None, 'space'), may hold values from -15 to 15
- tail: bfloat16 [64, 3, 49152], P(None, None, 'space'), may hold values from -15 to 15
- volume: float32 [49152], P('space'), may hold values from 0.3 to 3
Outputs:
- gram: float32 [64, 2, 32, 32], P('tm')
- modes: bfloat16 [64, 2, 32, 3, 49152], P('tm', None, None, None, 'space')
All inputs are finite; a program needn't handle non-finite values.
Results may differ from a plain program's by a relative error of at most 0.00055.
The roundings to bfloat16 on the way count: a program that leaves them out, or rounds other values in their place, can miss the bound.
Values may be sent and summed in bfloat16 or wider, within the bound.
No kernel may reach another device: no remote copies, remote signals or barrier semaphores. Data moves between devices by JAX's collectives and lax.ppermute only.
A program may use at most 128 MiB of HBM per device.

v0:
```python
import jax
import jax.numpy as jnp
from jax import lax
from jax.sharding import PartitionSpec as P

NB = 32
NFFT = 128
HOP = 64


def from_behind(block, axis, distance):
    devices = range(lax.axis_size(axis))
    route = [(i - distance, i) for i in devices if i - distance in devices]
    return lax.ppermute(block, axis, route)


def transform_table():
    times = jnp.arange(NFFT, dtype=jnp.float32)
    freq = jnp.arange(NFFT // 2, dtype=jnp.float32)[:, None]
    window = 0.5 - 0.5 * jnp.cos(2.0 * jnp.pi * times / NFFT)
    window = window / jnp.sqrt(jnp.sum(window * window))
    angles = 2.0 * jnp.pi * freq * times[None, :] / NFFT
    real_rows = window * jnp.cos(angles)
    imag_rows = -window * jnp.sin(angles)
    nyquist = window * jnp.cos(jnp.pi * times)
    imag_rows = jnp.where(freq == 0.0, nyquist[None, :], imag_rows)
    return jnp.stack([real_rows, imag_rows], axis=1).reshape(NFFT, NFFT).astype(jnp.bfloat16)


def half_transform(rows_table, halves):
    first = jnp.einsum(
        "rt,htx->hrx", rows_table[:, :HOP], halves[:-1], preferred_element_type=jnp.float32
    )
    second = jnp.einsum(
        "rt,htx->hrx", rows_table[:, HOP:], halves[1:], preferred_element_type=jnp.float32
    )
    return (first + second).astype(jnp.bfloat16)


def assemble(total, first_slot):
    count = total.shape[0]
    is_zero = (first_slot + jnp.arange(count, dtype=jnp.int32) == 0)[:, None, None]
    gram_real = total[:, 0] + total[:, 1]
    gram_imag = total[:, 2] - jnp.swapaxes(total[:, 2], 1, 2)
    mat_a = jnp.where(is_zero, total[:, 0], gram_real)
    mat_b = jnp.where(is_zero, total[:, 1], gram_real)
    mat_i = jnp.where(is_zero, jnp.zeros_like(gram_imag), gram_imag)
    gram = jnp.stack([mat_a, jnp.where(is_zero, total[:, 1], gram_imag)], axis=1)
    norm_a = jnp.sqrt(jnp.sum(mat_a * mat_a + mat_i * mat_i, axis=(1, 2)) + 1e-06)[:, None, None]
    norm_b = jnp.sqrt(jnp.sum(mat_b * mat_b + mat_i * mat_i, axis=(1, 2)) + 1e-06)[:, None, None]
    scaled = (
        (mat_a / norm_a).astype(jnp.bfloat16),
        (mat_i / norm_a).astype(jnp.bfloat16),
        (mat_b / norm_b).astype(jnp.bfloat16),
        (mat_i / norm_b).astype(jnp.bfloat16),
    )
    return (gram, scaled)


def body(snapshots, tail, volume):
    table = transform_table()
    tm_count = lax.axis_size("tm")
    tm_rank = lax.axis_index("tm")
    points = snapshots.shape[2]
    flat = snapshots.reshape(snapshots.shape[0], 3 * points)
    tail_flat = tail.reshape(HOP, 3 * points)
    following = from_behind(flat[:HOP], "tm", -1)
    following = jnp.where(tm_rank == tm_count - 1, tail_flat, following)
    halves = jnp.concatenate([flat, following], 0).reshape(-1, HOP, 3 * points)
    local = half_transform(table, halves)
    spectra = lax.all_to_all(local, "tm", split_axis=1, concat_axis=0, tiled=True)
    slots_here = spectra.shape[1] // 2
    parts = spectra.reshape(NB, slots_here, 2, 3 * points)
    real_part = parts[:, :, 0]
    imag_part = parts[:, :, 1]
    weights = jnp.tile(volume, 3)
    w_real = (real_part * weights).astype(jnp.bfloat16)
    w_imag = (imag_part * weights).astype(jnp.bfloat16)
    terms = jnp.stack(
        [
            jnp.einsum("isx,jsx->sij", w_real, real_part, preferred_element_type=jnp.float32),
            jnp.einsum("isx,jsx->sij", w_imag, imag_part, preferred_element_type=jnp.float32),
            jnp.einsum("isx,jsx->sij", w_real, imag_part, preferred_element_type=jnp.float32),
        ],
        axis=1,
    )
    summed = lax.psum(terms, "space")
    total = summed / (NB * 3 * points * lax.axis_size("space"))
    gram, scaled = assemble(total, tm_rank * slots_here)
    ga, gia, gb, gib = scaled
    first = jnp.einsum(
        "skj,jsx->skx", ga, real_part, preferred_element_type=jnp.float32
    ) + jnp.einsum("skj,jsx->skx", gia, imag_part, preferred_element_type=jnp.float32)
    second = jnp.einsum(
        "skj,jsx->skx", gb, imag_part, preferred_element_type=jnp.float32
    ) - jnp.einsum("skj,jsx->skx", gib, real_part, preferred_element_type=jnp.float32)
    modes = jnp.stack([first, second], axis=1).astype(jnp.bfloat16)
    return (gram, modes.reshape(slots_here, 2, NB, 3, points))


def solution(mesh):
    placed = (P("tm", None, "space"), P(None, None, "space"), P("space"))
    return jax.shard_map(
        body,
        mesh=mesh,
        in_specs=placed,
        out_specs=(P("tm", None, None, None), P("tm", None, None, None, "space")),
        check_vma=False,
    )
```

profile of v0, /device:TPU:1, one launch (start us, length us, event | category | flops | bytes accessed | tf_op | source)
XLA Modules:
  0.0 739.6 jit_solution(6089579620773087655)
XLA Ops:
  7.2 1.0 slice_bitcast_fusion.16
  8.2 0.7 copy.68
  8.9 1.3 collective-permute-start
  10.2 0.7 multiply_reduce_fusion
  11.5 0.1 broadcast_divide_fusion
  11.6 0.1 cosine_multiply_fusion
  11.7 3.7 copy.43
  15.4 0.0 copy-start.6
  15.4 4.3 copy.44
  19.7 4.5 slice.42
  24.2 0.0 copy-done.6
  24.2 0.3 copy.61
  24.6 0.9 multiply_convert_fusion.11
  25.5 1.0 fusion.24
  26.5 0.1 pad_maximum_fusion.4
  26.6 0.0 copy-start.4
  26.6 0.0 copy-start.1
  26.6 6.8 fusion.23
  33.4 0.0 copy-done.4
  33.4 0.0 collective-permute-done
  33.4 1.3 copy.48
  34.7 0.1 bitcast_select_fusion
  34.8 0.0 copy-done.1
  34.8 0.0 copy-start.5
  34.8 2.9 pad_maximum_fusion.1
  37.7 3.0 copy.49
  40.7 0.0 copy-done.5
  40.7 5.1 fusion
  45.9 4.8 copy.52
  50.6 10.7 %all-to-all-start = ((bf16[8,128,2304]{2,0,1:T(8,128)(2,1)}), bf16[8,128,2304]{2,0,1:T(8,128)(2,1)}, u32[]{:S(2)}, u32[]{:S(2)}) async-start(bf16[8,128,2304]{2,0,1:T(8,128)(2,1)} %copy.52), calls=%async_computation | async-start | bytes 9437184 | tf_op jit(solution)/shard_map/all_to_all | solution.py:71
  61.4 0.0 all-reduce.2.cloned.1.call-start
  61.4 0.0 copy-done.7
  61.4 97.8 %all-to-all-done = bf16[8,128,2304]{2,0,1:T(8,128)(2,1)} async-done(((bf16[8,128,2304]{2,0,1:T(8,128)(2,1)}), bf16[8,128,2304]{2,0,1:T(8,128)(2,1)}, u32[]{:S(2)}, u32[]{:S(2)}) %all-to-all-start) | async-done | bytes 4718624 | tf_op jit(solution)/shard_map/all_to_all | solution.py:71
  159.2 2.9 copy.54
  162.1 0.0 copy-start
  162.1 0.8 fusion.11
  162.9 0.8 fusion.12
  163.7 0.6 copy-done
  164.3 0.8 fusion.13
  165.1 1.0 pad_maximum_fusion.2
  166.1 0.0 all-reduce.2.cloned.1.call-update
  166.1 535.4 %all-reduce.2.cloned.1.call-done = f32[16,3,32,32]{3,2,0,1:T(8,128)} async-done(((f32[16,3,32,32]{3,2,0,1:T(8,128)}), f32[16,3,32,32]{3,2,0,1:T(8,128)}) %all-reduce.2.cloned.1.call-update) | async-done | bytes 196624 | tf_op jit(solution)/shard_map/psum | solution.py:87
  701.6 1.2 broadcast_multiply_fusion
  702.8 0.8 add_select_fusion
  703.6 0.1 copy.57
  703.7 0.0 slice-start
  703.7 0.3 add_reduce_fusion.1
  704.0 0.0 slice-start.1
  704.0 2.7 fusion.9
  706.7 0.8 fusion.14
  707.5 0.0 slice-done
  707.5 0.0 slice-done.1
  707.5 0.9 fusion.1
  708.4 3.9 stack.41
  712.3 2.5 fusion.10
  714.8 2.5 fusion.2
  717.3 3.6 stack.42
  720.9 7.6 %pad_maximum_fusion = bf16[16,2,32,3,768]{4,3,2,0,1:T(4,128)(2,1)S(1)} fusion(bf16[16,1,32,3,768]{4,3,2,0,1:T(4,128)(2,1)} %stack.42, bf16[16,1,32,3,768]{4,3,2,0,1:T(4,128)(2,1)} %stack.41), kind=kLoop, calls=%fused_computation.2 | loop fusion | flops 2359296 | bytes 9437184 | tf_op jit(solution)/shard_map/stack | solution.py:97
  728.4 0.0 copy-start.2
  728.5 0.0 copy-start.3
  728.5 3.4 copy.59
  731.8 0.0 copy-done.2
  731.8 0.0 copy-done.3
  731.9 0.8 copy.58
  (10 shorter events, 0.1 us)
Async XLA Ops:
  8.9 24.5 %collective-permute-start = (bf16[64,2304]{1,0:T(8,128)(2,1)}, bf16[64,2304]{1,0:T(8,128)(2,1)}, u32[]{:S(2)}, u32[]{:S(2)}) collective-permute-start(bf16[64,2304]{1,0:T(8,128)(2,1)} %bitcast.29), channel_id=1, source_target_pairs={{1,0},{2,1},{3,2},{5,4},{6,5},{7,6},{9,8},{10,9},{11,10},{13,12},{... | collective-permute-start | bytes 884744 | tf_op jit(solution)/shard_map/ppermute | solution.py:14
  15.4 8.9 %copy-start.6 = (bf16[64,3,768]{2,0,1:T(8,128)(2,1)S(1)}, bf16[64,3,768]{2,0,1:T(8,128)(2,1)}, u32[]{:S(2)}) copy-start(bf16[64,3,768]{2,0,1:T(8,128)(2,1)} %param.4) | copy-start | bytes 884740
  26.6 6.8 copy-start.4
  26.6 8.2 %copy-start.1 = (bf16[512,3,768]{0,2,1:T(8,128)(2,1)S(1)}, bf16[512,3,768]{0,2,1:T(8,128)(2,1)}, u32[]{:S(2)}) copy-start(bf16[512,3,768]{0,2,1:T(8,128)(2,1)} %copy.44) | copy-start | bytes 7077892
  34.8 5.9 copy-start.5
  50.6 10.7 %copy-start.7 = (f32[768]{0:T(1024)S(1)}, f32[768]{0:T(1024)}, u32[]{:S(2)}) copy-start(f32[768]{0:T(1024)} %param.5) | copy-start | bytes 9220
  50.6 108.6 %all-to-all-start = ((bf16[8,128,2304]{2,0,1:T(8,128)(2,1)}), bf16[8,128,2304]{2,0,1:T(8,128)(2,1)}, u32[]{:S(2)}, u32[]{:S(2)}) async-start(bf16[8,128,2304]{2,0,1:T(8,128)(2,1)} %copy.52), calls=%async_computation | async-start | bytes 9437184 | tf_op jit(solution)/shard_map/all_to_all | solution.py:71
  61.4 640.2 %all-reduce.2.cloned.1.call-start = ((), (), s32[]{:S(2)}) async-start(), calls=%async_computation.1 | async-start | bytes 1572864 | tf_op jit(solution)/shard_map/psum | solution.py:87
  162.1 2.2 copy-start
  703.7 3.8 slice-start
  704.0 3.5 slice-start.1
  728.4 3.4 copy-start.2
  728.5 3.4 copy-start.3
Sparse Core Ops, SparseCore 0:
  166.2 535.2 all-reduce.1
where the time goes:
time: 741 us; the launch traced here: 740 us
  waiting for transfers between devices  633 us (85%)
  local copies, waits for them, and re-layouts  39.1 us (5%)
  matrix products  22.8 us (3%)
  other arithmetic  17.5 us (2%)
  between operations  15 us (2%)
  starting transfers between devices  12 us (2%)
    psum x1, waiting for transfers between devices, body(): summed = lax.psum(terms, 'space')  535 us
    all_to_all x1, waiting for transfers between devices, body(): lax.all_to_all(local, 'tm', split_axis=1, concat_axis=0, tiled=True)  97.8 us
  transfers between devices with their start and end apart: 3, of which 2 were waited for; matrix products, arithmetic and copies ran while one was open for 3% of the time, Pallas kernels for 0%

commit v1 on v0

v1 whole, which is shorter than its diff:
```python
import functools

import jax
import jax.numpy as jnp
import ml_dtypes
import numpy as np
from jax import lax
from jax.experimental import pallas as pl
from jax.experimental.pallas import tpu as pltpu
from jax.sharding import PartitionSpec as P

NB = 32
NFFT = 128
HOP = 64
SLOTS = 64
PDEV = 768
NPOINTS = 49152
TM = 4
OWN = NB // TM
HERE = SLOTS // TM
SPAN = OWN * HOP
CHUNKS = (6, 6, 4)
F32, BF16 = jnp.float32, jnp.bfloat16


def transform_table():
    times = np.arange(NFFT)
    freq = np.arange(SLOTS)[:, None]
    window = 0.5 - 0.5 * np.cos(2.0 * np.pi * times / NFFT)
    window = window / np.sqrt(np.sum(window * window))
    angles = 2.0 * np.pi * ((freq * times[None, :]) % NFFT) / NFFT
    real_rows = window * np.cos(angles)
    imag_rows = -window * np.sin(angles)
    nyquist = window * np.cos(np.pi * times)
    imag_rows = np.where(freq == 0, nyquist[None, :], imag_rows)
    return np.stack([real_rows, imag_rows], axis=1).astype(ml_dtypes.bfloat16)


def banded_table():
    table = transform_table()
    band = np.zeros((SLOTS, 2, OWN, SPAN + HOP), ml_dtypes.bfloat16)
    for b in range(OWN):
        band[:, :, b, b * HOP : b * HOP + NFFT] = table
    return band.reshape(TM, HERE, 2 * OWN, SPAN + HOP)


def transform_kernel(band, snaps, follow, tail, *outs):
    rank = lax.axis_index("tm")
    own = snaps[0]
    last = (rank == TM - 1).astype(jnp.int32)
    pick = jnp.full((HOP, PDEV), last, jnp.int32) > 0
    next_half = jnp.where(pick, tail[0].astype(F32), follow[0].astype(F32)).astype(BF16)
    for k, out in enumerate(outs):
        rows = band[(rank + k) % TM]
        got = jnp.dot(rows[:, :SPAN], own, preferred_element_type=F32)
        got += jnp.dot(rows[:, SPAN:], next_half, preferred_element_type=F32)
        out[:, 0] = got.reshape(out.shape[0], 2 * OWN, PDEV).astype(BF16)


def transform(band, snaps, follow, tail):
    count = band.shape[1]
    rows = jnp.asarray(band.reshape(TM, count * 2 * OWN, SPAN + HOP))
    return pl.pallas_call(
        transform_kernel,
        grid=(3,),
        in_specs=[
            pl.BlockSpec(rows.shape, lambda c: (0, 0, 0)),
            pl.BlockSpec((1, SPAN, PDEV), lambda c: (c, 0, 0)),
            pl.BlockSpec((1, HOP, PDEV), lambda c: (c, 0, 0)),
            pl.BlockSpec((1, HOP, PDEV), lambda c: (c, 0, 0)),
        ],
        out_specs=[pl.BlockSpec((count, 1, 2 * OWN, PDEV), lambda c: (0, c, 0, 0))] * TM,
        out_shape=[jax.ShapeDtypeStruct((count, 3, 2 * OWN, PDEV), BF16)] * TM,
        compiler_params=pltpu.CompilerParams(vmem_limit_bytes=32 << 20),
        cost_estimate=pl.CostEstimate(
            flops=2 * TM * count * 16 * 576 * 3 * PDEV, bytes_accessed=8 << 20, transcendentals=0
        ),
        name="transform",
    )(rows, snaps, follow, tail)


def zero_lanes(first_pair):
    is_zero = (lax.axis_index("tm") == 0) & (pl.program_id(0) + first_pair == 0)
    return jnp.where(is_zero, 2 * NB, 0)


def gram_kernel(first_pair, own, behind1, behind2, behind3, volume, terms, spec, held):
    rank = lax.axis_index("tm")
    for k, piece in enumerate((own, behind1, behind2, behind3)):
        held[(rank + TM - k) % TM] = piece[...]
    weights = volume[...]
    total = jnp.zeros((4 * NB, 4 * NB), F32)
    for c in range(3):
        rows = []
        for s in range(2):
            pieces = [held[q, s, c].astype(F32) for q in range(TM)]
            rows += [p[:OWN] for p in pieces] + [p[OWN:] for p in pieces]
        both = jnp.concatenate(rows, 0)
        plain = both.astype(BF16)
        weighted = (both * weights).astype(BF16)
        spec[0, c] = plain
        total += lax.dot_general(
            weighted, plain, (((1,), (1,)), ((), ())), preferred_element_type=F32
        )
    lane = lax.broadcasted_iota(jnp.int32, (NB, 4 * NB), 1)
    first, low = lane < 2 * NB, (lane % (2 * NB)) < NB
    top = jnp.where(first, total[:NB], total[2 * NB : 3 * NB])
    bottom = jnp.where(first, total[NB : 2 * NB], total[3 * NB :])
    summed = top + jnp.where(low, pltpu.roll(bottom, 3 * NB, 1), 0.0)
    apart = jnp.where(lane < NB, top, bottom)
    terms[0] = jnp.where(lane < zero_lanes(first_pair), apart, summed)


def gram_terms(first_pair, pieces, volume):
    pairs = pieces[0].shape[0] // 2
    piece = pl.BlockSpec((2, 3, 2 * OWN, PDEV), lambda p: (p, 0, 0, 0))
    return pl.pallas_call(
        functools.partial(gram_kernel, first_pair),
        grid=(pairs,),
        in_specs=[piece] * TM + [pl.BlockSpec((1, PDEV), lambda p: (0, 0))],
        out_specs=[
            pl.BlockSpec((1, NB, 4 * NB), lambda p: (p, 0, 0)),
            pl.BlockSpec((1, 3, 4 * NB, PDEV), lambda p: (p, 0, 0, 0)),
        ],
        out_shape=[
            jax.ShapeDtypeStruct((pairs, NB, 4 * NB), F32),
            jax.ShapeDtypeStruct((pairs, 3, 4 * NB, PDEV), BF16),
        ],
        scratch_shapes=[pltpu.VMEM((TM, 2, 3, 2 * OWN, PDEV), BF16)],
        compiler_params=pltpu.CompilerParams(vmem_limit_bytes=32 << 20),
        cost_estimate=pl.CostEstimate(
            flops=pairs * 2 * 128 * 128 * 3 * PDEV,
            bytes_accessed=pairs * 4 * 3 * 128 * PDEV,
            transcendentals=0,
        ),
        name="gram_terms",
    )(*pieces, volume)


def modes_kernel(first_pair, t0, t1, t2, t3, spec, *rest):
    gram, modes = rest[-2:]
    total = ((t0[0] + t1[0]) + (t2[0] + t3[0])) / (NB * 3 * NPOINTS)
    lane = lax.broadcasted_iota(jnp.int32, (NB, 4 * NB), 1)
    first, low = lane < 2 * NB, (lane % (2 * NB)) < NB
    zero = lane < zero_lanes(first_pair)
    flipped = jnp.concatenate([total] * 4, 0).T
    cross_t = jnp.where(first, flipped[NB : 2 * NB], flipped[3 * NB :])
    mat = jnp.where(low, total, jnp.where(zero, total, total - cross_t))
    for s in range(2):
        for part in range(2):
            at = (2 * s + part) * NB
            gram[s, part] = mat[:, at : at + NB]
    squares = mat * mat

    def part_sum(keep):
        return jnp.sum(jnp.where(keep, squares, 0.0), keepdims=True)

    e0, e1 = part_sum(lane < NB), part_sum(first & ~low)
    rest_sum = part_sum(~first)
    zero_here = zero[:1, :1]
    norm_a = jnp.sqrt(jnp.where(zero_here, e0, e0 + e1) + 1e-06)
    norm_b = jnp.sqrt(jnp.where(zero_here, e1, e0 + e1) + 1e-06)
    norm_rest = jnp.sqrt(rest_sum + 1e-06)
    turned = jnp.where(low, -pltpu.roll(mat, 3 * NB, 1), pltpu.roll(mat, NB, 1))
    part_a = jnp.where(zero, jnp.where(low, mat, 0.0), mat)
    part_b = jnp.where(zero, jnp.where(low, 0.0, mat), turned)
    part_a = part_a / jnp.where(first, norm_a, norm_rest)
    part_b = part_b / jnp.where(first, norm_b, norm_rest)
    mixing = jnp.concatenate(
        [
            jnp.where(first, part_a, 0.0),
            jnp.where(first, part_b, 0.0),
            jnp.where(first, 0.0, part_a),
            jnp.where(first, 0.0, part_b),
        ],
        0,
    ).astype(BF16)
    for c in range(3):
        got = jnp.dot(mixing, spec[0, c], preferred_element_type=F32)
        modes[:, :, c] = got.reshape(2, 2, NB, PDEV).astype(BF16)


def project(first_pair, totals, spec, before):
    pairs = spec.shape[0]
    term = pl.BlockSpec((1, NB, 4 * NB), lambda p: (p, 0, 0))
    return pl.pallas_call(
        functools.partial(modes_kernel, first_pair),
        grid=(pairs,),
        in_specs=[term] * 4
        + [pl.BlockSpec((1, 3, 4 * NB, PDEV), lambda p: (p, 0, 0, 0))]
        + [pl.BlockSpec(memory_space=pl.ANY)] * len(before),
        out_specs=[
            pl.BlockSpec((2, 2, NB, NB), lambda p: (p + first_pair, 0, 0, 0)),
            pl.BlockSpec((2, 2, 3, NB, PDEV), lambda p: (p + first_pair, 0, 0, 0, 0)),
        ],
        out_shape=[
            jax.ShapeDtypeStruct((HERE, 2, NB, NB), F32),
            jax.ShapeDtypeStruct((HERE, 2, 3, NB, PDEV), BF16),
        ],
        input_output_aliases={5 + i: i for i in range(len(before))},
        compiler_params=pltpu.CompilerParams(vmem_limit_bytes=32 << 20),
        cost_estimate=pl.CostEstimate(
            flops=pairs * 2 * 128 * 128 * 3 * PDEV,
            bytes_accessed=pairs * 4 * 3 * 128 * PDEV,
            transcendentals=0,
        ),
        name="modes",
    )(*totals, spec, *before)


def over_space(block, mask):
    route = [(i, i ^ mask) for i in range(lax.axis_size("space"))]
    return lax.ppermute(block, "space", route)


def from_behind(block, distance):
    route = [(i, (i + distance) % TM) for i in range(TM)]
    return lax.ppermute(block, "tm", route)


def sum_over_space(terms):
    for shift in (4, 2, 0):
        got = [terms] + [over_space(terms, m << shift) for m in (1, 2, 3)]
        if shift:
            terms = (got[0] + got[1]) + (got[2] + got[3])
    return got


def body(snapshots, tail, volume):
    snaps = jnp.transpose(snapshots, (1, 0, 2))
    tail = jnp.transpose(tail, (1, 0, 2))
    weights = volume.reshape(1, PDEV)
    follow = lax.ppermute(snaps[:, :HOP], "tm", [(i, i - 1) for i in range(1, TM)])
    band = banded_table()
    start = 0
    done = ()
    sent = []
    for count in CHUNKS:
        pieces = transform(band[:, start : start + count], snaps, follow, tail)
        sent.append([pieces[0]] + [from_behind(pieces[k], k) for k in range(1, TM)])
        start += count
    start = 0
    for count, pieces in zip(CHUNKS, sent):
        terms, spec = gram_terms(start // 2, pieces, weights)
        done = project(start // 2, sum_over_space(terms), spec, done)
        start += count
    gram, modes = done
    return gram, jnp.transpose(modes, (0, 1, 3, 2, 4))


def solution(mesh):
    placed = (P("tm", None, "space"), P(None, None, "space"), P("space"))
    return jax.shard_map(
        body,
        mesh=mesh,
        in_specs=placed,
        out_specs=(P("tm", None, None, None), P("tm", None, None, None, "space")),
        check_vma=False,
    )
```

time: 741 us -> 181 us (0.24)
  waiting for transfers between devices: 633 us -> 94.6 us
  starting transfers between devices: 12 us -> 59.8 us
  local copies, waits for them, and re-layouts: 39.1 us -> 4.66 us
  matrix products: 22.8 us -> 0 us
  Pallas kernels: 0 us -> 19.1 us
  other arithmetic: 17.5 us -> 0.09 us
  between operations: 15 us -> 0.82 us
    psum x1 -> x0, waiting for transfers between devices: 535 us -> none  [body(): summed = lax.psum(terms, 'space')]
    all_to_all x1 -> x0, waiting for transfers between devices: 97.8 us -> none  [body(): lax.all_to_all(local, 'tm', split_axis=1, concat_axis=0, tiled=True)]
    ppermute x1 -> x37, waiting for transfers between devices: 0.01 us -> 94.6 us  [the longest x9 68.1 us: from_behind(): return lax.ppermute(block, 'tm', route)]
    ppermute x1 -> x37, starting transfers between devices: 1.28 us -> 59.8 us  [the longest x27 34 us: over_space(): return lax.ppermute(block, 'space', route)]
    dot_general x9 -> x0, matrix products: 22.8 us -> none  [the longest x1 6.82 us: half_transform(): jnp.einsum('rt,htx->hrx', rows_table[:, :HOP], halves[:-1], preferred_ele...]
    pallas_call x0 -> x9, Pallas kernels: none -> 19.1 us  [the longest x3 7.8 us: project(): pl.pallas_call(functools.partial(modes_kernel, first_pair), grid=(pairs,)...]
    another operation x7 -> x0, other arithmetic: 11.4 us -> none  [the longest x1 7.56 us: body(): modes = jnp.stack([first, second], axis=1).astype(jnp.bfloat16)]
    all_to_all x1 -> x0, starting transfers between devices: 10.7 us -> none  [body(): lax.all_to_all(local, 'tm', split_axis=1, concat_axis=0, tiled=True)]
  transfers between devices with their start and end apart: 3 -> 37, of which waited for: 2 -> 12; matrix products, arithmetic and copies ran while one was open for 3% -> 0% of each run, Pallas kernels for 0% -> 8%
where the time goes in v1:
time: 181 us; the launch traced here: 179 us
  waiting for transfers between devices  94.6 us (52%)
  starting transfers between devices  59.8 us (33%)
  Pallas kernels  19.1 us (11%)
  local copies, waits for them, and re-layouts  4.66 us (3%)
    ppermute x9, waiting for transfers between devices, from_behind(): return lax.ppermute(block, 'tm', route)  68.1 us
    ppermute x27, starting transfers between devices, over_space(): return lax.ppermute(block, 'space', route)  34 us
    ppermute x9, starting transfers between devices, from_behind(): return lax.ppermute(block, 'tm', route)  24.5 us
    ppermute x1, waiting for transfers between devices, body(): lax.ppermute(snaps[:, :HOP], 'tm', [(i, i - 1) for i in range(1, TM)])  16.8 us
    ppermute x27, waiting for transfers between devices, over_space(): return lax.ppermute(block, 'space', route)  9.73 us
    pallas_call x3, Pallas kernels, project(): pl.pallas_call(functools.partial(modes_kernel, first_pair), grid=(pairs,)...  7.8 us
    pallas_call x3, Pallas kernels, transform(): pl.pallas_call(transform_kernel, grid=(3,), in_specs=[pl.BlockSpec(rows.s...  7.62 us
    pallas_call x3, Pallas kernels, gram_terms(): pl.pallas_call(functools.partial(gram_kernel, first_pair), grid=(pairs,),...  3.69 us
  transfers between devices with their start and end apart: 37, of which 12 were waited for; matrix products, arithmetic and copies ran while one was open for 0% of the time, Pallas kernels for 8%

profile of v1, /device:TPU:1, one launch (start us, length us, event | category | flops | bytes accessed | tf_op | source)
XLA Modules:
  0.0 179.1 jit_solution(8410168184218665496)
XLA Ops:
  0.6 0.0 copy-start.4
  0.6 1.0 slice.4
  1.7 1.3 collective-permute-start
  3.0 16.8 %collective-permute-done.follow = bf16[3,64,768]{2,1,0:T(8,128)(2,1)S(1)} collective-permute-done((bf16[3,64,768]{2,1,0:T(8,128)(2,1)S(1)}, bf16[3,64,768]{2,1,0:T(8,128)(2,1)S(1)}, u32[]{:S(2)}, u32[]{:S(2)}) %collective-permute-start) | collective-permute-done | bytes 294944 | tf_op jit(solution)/shard_map/ppermute | solution.py:233
  19.8 1.7 copy-done
  21.4 1.0 copy-done.2
  22.4 1.0 copy-done.3
  23.4 2.5 %transform.3 = (bf16[4,3,16,768]{3,2,1,0:T(8,128)(2,1)S(1)}, bf16[4,3,16,768]{3,2,1,0:T(8,128)(2,1)S(1)}, bf16[4,3,16,768]{3,2,1,0:T(8,128)(2,1)S(1)}, bf16[4,3,16,768]{3,2,1,0:T(8,128)(2,1)S(1)}) custom-call(bf16[4,64,576]{2,1,0:T(8,128)(2,1)S(1)} %copy-done.2, bf16[3,512,768]{2,1,0:T(8,128)(2,1)S(1)} %bitcast.4, ...), custom_call_target="tpu_custom_call" | custom-call | flops 679477248 | bytes 8388608 | tf_op jit(solution)/shard_map/transform/pallas_call | solution.py:63
  25.9 0.0 copy-start.5
  25.9 5.0 %collective-permute-start.1 = (bf16[4,3,16,768]{3,2,1,0:T(8,128)(2,1)S(1)}, bf16[4,3,16,768]{3,2,1,0:T(8,128)(2,1)S(1)}, u32[]{:S(2)}, u32[]{:S(2)}) collective-permute-start(bf16[4,3,16,768]{3,2,1,0:T(8,128)(2,1)S(1)} %get-tuple-element.27), channel_id=1, source_target_pairs={{0,1},{1,2},{2,3},{3,0},{4,5},{5,6},{6,7},{7,4},{8,9},{9,10},{10,1... | collective-permute-start | bytes 884744 | tf_op jit(solution)/shard_map/ppermute | solution.py:218
  30.9 2.4 %collective-permute-start.2 = (bf16[4,3,16,768]{3,2,1,0:T(8,128)(2,1)S(1)}, bf16[4,3,16,768]{3,2,1,0:T(8,128)(2,1)S(1)}, u32[]{:S(2)}, u32[]{:S(2)}) collective-permute-start(bf16[4,3,16,768]{3,2,1,0:T(8,128)(2,1)S(1)} %get-tuple-element.28), channel_id=1, source_target_pairs={{0,2},{1,3},{2,0},{3,1},{4,6},{5,7},{6,4},{7,5},{8,10},{9,11},{10,... | collective-permute-start | bytes 884744 | tf_op jit(solution)/shard_map/ppermute | solution.py:218
  33.3 2.6 %transform.5 = (bf16[6,3,16,768]{3,2,1,0:T(8,128)(2,1)S(1)}, bf16[6,3,16,768]{3,2,1,0:T(8,128)(2,1)S(1)}, bf16[6,3,16,768]{3,2,1,0:T(8,128)(2,1)S(1)}, bf16[6,3,16,768]{3,2,1,0:T(8,128)(2,1)S(1)}) custom-call(bf16[4,96,576]{2,1,0:T(8,128)(2,1)S(1)} %copy-done.6, bf16[3,512,768]{2,1,0:T(8,128)(2,1)S(1)} %bitcast.5, ...), custom_call_target="tpu_custom_call" | custom-call | flops 1019215872 | bytes 8388608 | tf_op jit(solution)/shard_map/transform/pallas_call | solution.py:63
  35.9 0.0 copy-start.7
  35.9 0.3 collective-permute-start.25
  36.2 3.4 %collective-permute-start.3 = (bf16[4,3,16,768]{3,2,1,0:T(8,128)(2,1)S(1)}, bf16[4,3,16,768]{3,2,1,0:T(8,128)(2,1)S(1)}, u32[]{:S(2)}, u32[]{:S(2)}) collective-permute-start(bf16[4,3,16,768]{3,2,1,0:T(8,128)(2,1)S(1)} %get-tuple-element.29), channel_id=1, source_target_pairs={{0,3},{1,0},{2,1},{3,2},{4,7},{5,4},{6,5},{7,6},{8,11},{9,8},{10,9... | collective-permute-start | bytes 884744 | tf_op jit(solution)/shard_map/ppermute | solution.py:218
  39.5 3.0 %collective-permute-start.26 = (bf16[6,3,16,768]{3,2,1,0:T(8,128)(2,1)S(1)}, bf16[6,3,16,768]{3,2,1,0:T(8,128)(2,1)S(1)}, u32[]{:S(2)}, u32[]{:S(2)}) collective-permute-start(bf16[6,3,16,768]{3,2,1,0:T(8,128)(2,1)S(1)} %get-tuple-element.40), channel_id=1, source_target_pairs={{0,2},{1,3},{2,0},{3,1},{4,6},{5,7},{6,4},{7,5},{8,10},{9,11},{10,... | collective-permute-start | bytes 1327112 | tf_op jit(solution)/shard_map/ppermute | solution.py:218
  42.5 2.2 %collective-permute-done.1.behind1 = bf16[4,3,16,768]{3,2,1,0:T(8,128)(2,1)S(1)} collective-permute-done((bf16[4,3,16,768]{3,2,1,0:T(8,128)(2,1)S(1)}, bf16[4,3,16,768]{3,2,1,0:T(8,128)(2,1)S(1)}, u32[]{:S(2)}, u32[]{:S(2)}) %collective-permute-start.1) | collective-permute-done | bytes 294944 | tf_op jit(solution)/shard_map/ppermute | solution.py:218
  44.7 4.7 %collective-permute-start.27 = (bf16[6,3,16,768]{3,2,1,0:T(8,128)(2,1)S(1)}, bf16[6,3,16,768]{3,2,1,0:T(8,128)(2,1)S(1)}, u32[]{:S(2)}, u32[]{:S(2)}) collective-permute-start(bf16[6,3,16,768]{3,2,1,0:T(8,128)(2,1)S(1)} %get-tuple-element.41), channel_id=1, source_target_pairs={{0,3},{1,0},{2,1},{3,2},{4,7},{5,4},{6,5},{7,6},{8,11},{9,8},{10,9... | collective-permute-start | bytes 1327112 | tf_op jit(solution)/shard_map/ppermute | solution.py:218
  49.4 2.6 %transform.4 = (bf16[6,3,16,768]{3,2,1,0:T(8,128)(2,1)S(1)}, bf16[6,3,16,768]{3,2,1,0:T(8,128)(2,1)S(1)}, bf16[6,3,16,768]{3,2,1,0:T(8,128)(2,1)S(1)}, bf16[6,3,16,768]{3,2,1,0:T(8,128)(2,1)S(1)}) custom-call(bf16[4,96,576]{2,1,0:T(8,128)(2,1)S(1)} %copy-done.5, bf16[3,512,768]{2,1,0:T(8,128)(2,1)S(1)} %bitcast.6, ...), custom_call_target="tpu_custom_call" | custom-call | flops 1019215872 | bytes 8388608 | tf_op jit(solution)/shard_map/transform/pallas_call | solution.py:63
  52.0 21.3 %collective-permute-done.2.behind2 = bf16[4,3,16,768]{3,2,1,0:T(8,128)(2,1)S(1)} collective-permute-done((bf16[4,3,16,768]{3,2,1,0:T(8,128)(2,1)S(1)}, bf16[4,3,16,768]{3,2,1,0:T(8,128)(2,1)S(1)}, u32[]{:S(2)}, u32[]{:S(2)}) %collective-permute-start.2) | collective-permute-done | bytes 294944 | tf_op jit(solution)/shard_map/ppermute | solution.py:218
  73.3 0.0 collective-permute-start.13
  73.3 38.8 %collective-permute-done.3.behind3 = bf16[4,3,16,768]{3,2,1,0:T(8,128)(2,1)S(1)} collective-permute-done((bf16[4,3,16,768]{3,2,1,0:T(8,128)(2,1)S(1)}, bf16[4,3,16,768]{3,2,1,0:T(8,128)(2,1)S(1)}, u32[]{:S(2)}, u32[]{:S(2)}) %collective-permute-start.3) | collective-permute-done | bytes 294944 | tf_op jit(solution)/shard_map/ppermute | solution.py:218
  112.1 0.9 gram_terms.3
  113.0 1.3 collective-permute-start.4
  114.3 1.9 %collective-permute-done.4 = f32[2,32,128]{2,1,0:T(8,128)S(1)} collective-permute-done((f32[2,32,128]{2,1,0:T(8,128)S(1)}, f32[2,32,128]{2,1,0:T(8,128)S(1)}, u32[]{:S(2)}, u32[]{:S(2)}) %collective-permute-start.4) | collective-permute-done | bytes 32800 | tf_op jit(solution)/shard_map/ppermute | solution.py:213
  116.1 3.6 %collective-permute-start.14 = (bf16[6,3,16,768]{3,2,1,0:T(8,128)(2,1)S(1)}, bf16[6,3,16,768]{3,2,1,0:T(8,128)(2,1)S(1)}, u32[]{:S(2)}, u32[]{:S(2)}) collective-permute-start(bf16[6,3,16,768]{3,2,1,0:T(8,128)(2,1)S(1)} %get-tuple-element.34), channel_id=1, source_target_pairs={{0,2},{1,3},{2,0},{3,1},{4,6},{5,7},{6,4},{7,5},{8,10},{9,11},{10,... | collective-permute-start | bytes 1327112 | tf_op jit(solution)/shard_map/ppermute | solution.py:218
  119.7 0.0 collective-permute-done.25.behind1
  119.7 2.1 %collective-permute-start.15 = (bf16[6,3,16,768]{3,2,1,0:T(8,128)(2,1)S(1)}, bf16[6,3,16,768]{3,2,1,0:T(8,128)(2,1)S(1)}, u32[]{:S(2)}, u32[]{:S(2)}) collective-permute-start(bf16[6,3,16,768]{3,2,1,0:T(8,128)(2,1)S(1)} %get-tuple-element.35), channel_id=1, source_target_pairs={{0,3},{1,0},{2,1},{3,2},{4,7},{5,4},{6,5},{7,6},{8,11},{9,8},{10,9... | collective-permute-start | bytes 1327112 | tf_op jit(solution)/shard_map/ppermute | solution.py:218
  121.9 2.7 %collective-permute-start.5 = (f32[2,32,128]{2,1,0:T(8,128)S(1)}, f32[2,32,128]{2,1,0:T(8,128)S(1)}, u32[]{:S(2)}, u32[]{:S(2)}) collective-permute-start(f32[2,32,128]{2,1,0:T(8,128)S(1)} %get-tuple-element.30), channel_id=1, source_target_pairs={{0,128},{4,132},{8,136},{12,140},{16,144},{20,148},{24,152},{28,15... | collective-permute-start | bytes 98312 | tf_op jit(solution)/shard_map/ppermute | solution.py:213
  124.6 0.0 collective-permute-done.27.behind3
  124.6 0.9 collective-permute-start.6
  125.5 1.4 gram_terms.5
  126.9 0.8 collective-permute-start.28
  127.6 1.6 collective-permute-done.6
  129.2 0.9 collective-permute-start.29
  130.1 0.7 collective-permute-start.30
  130.8 5.8 %collective-permute-done.14.behind2 = bf16[6,3,16,768]{3,2,1,0:T(8,128)(2,1)S(1)} collective-permute-done((bf16[6,3,16,768]{3,2,1,0:T(8,128)(2,1)S(1)}, bf16[6,3,16,768]{3,2,1,0:T(8,128)(2,1)S(1)}, u32[]{:S(2)}, u32[]{:S(2)}) %collective-permute-start.14) | collective-permute-done | bytes 442400 | tf_op jit(solution)/shard_map/ppermute | solution.py:218
  136.7 1.3 collective-permute-start.7
  138.0 2.6 %collective-permute-start.8 = (f32[2,32,128]{2,1,0:T(8,128)S(1)}, f32[2,32,128]{2,1,0:T(8,128)S(1)}, u32[]{:S(2)}, u32[]{:S(2)}) collective-permute-start(f32[2,32,128]{2,1,0:T(8,128)S(1)} %add_add_fusion.5), channel_id=1, source_target_pairs={{0,32},{4,36},{8,40},{12,44},{16,48},{20,52},{24,56},{28,60},{32,0... | collective-permute-start | bytes 98312 | tf_op jit(solution)/shard_map/ppermute | solution.py:213
  140.6 1.4 gram_terms.4
  142.0 1.3 collective-permute-start.16
  143.3 2.5 %collective-permute-start.17 = (f32[3,32,128]{2,1,0:T(8,128)S(1)}, f32[3,32,128]{2,1,0:T(8,128)S(1)}, u32[]{:S(2)}, u32[]{:S(2)}) collective-permute-start(f32[3,32,128]{2,1,0:T(8,128)S(1)} %get-tuple-element.36), channel_id=1, source_target_pairs={{0,128},{4,132},{8,136},{12,140},{16,144},{20,148},{24,152},{28,15... | collective-permute-start | bytes 147464 | tf_op jit(solution)/shard_map/ppermute | solution.py:213
  145.8 0.2 collective-permute-start.18
  146.0 0.1 collective-permute-start.31
  146.1 1.7 collective-permute-done.17
  147.8 0.3 collective-permute-start.32
  148.1 1.9 %collective-permute-done.18 = f32[3,32,128]{2,1,0:T(8,128)S(1)} collective-permute-done((f32[3,32,128]{2,1,0:T(8,128)S(1)}, f32[3,32,128]{2,1,0:T(8,128)S(1)}, u32[]{:S(2)}, u32[]{:S(2)}) %collective-permute-start.18) | collective-permute-done | bytes 49184 | tf_op jit(solution)/shard_map/ppermute | solution.py:213
  149.9 0.1 collective-permute-start.33
  150.1 0.5 collective-permute-start.19
  150.5 1.8 %collective-permute-done.32 = f32[3,32,128]{2,1,0:T(8,128)S(1)} collective-permute-done((f32[3,32,128]{2,1,0:T(8,128)S(1)}, f32[3,32,128]{2,1,0:T(8,128)S(1)}, u32[]{:S(2)}, u32[]{:S(2)}) %collective-permute-start.32) | collective-permute-done | bytes 49184 | tf_op jit(solution)/shard_map/ppermute | solution.py:213
  152.3 1.6 collective-permute-start.20
  153.9 0.2 collective-permute-done.33
  154.1 0.4 collective-permute-start.21
  154.5 2.4 %collective-permute-start.9 = (f32[2,32,128]{2,1,0:T(8,128)S(1)}, f32[2,32,128]{2,1,0:T(8,128)S(1)}, u32[]{:S(2)}, u32[]{:S(2)}) collective-permute-start(f32[2,32,128]{2,1,0:T(8,128)S(1)} %add_add_fusion.5), channel_id=1, source_target_pairs={{0,48},{4,52},{8,56},{12,60},{16,32},{20,36},{24,40},{28,44},{32,1... | collective-permute-start | bytes 98312 | tf_op jit(solution)/shard_map/ppermute | solution.py:213
  156.9 0.7 collective-permute-done.20
  157.6 6.0 %collective-permute-start.34 = (f32[3,32,128]{2,1,0:T(8,128)S(1)}, f32[3,32,128]{2,1,0:T(8,128)S(1)}, u32[]{:S(2)}, u32[]{:S(2)}) collective-permute-start(f32[3,32,128]{2,1,0:T(8,128)S(1)} %add_add_fusion.t0), channel_id=1, source_target_pairs={{0,4},{4,0},{8,12},{12,8},{16,20},{20,16},{24,28},{28,24},{32,36},... | collective-permute-start | bytes 147464 | tf_op jit(solution)/shard_map/ppermute | solution.py:213
  163.6 3.2 %collective-permute-start.36 = (f32[3,32,128]{2,1,0:T(8,128)S(1)}, f32[3,32,128]{2,1,0:T(8,128)S(1)}, u32[]{:S(2)}, u32[]{:S(2)}) collective-permute-start(f32[3,32,128]{2,1,0:T(8,128)S(1)} %add_add_fusion.t0), channel_id=1, source_target_pairs={{0,12},{4,8},{8,4},{12,0},{16,28},{20,24},{24,20},{28,16},{32,44},... | collective-permute-start | bytes 147464 | tf_op jit(solution)/shard_map/ppermute | solution.py:213
  166.9 0.2 collective-permute-start.23
  167.1 1.9 %collective-permute-start.24 = (f32[3,32,128]{2,1,0:T(8,128)S(1)}, f32[3,32,128]{2,1,0:T(8,128)S(1)}, u32[]{:S(2)}, u32[]{:S(2)}) collective-permute-start(f32[3,32,128]{2,1,0:T(8,128)S(1)} %add_add_fusion.2.t0), channel_id=1, source_target_pairs={{0,12},{4,8},{8,4},{12,0},{16,28},{20,24},{24,20},{28,16},{32,44},... | collective-permute-start | bytes 147464 | tf_op jit(solution)/shard_map/ppermute | solution.py:213
  169.0 0.2 collective-permute-start.10
  169.3 2.0 %collective-permute-start.12 = (f32[2,32,128]{2,1,0:T(8,128)S(1)}, f32[2,32,128]{2,1,0:T(8,128)S(1)}, u32[]{:S(2)}, u32[]{:S(2)}) collective-permute-start(f32[2,32,128]{2,1,0:T(8,128)S(1)} %add_add_fusion.4.t0), channel_id=1, source_target_pairs={{0,12},{4,8},{8,4},{12,0},{16,28},{20,24},{24,20},{28,16},{32,44},... | collective-permute-start | bytes 98312 | tf_op jit(solution)/shard_map/ppermute | solution.py:213
  171.3 2.8 %modes.3 = (f32[16,2,32,32]{3,2,1,0:T(8,128)}, bf16[16,2,3,32,768]{4,3,2,1,0:T(8,128)(2,1)}) custom-call(f32[3,32,128]{2,1,0:T(8,128)S(1)} %add_add_fusion.t0, f32[3,32,128]{2,1,0:T(8,128)S(1)} %collective-permute-done.34.t1, f32[3,32,128]{2,1,0:T(8,128)S(1)} %collective-permute-done.35.t2, f32[3,32,128]{2,1,0:T(8,128)S(1)} %collective-permute-done.36.t3, ...), custom_call_target="tpu_custom_call" | custom-call | flops 226492416 | bytes 3538944 | tf_op jit(solution)/shard_map/modes/pallas_call | solution.py:186
  174.1 2.9 %modes.4 = (f32[16,2,32,32]{3,2,1,0:T(8,128)}, bf16[16,2,3,32,768]{4,3,2,1,0:T(8,128)(2,1)}) custom-call(f32[3,32,128]{2,1,0:T(8,128)S(1)} %add_add_fusion.2.t0, f32[3,32,128]{2,1,0:T(8,128)S(1)} %collective-permute-done.22.t1, f32[3,32,128]{2,1,0:T(8,128)S(1)} %collective-permute-done.23.t2, ...), custom_call_target="tpu_custom_call", output_to_operand_aliasing={{0}: (5, {}), {1}: (6, {})} | custom-call | flops 226492416 | bytes 3538944 | tf_op jit(solution)/shard_map/modes/pallas_call | solution.py:186
  177.0 2.1 %modes.5 = (f32[16,2,32,32]{3,2,1,0:T(8,128)}, bf16[16,2,3,32,768]{4,3,2,1,0:T(8,128)(2,1)}) custom-call(f32[2,32,128]{2,1,0:T(8,128)S(1)} %add_add_fusion.4.t0, f32[2,32,128]{2,1,0:T(8,128)S(1)} %collective-permute-done.10.t1, f32[2,32,128]{2,1,0:T(8,128)S(1)} %collective-permute-done.11.t2, ...), custom_call_target="tpu_custom_call", output_to_operand_aliasing={{0}: (5, {}), {1}: (6, {})} | custom-call | flops 150994944 | bytes 2359296 | tf_op jit(solution)/shard_map/modes/pallas_call | solution.py:186
  (43 shorter events, 0.2 us)
Async XLA Ops:
  0.6 32.6 %copy-start.4 = (bf16[64,3,768]{2,0,1:T(8,128)(2,1)S(1)}, bf16[64,3,768]{2,0,1:T(8,128)(2,1)}, u32[]{:S(2)}) copy-start(bf16[64,3,768]{2,0,1:T(8,128)(2,1)} %param.7) | copy-start | bytes 884740
  1.7 18.1 %collective-permute-start = (bf16[3,64,768]{2,1,0:T(8,128)(2,1)S(1)}, bf16[3,64,768]{2,1,0:T(8,128)(2,1)S(1)}, u32[]{:S(2)}, u32[]{:S(2)}) collective-permute-start(bf16[3,64,768]{2,1,0:T(8,128)(2,1)S(1)} %slice.4), channel_id=1, source_target_pairs={{1,0},{2,1},{3,2},{5,4},{6,5},{7,6},{9,8},{10,9},{11,10},{13,12},{... | collective-permute-start | bytes 884744 | tf_op jit(solution)/shard_map/ppermute | solution.py:233
  19.8 1.7 copy-start
  21.4 1.0 copy-start.2
  22.4 1.0 copy-start.3
  23.4 9.9 %copy-start.1 = (bf16[512,3,768]{2,0,1:T(8,128)(2,1)S(1)}, bf16[512,3,768]{2,0,1:T(8,128)(2,1)}, u32[]{:S(2)}) copy-start(bf16[512,3,768]{2,0,1:T(8,128)(2,1)} %param.6) | copy-start | bytes 7077892
  23.4 9.9 %copy-start.6 = (bf16[4,96,576]{2,1,0:T(8,128)(2,1)S(1)}, bf16[4,96,576]{2,1,0:T(8,128)(2,1)}, u32[]{:S(2)}) copy-start(bf16[4,96,576]{2,1,0:T(8,128)(2,1)} %constant.6.clone.band) | copy-start | bytes 1327108
  25.9 23.6 %copy-start.5 = (bf16[4,96,576]{2,1,0:T(8,128)(2,1)S(1)}, bf16[4,96,576]{2,1,0:T(8,128)(2,1)}, u32[]{:S(2)}) copy-start(bf16[4,96,576]{2,1,0:T(8,128)(2,1)} %constant.7.clone.band) | copy-start | bytes 1327108
  25.9 18.8 %collective-permute-start.1 = (bf16[4,3,16,768]{3,2,1,0:T(8,128)(2,1)S(1)}, bf16[4,3,16,768]{3,2,1,0:T(8,128)(2,1)S(1)}, u32[]{:S(2)}, u32[]{:S(2)}) collective-permute-start(bf16[4,3,16,768]{3,2,1,0:T(8,128)(2,1)S(1)} %get-tuple-element.27), channel_id=1, source_target_pairs={{0,1},{1,2},{2,3},{3,0},{4,5},{5,6},{6,7},{7,4},{8,9},{9,10},{10,1... | collective-permute-start | bytes 884744 | tf_op jit(solution)/shard_map/ppermute | solution.py:218
  30.9 42.4 %collective-permute-start.2 = (bf16[4,3,16,768]{3,2,1,0:T(8,128)(2,1)S(1)}, bf16[4,3,16,768]{3,2,1,0:T(8,128)(2,1)S(1)}, u32[]{:S(2)}, u32[]{:S(2)}) collective-permute-start(bf16[4,3,16,768]{3,2,1,0:T(8,128)(2,1)S(1)} %get-tuple-element.28), channel_id=1, source_target_pairs={{0,2},{1,3},{2,0},{3,1},{4,6},{5,7},{6,4},{7,5},{8,10},{9,11},{10,... | collective-permute-start | bytes 884744 | tf_op jit(solution)/shard_map/ppermute | solution.py:218
  35.9 37.4 %copy-start.7 = (f32[768]{0:T(1024)S(1)}, f32[768]{0:T(1024)}, u32[]{:S(2)}) copy-start(f32[768]{0:T(1024)} %param.8) | copy-start | bytes 9220
  35.9 83.8 %collective-permute-start.25 = (bf16[6,3,16,768]{3,2,1,0:T(8,128)(2,1)S(1)}, bf16[6,3,16,768]{3,2,1,0:T(8,128)(2,1)S(1)}, u32[]{:S(2)}, u32[]{:S(2)}) collective-permute-start(bf16[6,3,16,768]{3,2,1,0:T(8,128)(2,1)S(1)} %get-tuple-element.39), channel_id=1, source_target_pairs={{0,1},{1,2},{2,3},{3,0},{4,5},{5,6},{6,7},{7,4},{8,9},{9,10},{10,1... | collective-permute-start | bytes 1327112 | tf_op jit(solution)/shard_map/ppermute | solution.py:218
  36.2 75.9 %collective-permute-start.3 = (bf16[4,3,16,768]{3,2,1,0:T(8,128)(2,1)S(1)}, bf16[4,3,16,768]{3,2,1,0:T(8,128)(2,1)S(1)}, u32[]{:S(2)}, u32[]{:S(2)}) collective-permute-start(bf16[4,3,16,768]{3,2,1,0:T(8,128)(2,1)S(1)} %get-tuple-element.29), channel_id=1, source_target_pairs={{0,3},{1,0},{2,1},{3,2},{4,7},{5,4},{6,5},{7,6},{8,11},{9,8},{10,9... | collective-permute-start | bytes 884744 | tf_op jit(solution)/shard_map/ppermute | solution.py:218
  39.5 82.3 %collective-permute-start.26 = (bf16[6,3,16,768]{3,2,1,0:T(8,128)(2,1)S(1)}, bf16[6,3,16,768]{3,2,1,0:T(8,128)(2,1)S(1)}, u32[]{:S(2)}, u32[]{:S(2)}) collective-permute-start(bf16[6,3,16,768]{3,2,1,0:T(8,128)(2,1)S(1)} %get-tuple-element.40), channel_id=1, source_target_pairs={{0,2},{1,3},{2,0},{3,1},{4,6},{5,7},{6,4},{7,5},{8,10},{9,11},{10,... | collective-permute-start | bytes 1327112 | tf_op jit(solution)/shard_map/ppermute | solution.py:218
  44.7 79.9 %collective-permute-start.27 = (bf16[6,3,16,768]{3,2,1,0:T(8,128)(2,1)S(1)}, bf16[6,3,16,768]{3,2,1,0:T(8,128)(2,1)S(1)}, u32[]{:S(2)}, u32[]{:S(2)}) collective-permute-start(bf16[6,3,16,768]{3,2,1,0:T(8,128)(2,1)S(1)} %get-tuple-element.41), channel_id=1, source_target_pairs={{0,3},{1,0},{2,1},{3,2},{4,7},{5,4},{6,5},{7,6},{8,11},{9,8},{10,9... | collective-permute-start | bytes 1327112 | tf_op jit(solution)/shard_map/ppermute | solution.py:218
  73.3 56.8 %collective-permute-start.13 = (bf16[6,3,16,768]{3,2,1,0:T(8,128)(2,1)S(1)}, bf16[6,3,16,768]{3,2,1,0:T(8,128)(2,1)S(1)}, u32[]{:S(2)}, u32[]{:S(2)}) collective-permute-start(bf16[6,3,16,768]{3,2,1,0:T(8,128)(2,1)S(1)} %get-tuple-element.33), channel_id=1, source_target_pairs={{0,1},{1,2},{2,3},{3,0},{4,5},{5,6},{6,7},{7,4},{8,9},{9,10},{10,1... | collective-permute-start | bytes 1327112 | tf_op jit(solution)/shard_map/ppermute | solution.py:218
  113.0 3.1 %collective-permute-start.4 = (f32[2,32,128]{2,1,0:T(8,128)S(1)}, f32[2,32,128]{2,1,0:T(8,128)S(1)}, u32[]{:S(2)}, u32[]{:S(2)}) collective-permute-start(f32[2,32,128]{2,1,0:T(8,128)S(1)} %get-tuple-element.30), channel_id=1, source_target_pairs={{0,64},{4,68},{8,72},{12,76},{16,80},{20,84},{24,88},{28,92},{32,9... | collective-permute-start | bytes 98312 | tf_op jit(solution)/shard_map/ppermute | solution.py:213
  116.1 20.6 %collective-permute-start.14 = (bf16[6,3,16,768]{3,2,1,0:T(8,128)(2,1)S(1)}, bf16[6,3,16,768]{3,2,1,0:T(8,128)(2,1)S(1)}, u32[]{:S(2)}, u32[]{:S(2)}) collective-permute-start(bf16[6,3,16,768]{3,2,1,0:T(8,128)(2,1)S(1)} %get-tuple-element.34), channel_id=1, source_target_pairs={{0,2},{1,3},{2,0},{3,1},{4,6},{5,7},{6,4},{7,5},{8,10},{9,11},{10,... | collective-permute-start | bytes 1327112 | tf_op jit(solution)/shard_map/ppermute | solution.py:218
  119.7 18.2 %collective-permute-start.15 = (bf16[6,3,16,768]{3,2,1,0:T(8,128)(2,1)S(1)}, bf16[6,3,16,768]{3,2,1,0:T(8,128)(2,1)S(1)}, u32[]{:S(2)}, u32[]{:S(2)}) collective-permute-start(bf16[6,3,16,768]{3,2,1,0:T(8,128)(2,1)S(1)} %get-tuple-element.35), channel_id=1, source_target_pairs={{0,3},{1,0},{2,1},{3,2},{4,7},{5,4},{6,5},{7,6},{8,11},{9,8},{10,9... | collective-permute-start | bytes 1327112 | tf_op jit(solution)/shard_map/ppermute | solution.py:218
  121.9 5.0 %collective-permute-start.5 = (f32[2,32,128]{2,1,0:T(8,128)S(1)}, f32[2,32,128]{2,1,0:T(8,128)S(1)}, u32[]{:S(2)}, u32[]{:S(2)}) collective-permute-start(f32[2,32,128]{2,1,0:T(8,128)S(1)} %get-tuple-element.30), channel_id=1, source_target_pairs={{0,128},{4,132},{8,136},{12,140},{16,144},{20,148},{24,152},{28,15... | collective-permute-start | bytes 98312 | tf_op jit(solution)/shard_map/ppermute | solution.py:213
  124.6 4.6 %collective-permute-start.6 = (f32[2,32,128]{2,1,0:T(8,128)S(1)}, f32[2,32,128]{2,1,0:T(8,128)S(1)}, u32[]{:S(2)}, u32[]{:S(2)}) collective-permute-start(f32[2,32,128]{2,1,0:T(8,128)S(1)} %get-tuple-element.30), channel_id=1, source_target_pairs={{0,192},{4,196},{8,200},{12,204},{16,208},{20,212},{24,216},{28,22... | collective-permute-start | bytes 98312 | tf_op jit(solution)/shard_map/ppermute | solution.py:213
  126.9 15.1 %collective-permute-start.28 = (f32[3,32,128]{2,1,0:T(8,128)S(1)}, f32[3,32,128]{2,1,0:T(8,128)S(1)}, u32[]{:S(2)}, u32[]{:S(2)}) collective-permute-start(f32[3,32,128]{2,1,0:T(8,128)S(1)} %get-tuple-element.42), channel_id=1, source_target_pairs={{0,64},{4,68},{8,72},{12,76},{16,80},{20,84},{24,88},{28,92},{32,9... | collective-permute-start | bytes 147464 | tf_op jit(solution)/shard_map/ppermute | solution.py:213
  129.2 14.1 %collective-permute-start.29 = (f32[3,32,128]{2,1,0:T(8,128)S(1)}, f32[3,32,128]{2,1,0:T(8,128)S(1)}, u32[]{:S(2)}, u32[]{:S(2)}) collective-permute-start(f32[3,32,128]{2,1,0:T(8,128)S(1)} %get-tuple-element.42), channel_id=1, source_target_pairs={{0,128},{4,132},{8,136},{12,140},{16,144},{20,148},{24,152},{28,15... | collective-permute-start | bytes 147464 | tf_op jit(solution)/shard_map/ppermute | solution.py:213
  130.1 15.7 %collective-permute-start.30 = (f32[3,32,128]{2,1,0:T(8,128)S(1)}, f32[3,32,128]{2,1,0:T(8,128)S(1)}, u32[]{:S(2)}, u32[]{:S(2)}) collective-permute-start(f32[3,32,128]{2,1,0:T(8,128)S(1)} %get-tuple-element.42), channel_id=1, source_target_pairs={{0,192},{4,196},{8,200},{12,204},{16,208},{20,212},{24,216},{28,22... | collective-permute-start | bytes 147464 | tf_op jit(solution)/shard_map/ppermute | solution.py:213
  136.7 27.0 %collective-permute-start.7 = (f32[2,32,128]{2,1,0:T(8,128)S(1)}, f32[2,32,128]{2,1,0:T(8,128)S(1)}, u32[]{:S(2)}, u32[]{:S(2)}) collective-permute-start(f32[2,32,128]{2,1,0:T(8,128)S(1)} %add_add_fusion.5), channel_id=1, source_target_pairs={{0,16},{4,20},{8,24},{12,28},{16,0},{20,4},{24,8},{28,12},{32,48},... | collective-permute-start | bytes 98312 | tf_op jit(solution)/shard_map/ppermute | solution.py:213
  138.0 28.9 %collective-permute-start.8 = (f32[2,32,128]{2,1,0:T(8,128)S(1)}, f32[2,32,128]{2,1,0:T(8,128)S(1)}, u32[]{:S(2)}, u32[]{:S(2)}) collective-permute-start(f32[2,32,128]{2,1,0:T(8,128)S(1)} %add_add_fusion.5), channel_id=1, source_target_pairs={{0,32},{4,36},{8,40},{12,44},{16,48},{20,52},{24,56},{28,60},{32,0... | collective-permute-start | bytes 98312 | tf_op jit(solution)/shard_map/ppermute | solution.py:213
  142.0 4.0 %collective-permute-start.16 = (f32[3,32,128]{2,1,0:T(8,128)S(1)}, f32[3,32,128]{2,1,0:T(8,128)S(1)}, u32[]{:S(2)}, u32[]{:S(2)}) collective-permute-start(f32[3,32,128]{2,1,0:T(8,128)S(1)} %get-tuple-element.36), channel_id=1, source_target_pairs={{0,64},{4,68},{8,72},{12,76},{16,80},{20,84},{24,88},{28,92},{32,9... | collective-permute-start | bytes 147464 | tf_op jit(solution)/shard_map/ppermute | solution.py:213
  143.3 4.5 %collective-permute-start.17 = (f32[3,32,128]{2,1,0:T(8,128)S(1)}, f32[3,32,128]{2,1,0:T(8,128)S(1)}, u32[]{:S(2)}, u32[]{:S(2)}) collective-permute-start(f32[3,32,128]{2,1,0:T(8,128)S(1)} %get-tuple-element.36), channel_id=1, source_target_pairs={{0,128},{4,132},{8,136},{12,140},{16,144},{20,148},{24,152},{28,15... | collective-permute-start | bytes 147464 | tf_op jit(solution)/shard_map/ppermute | solution.py:213
  145.8 4.2 %collective-permute-start.18 = (f32[3,32,128]{2,1,0:T(8,128)S(1)}, f32[3,32,128]{2,1,0:T(8,128)S(1)}, u32[]{:S(2)}, u32[]{:S(2)}) collective-permute-start(f32[3,32,128]{2,1,0:T(8,128)S(1)} %get-tuple-element.36), channel_id=1, source_target_pairs={{0,192},{4,196},{8,200},{12,204},{16,208},{20,212},{24,216},{28,22... | collective-permute-start | bytes 147464 | tf_op jit(solution)/shard_map/ppermute | solution.py:213
  146.0 4.1 %collective-permute-start.31 = (f32[3,32,128]{2,1,0:T(8,128)S(1)}, f32[3,32,128]{2,1,0:T(8,128)S(1)}, u32[]{:S(2)}, u32[]{:S(2)}) collective-permute-start(f32[3,32,128]{2,1,0:T(8,128)S(1)} %add_add_fusion.1), channel_id=1, source_target_pairs={{0,16},{4,20},{8,24},{12,28},{16,0},{20,4},{24,8},{28,12},{32,48},... | collective-permute-start | bytes 147464 | tf_op jit(solution)/shard_map/ppermute | solution.py:213
  147.8 4.6 %collective-permute-start.32 = (f32[3,32,128]{2,1,0:T(8,128)S(1)}, f32[3,32,128]{2,1,0:T(8,128)S(1)}, u32[]{:S(2)}, u32[]{:S(2)}) collective-permute-start(f32[3,32,128]{2,1,0:T(8,128)S(1)} %add_add_fusion.1), channel_id=1, source_target_pairs={{0,32},{4,36},{8,40},{12,44},{16,48},{20,52},{24,56},{28,60},{32,0... | collective-permute-start | bytes 147464 | tf_op jit(solution)/shard_map/ppermute | solution.py:213
  149.9 4.2 %collective-permute-start.33 = (f32[3,32,128]{2,1,0:T(8,128)S(1)}, f32[3,32,128]{2,1,0:T(8,128)S(1)}, u32[]{:S(2)}, u32[]{:S(2)}) collective-permute-start(f32[3,32,128]{2,1,0:T(8,128)S(1)} %add_add_fusion.1), channel_id=1, source_target_pairs={{0,48},{4,52},{8,56},{12,60},{16,32},{20,36},{24,40},{28,44},{32,1... | collective-permute-start | bytes 147464 | tf_op jit(solution)/shard_map/ppermute | solution.py:213
  150.1 4.4 %collective-permute-start.19 = (f32[3,32,128]{2,1,0:T(8,128)S(1)}, f32[3,32,128]{2,1,0:T(8,128)S(1)}, u32[]{:S(2)}, u32[]{:S(2)}) collective-permute-start(f32[3,32,128]{2,1,0:T(8,128)S(1)} %add_add_fusion.3), channel_id=1, source_target_pairs={{0,16},{4,20},{8,24},{12,28},{16,0},{20,4},{24,8},{28,12},{32,48},... | collective-permute-start | bytes 147464 | tf_op jit(solution)/shard_map/ppermute | solution.py:213
  152.3 5.2 %collective-permute-start.20 = (f32[3,32,128]{2,1,0:T(8,128)S(1)}, f32[3,32,128]{2,1,0:T(8,128)S(1)}, u32[]{:S(2)}, u32[]{:S(2)}) collective-permute-start(f32[3,32,128]{2,1,0:T(8,128)S(1)} %add_add_fusion.3), channel_id=1, source_target_pairs={{0,32},{4,36},{8,40},{12,44},{16,48},{20,52},{24,56},{28,60},{32,0... | collective-permute-start | bytes 147464 | tf_op jit(solution)/shard_map/ppermute | solution.py:213
  154.1 9.5 %collective-permute-start.21 = (f32[3,32,128]{2,1,0:T(8,128)S(1)}, f32[3,32,128]{2,1,0:T(8,128)S(1)}, u32[]{:S(2)}, u32[]{:S(2)}) collective-permute-start(f32[3,32,128]{2,1,0:T(8,128)S(1)} %add_add_fusion.3), channel_id=1, source_target_pairs={{0,48},{4,52},{8,56},{12,60},{16,32},{20,36},{24,40},{28,44},{32,1... | collective-permute-start | bytes 147464 | tf_op jit(solution)/shard_map/ppermute | solution.py:213
  154.5 12.4 %collective-permute-start.9 = (f32[2,32,128]{2,1,0:T(8,128)S(1)}, f32[2,32,128]{2,1,0:T(8,128)S(1)}, u32[]{:S(2)}, u32[]{:S(2)}) collective-permute-start(f32[2,32,128]{2,1,0:T(8,128)S(1)} %add_add_fusion.5), channel_id=1, source_target_pairs={{0,48},{4,52},{8,56},{12,60},{16,32},{20,36},{24,40},{28,44},{32,1... | collective-permute-start | bytes 98312 | tf_op jit(solution)/shard_map/ppermute | solution.py:213
  157.6 9.5 %collective-permute-start.34 = (f32[3,32,128]{2,1,0:T(8,128)S(1)}, f32[3,32,128]{2,1,0:T(8,128)S(1)}, u32[]{:S(2)}, u32[]{:S(2)}) collective-permute-start(f32[3,32,128]{2,1,0:T(8,128)S(1)} %add_add_fusion.t0), channel_id=1, source_target_pairs={{0,4},{4,0},{8,12},{12,8},{16,20},{20,16},{24,28},{28,24},{32,36},... | collective-permute-start | bytes 147464 | tf_op jit(solution)/shard_map/ppermute | solution.py:213
  163.6 5.4 %collective-permute-start.35 = (f32[3,32,128]{2,1,0:T(8,128)S(1)}, f32[3,32,128]{2,1,0:T(8,128)S(1)}, u32[]{:S(2)}, u32[]{:S(2)}) collective-permute-start(f32[3,32,128]{2,1,0:T(8,128)S(1)} %add_add_fusion.t0), channel_id=1, source_target_pairs={{0,8},{4,12},{8,0},{12,4},{16,24},{20,28},{24,16},{28,20},{32,40},... | collective-permute-start | bytes 147464 | tf_op jit(solution)/shard_map/ppermute | solution.py:213
  163.6 5.6 %collective-permute-start.36 = (f32[3,32,128]{2,1,0:T(8,128)S(1)}, f32[3,32,128]{2,1,0:T(8,128)S(1)}, u32[]{:S(2)}, u32[]{:S(2)}) collective-permute-start(f32[3,32,128]{2,1,0:T(8,128)S(1)} %add_add_fusion.t0), channel_id=1, source_target_pairs={{0,12},{4,8},{8,4},{12,0},{16,28},{20,24},{24,20},{28,16},{32,44},... | collective-permute-start | bytes 147464 | tf_op jit(solution)/shard_map/ppermute | solution.py:213
  166.9 2.4 %collective-permute-start.22 = (f32[3,32,128]{2,1,0:T(8,128)S(1)}, f32[3,32,128]{2,1,0:T(8,128)S(1)}, u32[]{:S(2)}, u32[]{:S(2)}) collective-permute-start(f32[3,32,128]{2,1,0:T(8,128)S(1)} %add_add_fusion.2.t0), channel_id=1, source_target_pairs={{0,4},{4,0},{8,12},{12,8},{16,20},{20,16},{24,28},{28,24},{32,36},... | collective-permute-start | bytes 147464 | tf_op jit(solution)/shard_map/ppermute | solution.py:213
  166.9 7.3 %collective-permute-start.23 = (f32[3,32,128]{2,1,0:T(8,128)S(1)}, f32[3,32,128]{2,1,0:T(8,128)S(1)}, u32[]{:S(2)}, u32[]{:S(2)}) collective-permute-start(f32[3,32,128]{2,1,0:T(8,128)S(1)} %add_add_fusion.2.t0), channel_id=1, source_target_pairs={{0,8},{4,12},{8,0},{12,4},{16,24},{20,28},{24,16},{28,20},{32,40},... | collective-permute-start | bytes 147464 | tf_op jit(solution)/shard_map/ppermute | solution.py:213
  167.1 7.0 %collective-permute-start.24 = (f32[3,32,128]{2,1,0:T(8,128)S(1)}, f32[3,32,128]{2,1,0:T(8,128)S(1)}, u32[]{:S(2)}, u32[]{:S(2)}) collective-permute-start(f32[3,32,128]{2,1,0:T(8,128)S(1)} %add_add_fusion.2.t0), channel_id=1, source_target_pairs={{0,12},{4,8},{8,4},{12,0},{16,28},{20,24},{24,20},{28,16},{32,44},... | collective-permute-start | bytes 147464 | tf_op jit(solution)/shard_map/ppermute | solution.py:213
  169.0 8.0 %collective-permute-start.10 = (f32[2,32,128]{2,1,0:T(8,128)S(1)}, f32[2,32,128]{2,1,0:T(8,128)S(1)}, u32[]{:S(2)}, u32[]{:S(2)}) collective-permute-start(f32[2,32,128]{2,1,0:T(8,128)S(1)} %add_add_fusion.4.t0), channel_id=1, source_target_pairs={{0,4},{4,0},{8,12},{12,8},{16,20},{20,16},{24,28},{28,24},{32,36},... | collective-permute-start | bytes 98312 | tf_op jit(solution)/shard_map/ppermute | solution.py:213
  169.3 7.7 %collective-permute-start.11 = (f32[2,32,128]{2,1,0:T(8,128)S(1)}, f32[2,32,128]{2,1,0:T(8,128)S(1)}, u32[]{:S(2)}, u32[]{:S(2)}) collective-permute-start(f32[2,32,128]{2,1,0:T(8,128)S(1)} %add_add_fusion.4.t0), channel_id=1, source_target_pairs={{0,8},{4,12},{8,0},{12,4},{16,24},{20,28},{24,16},{28,20},{32,40},... | collective-permute-start | bytes 98312 | tf_op jit(solution)/shard_map/ppermute | solution.py:213
  169.3 7.7 %collective-permute-start.12 = (f32[2,32,128]{2,1,0:T(8,128)S(1)}, f32[2,32,128]{2,1,0:T(8,128)S(1)}, u32[]{:S(2)}, u32[]{:S(2)}) collective-permute-start(f32[2,32,128]{2,1,0:T(8,128)S(1)} %add_add_fusion.4.t0), channel_id=1, source_target_pairs={{0,12},{4,8},{8,4},{12,0},{16,28},{20,24},{24,20},{28,16},{32,44},... | collective-permute-start | bytes 98312 | tf_op jit(solution)/shard_map/ppermute | solution.py:213

commit v2 on v1

v2 whole, which is shorter than its diff:
```python
import functools

import jax
import jax.numpy as jnp
import ml_dtypes
import numpy as np
from jax import lax
from jax.experimental import pallas as pl
from jax.experimental.pallas import tpu as pltpu
from jax.sharding import PartitionSpec as P

NB = 32
NFFT = 128
HOP = 64
SLOTS = 64
PDEV = 768
NPOINTS = 49152
TM = 4
OWN = NB // TM
HALF = OWN // 2
HERE = SLOTS // TM
BODY = HALF * HOP
ALL = (0, HERE // 2)
LONG = 10**12
F32, BF16 = jnp.float32, jnp.bfloat16
ANY = pl.BlockSpec(memory_space=pl.ANY)
WHOLE, PART = 60 << 20, 16 << 20


def transform_table():
    f32 = np.float32
    times = np.arange(NFFT, dtype=f32)
    freq = np.arange(SLOTS, dtype=f32)[:, None]
    window = f32(0.5) - f32(0.5) * np.cos(f32(2.0 * np.pi) * times / f32(NFFT))
    window = window / np.sqrt(np.sum(window * window))
    angles = f32(2.0 * np.pi) * freq * times[None, :] / f32(NFFT)
    real_rows = window * np.cos(angles)
    imag_rows = -window * np.sin(angles)
    nyquist = window * np.cos(f32(np.pi) * times)
    imag_rows = np.where(freq == 0, nyquist[None, :], imag_rows)
    return np.stack([real_rows, imag_rows], axis=1).astype(ml_dtypes.bfloat16)


def banded_table():
    table = transform_table()
    band = np.zeros((SLOTS, 2, HALF, BODY + HOP), ml_dtypes.bfloat16)
    for b in range(HALF):
        band[:, :, b, b * HOP : b * HOP + NFFT] = table
    return band.reshape(TM, HERE * 2 * HALF, BODY + HOP)


def transform_kernel(pairs, late, band, main, *rest):
    rank = lax.axis_index("tm")
    if late:
        outs = rest[2:]
        follow, tail = rest[:2]
        last = (rank == TM - 1).astype(jnp.int32)
        pick = jnp.full((HOP, PDEV), last, jnp.int32) > 0
        after = jnp.where(pick, tail[0].astype(F32), follow[0].astype(F32)).astype(BF16)
    else:
        outs = rest[1:]
        after = rest[0][0]
    first, stop = (4 * HALF * p for p in pairs)
    rows = jnp.concatenate([band[(rank + k) % TM, first:stop] for k in range(TM)], 0)
    got = jnp.dot(rows[:, :BODY], main[0], preferred_element_type=F32)
    got += jnp.dot(rows[:, BODY:], after, preferred_element_type=F32)
    got = got.astype(BF16).reshape(TM, pairs[1] - pairs[0], 4 * HALF, PDEV)
    for k, out in enumerate(outs[:TM]):
        out[:, 0] = got[k]
    if len(outs) > TM:
        outs[TM][...] = main[:, :HOP]


def transform(band, snaps, pairs, half, ends=(), edge=False):
    count = pairs[1] - pairs[0]
    piece = jax.ShapeDtypeStruct((count, 3, 4 * HALF, PDEV), BF16)
    strip = jax.ShapeDtypeStruct((3, HOP, PDEV), BF16)
    if half:
        ends_specs = [pl.BlockSpec((1, HOP, PDEV), lambda c: (c, 0, 0))] * 2
    else:
        ends, ends_specs = (snaps,), [pl.BlockSpec((1, HOP, PDEV), lambda c: (c, HALF, 0))]
    return pl.pallas_call(
        functools.partial(transform_kernel, pairs, half),
        grid=(3,),
        in_specs=[
            pl.BlockSpec(band.shape, lambda c: (0, 0, 0)),
            pl.BlockSpec((1, BODY, PDEV), lambda c: (c, half, 0)),
        ]
        + ends_specs,
        out_specs=[pl.BlockSpec((count, 1, 4 * HALF, PDEV), lambda c: (0, c, 0, 0))] * TM
        + [pl.BlockSpec((1, HOP, PDEV), lambda c: (c, 0, 0))] * edge,
        out_shape=[piece] * TM + [strip] * edge,
        compiler_params=pltpu.CompilerParams(vmem_limit_bytes=PART if half else WHOLE),
        cost_estimate=pl.CostEstimate(flops=LONG, bytes_accessed=0, transcendentals=0),
        name="transform",
    )(band, snaps, *ends)


def zero_lanes(first_pair, pair):
    is_zero = (lax.axis_index("tm") == 0) & (pair + first_pair == 0)
    return jnp.where(is_zero, 2 * NB, 0)


def lane_masks():
    lane = lax.broadcasted_iota(jnp.int32, (NB, 4 * NB), 1)
    return lane, lane < 2 * NB, (lane % (2 * NB)) < NB


def gram_kernel(first_pair, *refs):
    early, late, volume = refs[:TM], refs[TM : 2 * TM], refs[2 * TM]
    terms, spec, held = refs[-3:]
    rank = lax.axis_index("tm")
    for k in range(TM):
        held[(rank + TM - k) % TM, 0] = early[k][0]
        held[(rank + TM - k) % TM, 1] = late[k][0]
    weights = volume[...]
    upper = lax.broadcasted_iota(jnp.int32, (OWN, PDEV), 0) < HALF
    total = jnp.zeros((4 * NB, 4 * NB), F32)
    for c in range(3):
        rows = []
        for s in range(2):
            real, imag = [], []
            for q in range(TM):
                a = held[q, 0, c].astype(F32)[s * OWN : (s + 1) * OWN]
                b = held[q, 1, c].astype(F32)[s * OWN : (s + 1) * OWN]
                real.append(jnp.where(upper, a, pltpu.roll(b, HALF, 0)))
                imag.append(jnp.where(upper, pltpu.roll(a, HALF, 0), b))
            rows += real + imag
        both = jnp.concatenate(rows, 0)
        plain = both.astype(BF16)
        weighted = (both * weights).astype(BF16)
        spec[0, c] = plain
        total += lax.dot_general(
            weighted, plain, (((1,), (1,)), ((), ())), preferred_element_type=F32
        )
    lane, first, low = lane_masks()
    top = jnp.where(first, total[:NB], total[2 * NB : 3 * NB])
    bottom = jnp.where(first, total[NB : 2 * NB], total[3 * NB :])
    summed = top + jnp.where(low, pltpu.roll(bottom, 3 * NB, 1), 0.0)
    apart = jnp.where(lane < NB, top, bottom)
    terms[0] = jnp.where(lane < zero_lanes(first_pair, pl.program_id(0)), apart, summed)


def gram_terms(group, pairs, early, late, volume, before=(), wait=(), cost=0):
    count = pairs[1] - pairs[0]
    skip = pairs[0] - group[0]
    size = group[1] - group[0]
    late_piece = pl.BlockSpec((1, 3, 4 * HALF, PDEV), lambda p: (p, 0, 0, 0))
    early_piece = pl.BlockSpec((1, 3, 4 * HALF, PDEV), lambda p: (p + skip, 0, 0, 0))
    return pl.pallas_call(
        functools.partial(gram_kernel, pairs[0]),
        grid=(count,),
        in_specs=[early_piece] * TM
        + [late_piece] * TM
        + [pl.BlockSpec((1, PDEV), lambda p: (0, 0))]
        + [ANY] * (len(before) + len(wait)),
        out_specs=[
            pl.BlockSpec((1, NB, 4 * NB), lambda p: (p + skip, 0, 0)),
            pl.BlockSpec((1, 3, 4 * NB, PDEV), lambda p: (p + skip, 0, 0, 0)),
        ],
        out_shape=[
            jax.ShapeDtypeStruct((size, NB, 4 * NB), F32),
            jax.ShapeDtypeStruct((size, 3, 4 * NB, PDEV), BF16),
        ],
        scratch_shapes=[pltpu.VMEM((TM, 2, 3, 4 * HALF, PDEV), BF16)],
        input_output_aliases={2 * TM + 1 + i: i for i in range(len(before))},
        compiler_params=pltpu.CompilerParams(vmem_limit_bytes=PART),
        cost_estimate=pl.CostEstimate(flops=cost, bytes_accessed=0, transcendentals=0),
        name="gram_terms",
    )(*early, *late, volume, *before, *wait)


def mix(first_pair, pair, total):
    lane, first, low = lane_masks()
    zero = lane < zero_lanes(first_pair, pair)
    flipped = jnp.concatenate([total] * 4, 0).T
    cross_t = jnp.where(first, flipped[NB : 2 * NB], flipped[3 * NB :])
    mat = jnp.where(low, total, jnp.where(zero, total, total - cross_t))
    squares = mat * mat

    def part_sum(keep):
        return jnp.sum(jnp.where(keep, squares, 0.0), keepdims=True)

    e0, e1 = part_sum(lane < NB), part_sum(first & ~low)
    rest_sum = part_sum(~first)
    zero_here = zero[:1, :1]
    norm_a = jnp.sqrt(jnp.where(zero_here, e0, e0 + e1) + 1e-06)
    norm_b = jnp.sqrt(jnp.where(zero_here, e1, e0 + e1) + 1e-06)
    norm_rest = jnp.sqrt(rest_sum + 1e-06)
    turned = jnp.where(low, -pltpu.roll(mat, 3 * NB, 1), pltpu.roll(mat, NB, 1))
    part_a = jnp.where(zero, jnp.where(low, mat, 0.0), mat)
    part_b = jnp.where(zero, jnp.where(low, 0.0, mat), turned)
    part_a = part_a / jnp.where(first, norm_a, norm_rest)
    part_b = part_b / jnp.where(first, norm_b, norm_rest)
    mixing = jnp.concatenate(
        [
            jnp.where(first, part_a, 0.0),
            jnp.where(first, part_b, 0.0),
            jnp.where(first, 0.0, part_a),
            jnp.where(first, 0.0, part_b),
        ],
        0,
    )
    return mat, mixing.astype(BF16)


def modes_kernel(pairs, t0, t1, t2, t3, spec, *rest):
    gram, modes, mats, mixings = rest[-4:]
    pair = pl.program_id(0)

    @pl.when(pair == 0)
    def _():
        for p in range(pairs[1] - pairs[0]):
            total = ((t0[p] + t1[p]) + (t2[p] + t3[p])) / (NB * 3 * NPOINTS)
            mats[p], mixings[p] = mix(pairs[0], p, total)

    mat = mats[pair]
    for s in range(2):
        for part in range(2):
            at = (2 * s + part) * NB
            gram[s, part] = mat[:, at : at + NB]
    for c in range(3):
        got = jnp.dot(mixings[pair], spec[0, c], preferred_element_type=F32)
        modes[:, :, c] = got.astype(BF16).reshape(2, 2, NB, PDEV)


def project(pairs, totals, spec, before):
    first, count = pairs[0], pairs[1] - pairs[0]
    return pl.pallas_call(
        functools.partial(modes_kernel, pairs),
        grid=(count,),
        in_specs=[pl.BlockSpec((count, NB, 4 * NB), lambda p: (0, 0, 0))] * 4
        + [pl.BlockSpec((1, 3, 4 * NB, PDEV), lambda p: (p, 0, 0, 0))]
        + [ANY] * len(before),
        out_specs=[
            pl.BlockSpec((2, 2, NB, NB), lambda p: (p + first, 0, 0, 0)),
            pl.BlockSpec((2, 2, 3, NB, PDEV), lambda p: (p + first, 0, 0, 0, 0)),
        ],
        out_shape=[
            jax.ShapeDtypeStruct((HERE, 2, NB, NB), F32),
            jax.ShapeDtypeStruct((HERE, 2, 3, NB, PDEV), BF16),
        ],
        scratch_shapes=[
            pltpu.VMEM((count, NB, 4 * NB), F32),
            pltpu.VMEM((count, 4 * NB, 4 * NB), BF16),
        ],
        input_output_aliases={5 + i: i for i in range(len(before))},
        compiler_params=pltpu.CompilerParams(vmem_limit_bytes=PART),
        cost_estimate=pl.CostEstimate(flops=0, bytes_accessed=0, transcendentals=0),
        name="modes",
    )(*totals, spec, *before)


def over_space(block, mask):
    route = [(i, i ^ mask) for i in range(lax.axis_size("space"))]
    return lax.ppermute(block, "space", route)


def from_behind(block, distance):
    route = [(i, (i + distance) % TM) for i in range(TM)]
    return lax.ppermute(block, "tm", route)


def to_owners(pieces):
    far = from_behind(pieces[2], 2)
    return [pieces[0], from_behind(pieces[1], 1), far, from_behind(pieces[3], 3)]


def sum_over_space(terms):
    for shift in (4, 2, 0):
        got = [terms] + [over_space(terms, m << shift) for m in (1, 2, 3)]
        if shift:
            terms = (got[0] + got[1]) + (got[2] + got[3])
    return got


def body(snapshots, tail, volume):
    snaps = jnp.transpose(snapshots, (1, 0, 2))
    tail = jnp.transpose(tail, (1, 0, 2))
    weights = volume.reshape(1, PDEV)
    band = jnp.asarray(banded_table())
    *first, edge = transform(band, snaps, ALL, 0, edge=True)
    early = to_owners(first)
    follow = lax.ppermute(edge, "tm", [(i, i - 1) for i in range(1, TM)])
    late = to_owners(transform(band, snaps, ALL, 1, (follow, tail)))
    terms, spec = gram_terms(ALL, ALL, early, late, weights)
    gram, modes = project(ALL, sum_over_space(terms), spec, ())
    return gram, jnp.transpose(modes, (0, 1, 3, 2, 4))


def solution(mesh):
    placed = (P("tm", None, "space"), P(None, None, "space"), P("space"))
    return jax.shard_map(
        body,
        mesh=mesh,
        in_specs=placed,
        out_specs=(P("tm", None, None, None), P("tm", None, None, None, "space")),
        check_vma=False,
    )
```

time: 181 us -> 183 us (1.011); the launches traced: 179 us -> 183 us
  waiting for transfers between devices: 94.6 us -> 128 us
  starting transfers between devices: 59.8 us -> 36.2 us
  local copies, waits for them, and re-layouts: 4.66 us -> 0.03 us
    ppermute x1, waiting for transfers between devices: 16.8 us -> 80.8 us  [body(): follow = lax.ppermute(edge, 'tm', [(i, i - 1) for i in range(1, TM)])]
    ppermute x9 -> x6, waiting for transfers between devices: 68.1 us -> 33.8 us  [from_behind(): return lax.ppermute(block, 'tm', route)]
    ppermute x27 -> x9, starting transfers between devices: 34 us -> 12.8 us  [over_space(): return lax.ppermute(block, 'space', route)]
    unnamed x16 -> x10, local copies, waits for them, and re-layouts: 3.63 us -> 0.03 us
    ppermute x27 -> x9, waiting for transfers between devices: 9.73 us -> 13 us  [over_space(): return lax.ppermute(block, 'space', route)]
    ppermute x9 -> x6, starting transfers between devices: 24.5 us -> 22.1 us  [from_behind(): return lax.ppermute(block, 'tm', route)]
    pallas_call x9 -> x4, Pallas kernels: 19.1 us -> 18.4 us  [the longest x2 6.56 us: transform(): pl.pallas_call(functools.partial(transform_kernel, pairs, half), grid=(3,...]
  transfers between devices with their start and end apart: 37 -> 16, of which waited for: 12 -> 9; matrix products, arithmetic and copies ran while one was open for 0% -> 0% of each run, Pallas kernels for 8% -> 1%
where the time goes in v2:
time: 183 us
  waiting for transfers between devices  128 us (70%)
  starting transfers between devices  36.2 us (20%)
  Pallas kernels  18.4 us (10%)
    ppermute x1, waiting for transfers between devices, body(): follow = lax.ppermute(edge, 'tm', [(i, i - 1) for i in range(1, TM)])  80.8 us
    ppermute x6, waiting for transfers between devices, from_behind(): return lax.ppermute(block, 'tm', route)  33.8 us
    ppermute x6, starting transfers between devices, from_behind(): return lax.ppermute(block, 'tm', route)  22.1 us
    ppermute x9, waiting for transfers between devices, over_space(): return lax.ppermute(block, 'space', route)  13 us
    ppermute x9, starting transfers between devices, over_space(): return lax.ppermute(block, 'space', route)  12.8 us
    pallas_call x2, Pallas kernels, transform(): pl.pallas_call(functools.partial(transform_kernel, pairs, half), grid=(3,...  6.56 us
    pallas_call x1, Pallas kernels, gram_terms(): pl.pallas_call(functools.partial(gram_kernel, pairs[0]), grid=(count,), i...  6.42 us
    pallas_call x1, Pallas kernels, project(): pl.pallas_call(functools.partial(modes_kernel, pairs), grid=(count,), in_...  5.4 us
  transfers between devices with their start and end apart: 16, of which 9 were waited for; matrix products, arithmetic and copies ran while one was open for 0% of the time, Pallas kernels for 1%

profile of v2, /device:TPU:1, one launch (start us, length us, event | category | flops | bytes accessed | tf_op | source)
XLA Modules:
  0.0 183.1 jit_solution(4070142210297714778)
XLA Ops:
  0.6 0.0 copy-start.1
  0.6 0.0 copy-start.2
  0.6 0.0 copy-start.3
  0.7 4.7 %transform.2 = (bf16[8,3,16,768]{3,2,1,0:T(8,128)(2,1)}, bf16[8,3,16,768]{3,2,1,0:T(8,128)(2,1)}, bf16[8,3,16,768]{3,2,1,0:T(8,128)(2,1)}, bf16[8,3,16,768]{3,2,1,0:T(8,128)(2,1)}, bf16[3,64,768]{2,1,0:T(8,128)(2,1)}) custom-call(bf16[4,128,320]{2,1,0:T(8,128)(2,1)} %constant.2.clone.band, bf16[3,512,768]{2,1,0:T(8,128)(2,1)} %bitcast.3, ...), custom_call_target="tpu_custom_call" | custom-call | flops 999999995904 | tf_op jit(solution)/shard_map/transform/pallas_call | solution.py:82
  5.4 1.3 collective-permute-start.3
  6.6 4.5 %collective-permute-start = (bf16[8,3,16,768]{3,2,1,0:T(8,128)(2,1)}, bf16[8,3,16,768]{3,2,1,0:T(8,128)(2,1)}, u32[]{:S(2)}, u32[]{:S(2)}) collective-permute-start(bf16[8,3,16,768]{3,2,1,0:T(8,128)(2,1)} %get-tuple-element.16), channel_id=1, source_target_pairs={{0,1},{1,2},{2,3},{3,0},{4,5},{5,6},{6,7},{7,4},{8,9},{9,10},{10,1... | collective-permute-start | bytes 1769480 | tf_op jit(solution)/shard_map/ppermute | solution.py:261
  11.2 6.3 %collective-permute-start.1 = (bf16[8,3,16,768]{3,2,1,0:T(8,128)(2,1)}, bf16[8,3,16,768]{3,2,1,0:T(8,128)(2,1)}, u32[]{:S(2)}, u32[]{:S(2)}) collective-permute-start(bf16[8,3,16,768]{3,2,1,0:T(8,128)(2,1)} %get-tuple-element.17), channel_id=1, source_target_pairs={{0,2},{1,3},{2,0},{3,1},{4,6},{5,7},{6,4},{7,5},{8,10},{9,11},{10,... | collective-permute-start | bytes 1769480 | tf_op jit(solution)/shard_map/ppermute | solution.py:261
  17.5 1.2 collective-permute-start.2
  18.7 80.8 %collective-permute-done.3.rest_0_ = bf16[3,64,768]{2,1,0:T(8,128)(2,1)S(1)} collective-permute-done((bf16[3,64,768]{2,1,0:T(8,128)(2,1)}, bf16[3,64,768]{2,1,0:T(8,128)(2,1)S(1)}, u32[]{:S(2)}, u32[]{:S(2)}) %collective-permute-start.3) | collective-permute-done | bytes 294944 | tf_op jit(solution)/shard_map/ppermute | solution.py:284
  99.5 0.0 copy-done.1
  99.5 0.0 copy-done.2
  99.5 0.0 copy-done.3
  99.5 0.0 copy-start.4
  99.5 0.0 copy-start
  99.5 1.9 %transform.3 = (bf16[8,3,16,768]{3,2,1,0:T(8,128)(2,1)S(1)}, bf16[8,3,16,768]{3,2,1,0:T(8,128)(2,1)S(1)}, bf16[8,3,16,768]{3,2,1,0:T(8,128)(2,1)S(1)}, bf16[8,3,16,768]{3,2,1,0:T(8,128)(2,1)S(1)}) custom-call(bf16[4,128,320]{2,1,0:T(8,128)(2,1)S(1)} %copy-done.3, bf16[3,512,768]{2,1,0:T(8,128)(2,1)S(1)} %bitcast.5, ...), custom_call_target="tpu_custom_call" | custom-call | flops 999999995904 | tf_op jit(solution)/shard_map/transform/pallas_call | solution.py:82
  101.4 5.0 %collective-permute-start.4 = (bf16[8,3,16,768]{3,2,1,0:T(8,128)(2,1)S(1)}, bf16[8,3,16,768]{3,2,1,0:T(8,128)(2,1)S(1)}, u32[]{:S(2)}, u32[]{:S(2)}) collective-permute-start(bf16[8,3,16,768]{3,2,1,0:T(8,128)(2,1)S(1)} %get-tuple-element.21), channel_id=1, source_target_pairs={{0,1},{1,2},{2,3},{3,0},{4,5},{5,6},{6,7},{7,4},{8,9},{9,10},{10,1... | collective-permute-start | bytes 1769480 | tf_op jit(solution)/shard_map/ppermute | solution.py:261
  106.4 1.6 collective-permute-start.5
  108.0 0.0 collective-permute-done.refs_1_
  108.0 3.5 %collective-permute-start.6 = (bf16[8,3,16,768]{3,2,1,0:T(8,128)(2,1)S(1)}, bf16[8,3,16,768]{3,2,1,0:T(8,128)(2,1)S(1)}, u32[]{:S(2)}, u32[]{:S(2)}) collective-permute-start(bf16[8,3,16,768]{3,2,1,0:T(8,128)(2,1)S(1)} %get-tuple-element.23), channel_id=1, source_target_pairs={{0,3},{1,0},{2,1},{3,2},{4,7},{5,4},{6,5},{7,6},{8,11},{9,8},{10,9... | collective-permute-start | bytes 1769480 | tf_op jit(solution)/shard_map/ppermute | solution.py:261
  111.5 0.0 copy-done.4
  111.5 0.0 collective-permute-done.1.refs_2_
  111.5 0.7 collective-permute-done.2.refs_3_
  112.2 7.0 %collective-permute-done.4.refs_5_ = bf16[8,3,16,768]{3,2,1,0:T(8,128)(2,1)S(1)} collective-permute-done((bf16[8,3,16,768]{3,2,1,0:T(8,128)(2,1)S(1)}, bf16[8,3,16,768]{3,2,1,0:T(8,128)(2,1)S(1)}, u32[]{:S(2)}, u32[]{:S(2)}) %collective-permute-start.4) | collective-permute-done | bytes 589856 | tf_op jit(solution)/shard_map/ppermute | solution.py:261
  119.3 26.0 %collective-permute-done.5.refs_6_ = bf16[8,3,16,768]{3,2,1,0:T(8,128)(2,1)S(1)} collective-permute-done((bf16[8,3,16,768]{3,2,1,0:T(8,128)(2,1)S(1)}, bf16[8,3,16,768]{3,2,1,0:T(8,128)(2,1)S(1)}, u32[]{:S(2)}, u32[]{:S(2)}) %collective-permute-start.5) | collective-permute-done | bytes 589856 | tf_op jit(solution)/shard_map/ppermute | solution.py:261
  145.3 0.0 collective-permute-done.6.refs_7_
  145.3 0.0 copy-done
  145.3 6.4 %gram_terms.1 = (f32[8,32,128]{2,1,0:T(8,128)S(1)}, bf16[8,3,128,768]{3,2,1,0:T(8,128)(2,1)S(1)}) custom-call(bf16[8,3,16,768]{3,2,1,0:T(8,128)(2,1)S(1)} %copy-done, bf16[8,3,16,768]{3,2,1,0:T(8,128)(2,1)} %collective-permute-done.refs_1_, bf16[8,3,16,768]{3,2,1,0:T(8,128)(2,1)} %collective-permute-done.1.refs_2_, ...), custom_call_target="tpu_custom_call" | custom-call | tf_op jit(solution)/shard_map/gram_terms/pallas_call | solution.py:150
  151.7 0.1 collective-permute-start.9
  151.8 0.1 collective-permute-start.8
  151.9 3.1 %collective-permute-start.7 = (f32[8,32,128]{2,1,0:T(8,128)S(1)}, f32[8,32,128]{2,1,0:T(8,128)S(1)}, u32[]{:S(2)}, u32[]{:S(2)}) collective-permute-start(f32[8,32,128]{2,1,0:T(8,128)S(1)} %get-tuple-element.24), channel_id=1, source_target_pairs={{0,64},{4,68},{8,72},{12,76},{16,80},{20,84},{24,88},{28,92},{32,9... | collective-permute-start | bytes 393224 | tf_op jit(solution)/shard_map/ppermute | solution.py:256
  155.1 3.6 %collective-permute-done.9 = f32[8,32,128]{2,1,0:T(8,128)S(1)} collective-permute-done((f32[8,32,128]{2,1,0:T(8,128)S(1)}, f32[8,32,128]{2,1,0:T(8,128)S(1)}, u32[]{:S(2)}, u32[]{:S(2)}) %collective-permute-start.9) | collective-permute-done | bytes 131104 | tf_op jit(solution)/shard_map/ppermute | solution.py:256
  158.7 0.0 collective-permute-done.8
  158.7 0.5 collective-permute-done.7
  159.2 0.1 collective-permute-start.12
  159.3 0.1 collective-permute-start.11
  159.4 3.1 %collective-permute-start.10 = (f32[8,32,128]{2,1,0:T(8,128)S(1)}, f32[8,32,128]{2,1,0:T(8,128)S(1)}, u32[]{:S(2)}, u32[]{:S(2)}) collective-permute-start(f32[8,32,128]{2,1,0:T(8,128)S(1)} %add_add_fusion.1), channel_id=1, source_target_pairs={{0,16},{4,20},{8,24},{12,28},{16,0},{20,4},{24,8},{28,12},{32,48},... | collective-permute-start | bytes 393224 | tf_op jit(solution)/shard_map/ppermute | solution.py:256
  162.5 3.2 %collective-permute-done.12 = f32[8,32,128]{2,1,0:T(8,128)S(1)} collective-permute-done((f32[8,32,128]{2,1,0:T(8,128)S(1)}, f32[8,32,128]{2,1,0:T(8,128)S(1)}, u32[]{:S(2)}, u32[]{:S(2)}) %collective-permute-start.12) | collective-permute-done | bytes 131104 | tf_op jit(solution)/shard_map/ppermute | solution.py:256
  165.7 0.0 collective-permute-done.11
  165.7 0.6 collective-permute-done.10
  166.3 0.1 collective-permute-start.15
  166.4 6.1 %collective-permute-start.14 = (f32[8,32,128]{2,1,0:T(8,128)S(1)}, f32[8,32,128]{2,1,0:T(8,128)S(1)}, u32[]{:S(2)}, u32[]{:S(2)}) collective-permute-start(f32[8,32,128]{2,1,0:T(8,128)S(1)} %add_add_fusion.t0), channel_id=1, source_target_pairs={{0,8},{4,12},{8,0},{12,4},{16,24},{20,28},{24,16},{28,20},{32,40},... | collective-permute-start | bytes 393224 | tf_op jit(solution)/shard_map/ppermute | solution.py:256
  172.5 0.0 collective-permute-start.13
  172.5 0.0 collective-permute-done.15.t3
  172.5 5.2 %collective-permute-done.14.t2 = f32[8,32,128]{2,1,0:T(8,128)S(1)} collective-permute-done((f32[8,32,128]{2,1,0:T(8,128)S(1)}, f32[8,32,128]{2,1,0:T(8,128)S(1)}, u32[]{:S(2)}, u32[]{:S(2)}) %collective-permute-start.14) | collective-permute-done | bytes 131104 | tf_op jit(solution)/shard_map/ppermute | solution.py:256
  177.7 0.0 collective-permute-done.13.t1
  177.7 5.4 %modes.1 = (f32[16,2,32,32]{3,2,1,0:T(8,128)}, bf16[16,2,3,32,768]{4,3,2,1,0:T(8,128)(2,1)}) custom-call(f32[8,32,128]{2,1,0:T(8,128)S(1)} %add_add_fusion.t0, f32[8,32,128]{2,1,0:T(8,128)S(1)} %collective-permute-done.13.t1, f32[8,32,128]{2,1,0:T(8,128)S(1)} %collective-permute-done.14.t2, f32[8,32,128]{2,1,0:T(8,128)S(1)} %collective-permute-done.15.t3, ...), custom_call_target="tpu_custom_call" | custom-call | tf_op jit(solution)/shard_map/modes/pallas_call | solution.py:229
  (3 shorter events, 0.1 us)
Async XLA Ops:
  0.6 98.9 %copy-start.1 = (bf16[512,3,768]{2,0,1:T(8,128)(2,1)S(1)}, bf16[512,3,768]{2,0,1:T(8,128)(2,1)}, u32[]{:S(2)}) copy-start(bf16[512,3,768]{2,0,1:T(8,128)(2,1)} %param.4) | copy-start | bytes 7077892
  0.6 98.9 %copy-start.2 = (bf16[64,3,768]{2,0,1:T(8,128)(2,1)S(1)}, bf16[64,3,768]{2,0,1:T(8,128)(2,1)}, u32[]{:S(2)}) copy-start(bf16[64,3,768]{2,0,1:T(8,128)(2,1)} %param.5) | copy-start | bytes 884740
  0.6 98.8 %copy-start.3 = (bf16[4,128,320]{2,1,0:T(8,128)(2,1)S(1)}, bf16[4,128,320]{2,1,0:T(8,128)(2,1)}, u32[]{:S(2)}) copy-start(bf16[4,128,320]{2,1,0:T(8,128)(2,1)} %constant.2.clone.band) | copy-start | bytes 983044
  5.4 94.1 %collective-permute-start.3 = (bf16[3,64,768]{2,1,0:T(8,128)(2,1)}, bf16[3,64,768]{2,1,0:T(8,128)(2,1)S(1)}, u32[]{:S(2)}, u32[]{:S(2)}) collective-permute-start(bf16[3,64,768]{2,1,0:T(8,128)(2,1)} %get-tuple-element.19), channel_id=1, source_target_pairs={{1,0},{2,1},{3,2},{5,4},{6,5},{7,6},{9,8},{10,9},{11,10},{13,12},{... | collective-permute-start | bytes 884744 | tf_op jit(solution)/shard_map/ppermute | solution.py:284
  6.6 101.4 %collective-permute-start = (bf16[8,3,16,768]{3,2,1,0:T(8,128)(2,1)}, bf16[8,3,16,768]{3,2,1,0:T(8,128)(2,1)}, u32[]{:S(2)}, u32[]{:S(2)}) collective-permute-start(bf16[8,3,16,768]{3,2,1,0:T(8,128)(2,1)} %get-tuple-element.16), channel_id=1, source_target_pairs={{0,1},{1,2},{2,3},{3,0},{4,5},{5,6},{6,7},{7,4},{8,9},{9,10},{10,1... | collective-permute-start | bytes 1769480 | tf_op jit(solution)/shard_map/ppermute | solution.py:261
  11.2 100.3 %collective-permute-start.1 = (bf16[8,3,16,768]{3,2,1,0:T(8,128)(2,1)}, bf16[8,3,16,768]{3,2,1,0:T(8,128)(2,1)}, u32[]{:S(2)}, u32[]{:S(2)}) collective-permute-start(bf16[8,3,16,768]{3,2,1,0:T(8,128)(2,1)} %get-tuple-element.17), channel_id=1, source_target_pairs={{0,2},{1,3},{2,0},{3,1},{4,6},{5,7},{6,4},{7,5},{8,10},{9,11},{10,... | collective-permute-start | bytes 1769480 | tf_op jit(solution)/shard_map/ppermute | solution.py:261
  17.5 94.8 %collective-permute-start.2 = (bf16[8,3,16,768]{3,2,1,0:T(8,128)(2,1)}, bf16[8,3,16,768]{3,2,1,0:T(8,128)(2,1)}, u32[]{:S(2)}, u32[]{:S(2)}) collective-permute-start(bf16[8,3,16,768]{3,2,1,0:T(8,128)(2,1)} %get-tuple-element.18), channel_id=1, source_target_pairs={{0,3},{1,0},{2,1},{3,2},{4,7},{5,4},{6,5},{7,6},{8,11},{9,8},{10,9... | collective-permute-start | bytes 1769480 | tf_op jit(solution)/shard_map/ppermute | solution.py:261
  99.5 12.0 %copy-start.4 = (f32[768]{0:T(1024)S(1)}, f32[768]{0:T(1024)}, u32[]{:S(2)}) copy-start(f32[768]{0:T(1024)} %param.6) | copy-start | bytes 9220
  99.5 45.8 %copy-start = (bf16[8,3,16,768]{3,2,1,0:T(8,128)(2,1)S(1)}, bf16[8,3,16,768]{3,2,1,0:T(8,128)(2,1)}, u32[]{:S(2)}) copy-start(bf16[8,3,16,768]{3,2,1,0:T(8,128)(2,1)} %get-tuple-element.15.refs_0_) | copy-start | bytes 1769476
  101.4 17.9 %collective-permute-start.4 = (bf16[8,3,16,768]{3,2,1,0:T(8,128)(2,1)S(1)}, bf16[8,3,16,768]{3,2,1,0:T(8,128)(2,1)S(1)}, u32[]{:S(2)}, u32[]{:S(2)}) collective-permute-start(bf16[8,3,16,768]{3,2,1,0:T(8,128)(2,1)S(1)} %get-tuple-element.21), channel_id=1, source_target_pairs={{0,1},{1,2},{2,3},{3,0},{4,5},{5,6},{6,7},{7,4},{8,9},{9,10},{10,1... | collective-permute-start | bytes 1769480 | tf_op jit(solution)/shard_map/ppermute | solution.py:261
  106.4 38.9 %collective-permute-start.5 = (bf16[8,3,16,768]{3,2,1,0:T(8,128)(2,1)S(1)}, bf16[8,3,16,768]{3,2,1,0:T(8,128)(2,1)S(1)}, u32[]{:S(2)}, u32[]{:S(2)}) collective-permute-start(bf16[8,3,16,768]{3,2,1,0:T(8,128)(2,1)S(1)} %get-tuple-element.22), channel_id=1, source_target_pairs={{0,2},{1,3},{2,0},{3,1},{4,6},{5,7},{6,4},{7,5},{8,10},{9,11},{10,... | collective-permute-start | bytes 1769480 | tf_op jit(solution)/shard_map/ppermute | solution.py:261
  108.0 37.3 %collective-permute-start.6 = (bf16[8,3,16,768]{3,2,1,0:T(8,128)(2,1)S(1)}, bf16[8,3,16,768]{3,2,1,0:T(8,128)(2,1)S(1)}, u32[]{:S(2)}, u32[]{:S(2)}) collective-permute-start(bf16[8,3,16,768]{3,2,1,0:T(8,128)(2,1)S(1)} %get-tuple-element.23), channel_id=1, source_target_pairs={{0,3},{1,0},{2,1},{3,2},{4,7},{5,4},{6,5},{7,6},{8,11},{9,8},{10,9... | collective-permute-start | bytes 1769480 | tf_op jit(solution)/shard_map/ppermute | solution.py:261
  151.7 6.9 %collective-permute-start.9 = (f32[8,32,128]{2,1,0:T(8,128)S(1)}, f32[8,32,128]{2,1,0:T(8,128)S(1)}, u32[]{:S(2)}, u32[]{:S(2)}) collective-permute-start(f32[8,32,128]{2,1,0:T(8,128)S(1)} %get-tuple-element.24), channel_id=1, source_target_pairs={{0,192},{4,196},{8,200},{12,204},{16,208},{20,212},{24,216},{28,22... | collective-permute-start | bytes 393224 | tf_op jit(solution)/shard_map/ppermute | solution.py:256
  151.8 6.8 %collective-permute-start.8 = (f32[8,32,128]{2,1,0:T(8,128)S(1)}, f32[8,32,128]{2,1,0:T(8,128)S(1)}, u32[]{:S(2)}, u32[]{:S(2)}) collective-permute-start(f32[8,32,128]{2,1,0:T(8,128)S(1)} %get-tuple-element.24), channel_id=1, source_target_pairs={{0,128},{4,132},{8,136},{12,140},{16,144},{20,148},{24,152},{28,15... | collective-permute-start | bytes 393224 | tf_op jit(solution)/shard_map/ppermute | solution.py:256
  151.9 7.2 %collective-permute-start.7 = (f32[8,32,128]{2,1,0:T(8,128)S(1)}, f32[8,32,128]{2,1,0:T(8,128)S(1)}, u32[]{:S(2)}, u32[]{:S(2)}) collective-permute-start(f32[8,32,128]{2,1,0:T(8,128)S(1)} %get-tuple-element.24), channel_id=1, source_target_pairs={{0,64},{4,68},{8,72},{12,76},{16,80},{20,84},{24,88},{28,92},{32,9... | collective-permute-start | bytes 393224 | tf_op jit(solution)/shard_map/ppermute | solution.py:256
  159.2 6.5 %collective-permute-start.12 = (f32[8,32,128]{2,1,0:T(8,128)S(1)}, f32[8,32,128]{2,1,0:T(8,128)S(1)}, u32[]{:S(2)}, u32[]{:S(2)}) collective-permute-start(f32[8,32,128]{2,1,0:T(8,128)S(1)} %add_add_fusion.1), channel_id=1, source_target_pairs={{0,48},{4,52},{8,56},{12,60},{16,32},{20,36},{24,40},{28,44},{32,1... | collective-permute-start | bytes 393224 | tf_op jit(solution)/shard_map/ppermute | solution.py:256
  159.3 6.4 %collective-permute-start.11 = (f32[8,32,128]{2,1,0:T(8,128)S(1)}, f32[8,32,128]{2,1,0:T(8,128)S(1)}, u32[]{:S(2)}, u32[]{:S(2)}) collective-permute-start(f32[8,32,128]{2,1,0:T(8,128)S(1)} %add_add_fusion.1), channel_id=1, source_target_pairs={{0,32},{4,36},{8,40},{12,44},{16,48},{20,52},{24,56},{28,60},{32,0... | collective-permute-start | bytes 393224 | tf_op jit(solution)/shard_map/ppermute | solution.py:256
  159.4 6.9 %collective-permute-start.10 = (f32[8,32,128]{2,1,0:T(8,128)S(1)}, f32[8,32,128]{2,1,0:T(8,128)S(1)}, u32[]{:S(2)}, u32[]{:S(2)}) collective-permute-start(f32[8,32,128]{2,1,0:T(8,128)S(1)} %add_add_fusion.1), channel_id=1, source_target_pairs={{0,16},{4,20},{8,24},{12,28},{16,0},{20,4},{24,8},{28,12},{32,48},... | collective-permute-start | bytes 393224 | tf_op jit(solution)/shard_map/ppermute | solution.py:256
  166.3 6.2 %collective-permute-start.15 = (f32[8,32,128]{2,1,0:T(8,128)S(1)}, f32[8,32,128]{2,1,0:T(8,128)S(1)}, u32[]{:S(2)}, u32[]{:S(2)}) collective-permute-start(f32[8,32,128]{2,1,0:T(8,128)S(1)} %add_add_fusion.t0), channel_id=1, source_target_pairs={{0,12},{4,8},{8,4},{12,0},{16,28},{20,24},{24,20},{28,16},{32,44},... | collective-permute-start | bytes 393224 | tf_op jit(solution)/shard_map/ppermute | solution.py:256
  166.4 11.2 %collective-permute-start.14 = (f32[8,32,128]{2,1,0:T(8,128)S(1)}, f32[8,32,128]{2,1,0:T(8,128)S(1)}, u32[]{:S(2)}, u32[]{:S(2)}) collective-permute-start(f32[8,32,128]{2,1,0:T(8,128)S(1)} %add_add_fusion.t0), channel_id=1, source_target_pairs={{0,8},{4,12},{8,0},{12,4},{16,24},{20,28},{24,16},{28,20},{32,40},... | collective-permute-start | bytes 393224 | tf_op jit(solution)/shard_map/ppermute | solution.py:256
  172.5 5.2 %collective-permute-start.13 = (f32[8,32,128]{2,1,0:T(8,128)S(1)}, f32[8,32,128]{2,1,0:T(8,128)S(1)}, u32[]{:S(2)}, u32[]{:S(2)}) collective-permute-start(f32[8,32,128]{2,1,0:T(8,128)S(1)} %add_add_fusion.t0), channel_id=1, source_target_pairs={{0,4},{4,0},{8,12},{12,8},{16,20},{20,16},{24,28},{28,24},{32,36},... | collective-permute-start | bytes 393224 | tf_op jit(solution)/shard_map/ppermute | solution.py:256

commit v3 on v2

--- a/solution.py
+++ b/solution.py
@@ -21,6 +21,7 @@
 HERE = SLOTS // TM
 BODY = HALF * HOP
 ALL = (0, HERE // 2)
+PARTS = ((0, 5), (5, HERE // 2))
 LONG = 10**12
 F32, BF16 = jnp.float32, jnp.bfloat16
 ANY = pl.BlockSpec(memory_space=pl.ANY)
@@ -41,59 +42,68 @@
     return np.stack([real_rows, imag_rows], axis=1).astype(ml_dtypes.bfloat16)
 
 
-def banded_table():
+def banded_tables():
     table = transform_table()
-    band = np.zeros((SLOTS, 2, HALF, BODY + HOP), ml_dtypes.bfloat16)
-    for b in range(HALF):
-        band[:, :, b, b * HOP : b * HOP + NFFT] = table
-    return band.reshape(TM, HERE * 2 * HALF, BODY + HOP)
-
-
-def transform_kernel(pairs, late, band, main, *rest):
+
+    def band(starts, span):
+        rows = np.zeros((SLOTS, 2, HALF, span), ml_dtypes.bfloat16)
+        for b, start in enumerate(starts):
+            rows[:, :, b, start : start + NFFT] = table
+        return rows.reshape(TM, HERE * 2 * HALF, span)
+
+    starts = [b * HOP for b in range(HALF)]
+    late = [band(starts, BODY + 2 * HOP), band(starts[:-1] + [BODY], BODY + 2 * HOP)]
+    return band(starts, BODY + HOP), np.concatenate(late, 0)
+
+
+def core():
+    return lax.axis_index("space") % 2
+
+
+def pick(flag, yes, no):
+    chosen = jnp.full(yes.shape, flag.astype(jnp.int32), jnp.int32) > 0
+    return jnp.where(chosen, yes.astype(F32), no.astype(F32)).astype(BF16)
+
+
+def apply_band(pairs, band, base, main, after, outs):
     rank = lax.axis_index("tm")
-    if late:
-        outs = rest[2:]
-        follow, tail = rest[:2]
-        last = (rank == TM - 1).astype(jnp.int32)
-        pick = jnp.full((HOP, PDEV), last, jnp.int32) > 0
-        after = jnp.where(pick, tail[0].astype(F32), follow[0].astype(F32)).astype(BF16)
-    else:
-        outs = rest[1:]
-        after = rest[0][0]
     first, stop = (4 * HALF * p for p in pairs)
-    rows = jnp.concatenate([band[(rank + k) % TM, first:stop] for k in range(TM)], 0)
-    got = jnp.dot(rows[:, :BODY], main[0], preferred_element_type=F32)
+    rows = jnp.concatenate([band[base + (rank + k) % TM, first:stop] for k in range(TM)], 0)
+    got = jnp.dot(rows[:, :BODY], main, preferred_element_type=F32)
     got += jnp.dot(rows[:, BODY:], after, preferred_element_type=F32)
     got = got.astype(BF16).reshape(TM, pairs[1] - pairs[0], 4 * HALF, PDEV)
-    for k, out in enumerate(outs[:TM]):
+    for k, out in enumerate(outs):
         out[:, 0] = got[k]
-    if len(outs) > TM:
-        outs[TM][...] = main[:, :HOP]
-
-
-def transform(band, snaps, pairs, half, ends=(), edge=False):
+
+
+def early_kernel(pairs, band, main, after, *outs):
+    apply_band(pairs, band, 0, main[0], after[0], outs)
+
+
+def late_kernel(pairs, band, main, head, moved, tail, *outs):
+    rank = lax.axis_index("tm")
+    half = pick((rank == TM - 1) & (core() == 0), tail[0], moved[0])
+    start = pick((rank == 0) & (core() == 1), tail[0], head[0])
+    apply_band(pairs, band, TM * core(), main[0], jnp.concatenate([half, start], 0), outs)
+
+
+def transform(kernel, pairs, band, blocks, limit):
     count = pairs[1] - pairs[0]
-    piece = jax.ShapeDtypeStruct((count, 3, 4 * HALF, PDEV), BF16)
-    strip = jax.ShapeDtypeStruct((3, HOP, PDEV), BF16)
-    if half:
-        ends_specs = [pl.BlockSpec((1, HOP, PDEV), lambda c: (c, 0, 0))] * 2
-    else:
-        ends, ends_specs = (snaps,), [pl.BlockSpec((1, HOP, PDEV), lambda c: (c, HALF, 0))]
+
+    def block(span, at):
+        return pl.BlockSpec((1, span, PDEV), lambda c: (c, at, 0))
+
     return pl.pallas_call(
-        functools.partial(transform_kernel, pairs, half),
+        functools.partial(kernel, pairs),
         grid=(3,),
-        in_specs=[
-            pl.BlockSpec(band.shape, lambda c: (0, 0, 0)),
-            pl.BlockSpec((1, BODY, PDEV), lambda c: (c, half, 0)),
-        ]
-        + ends_specs,
-        out_specs=[pl.BlockSpec((count, 1, 4 * HALF, PDEV), lambda c: (0, c, 0, 0))] * TM
-        + [pl.BlockSpec((1, HOP, PDEV), lambda c: (c, 0, 0))] * edge,
-        out_shape=[piece] * TM + [strip] * edge,
-        compiler_params=pltpu.CompilerParams(vmem_limit_bytes=PART if half else WHOLE),
+        in_specs=[pl.BlockSpec(band.shape, lambda c: (0, 0, 0))]
+        + [block(span, at) for _, span, at in blocks],
+        out_specs=[pl.BlockSpec((count, 1, 4 * HALF, PDEV), lambda c: (0, c, 0, 0))] * TM,
+        out_shape=[jax.ShapeDtypeStruct((count, 3, 4 * HALF, PDEV), BF16)] * TM,
+        compiler_params=pltpu.CompilerParams(vmem_limit_bytes=limit),
         cost_estimate=pl.CostEstimate(flops=LONG, bytes_accessed=0, transcendentals=0),
         name="transform",
-    )(band, snaps, *ends)
+    )(band, *(array for array, _, _ in blocks))
 
 
 def zero_lanes(first_pair, pair):
@@ -114,7 +124,9 @@
         held[(rank + TM - k) % TM, 0] = early[k][0]
         held[(rank + TM - k) % TM, 1] = late[k][0]
     weights = volume[...]
-    upper = lax.broadcasted_iota(jnp.int32, (OWN, PDEV), 0) < HALF
+    row = lax.broadcasted_iota(jnp.int32, (OWN, PDEV), 0)
+    upper = row < HALF
+    moved = (row % HALF) >= jnp.where(core() == 1, HALF - 1, HALF)
     total = jnp.zeros((4 * NB, 4 * NB), F32)
     for c in range(3):
         rows = []
@@ -123,6 +135,8 @@
             for q in range(TM):
                 a = held[q, 0, c].astype(F32)[s * OWN : (s + 1) * OWN]
                 b = held[q, 1, c].astype(F32)[s * OWN : (s + 1) * OWN]
+                after = held[(q + 1) % TM, 1, c].astype(F32)[s * OWN : (s + 1) * OWN]
+                b = jnp.where(moved, after, b)
                 real.append(jnp.where(upper, a, pltpu.roll(b, HALF, 0)))
                 imag.append(jnp.where(upper, pltpu.roll(a, HALF, 0), b))
             rows += real + imag
@@ -256,6 +270,17 @@
     return lax.ppermute(block, "space", route)
 
 
+def half_block_route():
+    route = []
+    for s in range(lax.axis_size("space")):
+        for t in range(TM):
+            if s % 2 == 1:
+                route.append((s * TM + t, s * TM + (t + 1) % TM))
+            elif t:
+                route.append((s * TM + t, s * TM + t - 1))
+    return route
+
+
 def from_behind(block, distance):
     route = [(i, (i + distance) % TM) for i in range(TM)]
     return lax.ppermute(block, "tm", route)
@@ -278,12 +303,16 @@
     snaps = jnp.transpose(snapshots, (1, 0, 2))
     tail = jnp.transpose(tail, (1, 0, 2))
     weights = volume.reshape(1, PDEV)
-    band = jnp.asarray(banded_table())
-    *first, edge = transform(band, snaps, ALL, 0, edge=True)
-    early = to_owners(first)
-    follow = lax.ppermute(edge, "tm", [(i, i - 1) for i in range(1, TM)])
-    late = to_owners(transform(band, snaps, ALL, 1, (follow, tail)))
-    terms, spec = gram_terms(ALL, ALL, early, late, weights)
+    early_band, late_band = (jnp.asarray(b) for b in banded_tables())
+    edge = lax.dynamic_slice_in_dim(snaps, core() * (OWN - 1) * HOP, HOP, 1)
+    moved = lax.ppermute(edge, ("space", "tm"), half_block_route())
+    blocks = [(snaps, BODY, 0), (snaps, HOP, HALF)]
+    early = to_owners(transform(early_kernel, ALL, early_band, blocks, WHOLE))
+    blocks = [(snaps, BODY, 1), (snaps, HOP, 0), (moved, HOP, 0), (tail, HOP, 0)]
+    late = [transform(late_kernel, part, late_band, blocks, PART) for part in PARTS]
+    late = [to_owners(pieces) for pieces in late]
+    sums = gram_terms(ALL, PARTS[0], early, late[0], weights, cost=LONG)
+    terms, spec = gram_terms(ALL, PARTS[1], early, late[1], weights, sums)
     gram, modes = project(ALL, sum_over_space(terms), spec, ())
     return gram, jnp.transpose(modes, (0, 1, 3, 2, 4))
 

time: 183 us -> 161 us (0.88); the launches traced: 183 us -> 159 us
  waiting for transfers between devices: 128 us -> 78.3 us
  starting transfers between devices: 36.2 us -> 53.3 us
  Pallas kernels: 18.4 us -> 24.8 us
    ppermute x1, waiting for transfers between devices: 80.8 us -> 0.01 us  [body(): moved = lax.ppermute(edge, ('space', 'tm'), half_block_route())]
    ppermute x6 -> x9, waiting for transfers between devices: 33.8 us -> 63.8 us  [from_behind(): return lax.ppermute(block, 'tm', route)]
    ppermute x6 -> x9, starting transfers between devices: 22.1 us -> 34.5 us  [from_behind(): return lax.ppermute(block, 'tm', route)]
    pallas_call x2 -> x3, Pallas kernels: 6.56 us -> 11.5 us  [transform(): pl.pallas_call(functools.partial(kernel, pairs), grid=(3,), in_specs=[pl....]
    ppermute x1, starting transfers between devices: 1.28 us -> 5.72 us  [body(): moved = lax.ppermute(edge, ('space', 'tm'), half_block_route())]
    pallas_call x1 -> x2, Pallas kernels: 6.42 us -> 7.89 us  [gram_terms(): pl.pallas_call(functools.partial(gram_kernel, pairs[0]), grid=(count,), i...]
  transfers between devices with their start and end apart: 16 -> 19, of which waited for: 9 -> 10; matrix products, arithmetic and copies ran while one was open for 0% -> 0% of each run, Pallas kernels for 1% -> 10%
where the time goes in v3:
time: 161 us; the launch traced here: 159 us
  waiting for transfers between devices  78.3 us (49%)
  starting transfers between devices  53.3 us (33%)
  Pallas kernels  24.8 us (15%)
  local copies, waits for them, and re-layouts  1.74 us (1%)
    ppermute x9, waiting for transfers between devices, from_behind(): return lax.ppermute(block, 'tm', route)  63.8 us
    ppermute x9, starting transfers between devices, from_behind(): return lax.ppermute(block, 'tm', route)  34.5 us
    ppermute x9, waiting for transfers between devices, over_space(): return lax.ppermute(block, 'space', route)  14.5 us
    ppermute x9, starting transfers between devices, over_space(): return lax.ppermute(block, 'space', route)  13.1 us
    pallas_call x3, Pallas kernels, transform(): pl.pallas_call(functools.partial(kernel, pairs), grid=(3,), in_specs=[pl....  11.5 us
    pallas_call x2, Pallas kernels, gram_terms(): pl.pallas_call(functools.partial(gram_kernel, pairs[0]), grid=(count,), i...  7.89 us
    ppermute x1, starting transfers between devices, body(): moved = lax.ppermute(edge, ('space', 'tm'), half_block_route())  5.72 us
    pallas_call x1, Pallas kernels, project(): pl.pallas_call(functools.partial(modes_kernel, pairs), grid=(count,), in_...  5.41 us
  transfers between devices with their start and end apart: 19, of which 10 were waited for; matrix products, arithmetic and copies ran while one was open for 0% of the time, Pallas kernels for 10%

profile of v3, /device:TPU:1, one launch (start us, length us, event | category | flops | bytes accessed | tf_op | source)
XLA Modules:
  0.0 159.1 jit_solution(1258906815041582622)
XLA Ops:
  0.6 1.7 %dynamic-slice_bitcast_fusion = bf16[3,64,768]{2,1,0:T(8,128)(2,1)} fusion(bf16[512,3,768]{2,0,1:T(8,128)(2,1)} %param.5, s32[]{:T(128)S(6)} %select_n.11), kind=kLoop, calls=%fused_computation | loop fusion | bytes 589828 | tf_op jit(solution)/shard_map/dynamic_slice | solution.py:307
  2.3 5.7 %collective-permute-start.3 = (bf16[3,64,768]{2,1,0:T(8,128)(2,1)}, bf16[3,64,768]{2,1,0:T(8,128)(2,1)}, u32[]{:S(2)}, u32[]{:S(2)}) collective-permute-start(bf16[3,64,768]{2,1,0:T(8,128)(2,1)} %dynamic-slice_bitcast_fusion), channel_id=1, source_target_pairs={{1,0},{2,1},{3,2},{4,5},{5,6},{6,7},{7,4},{9,8},{10,9},{11,10},{12... | collective-permute-start | bytes 884744 | tf_op jit(solution)/shard_map/ppermute | solution.py:308
  8.1 0.0 copy-start.4
  8.1 0.0 copy-start.1
  8.1 0.0 copy-start.2
  8.1 0.0 copy-start.3
  8.1 4.7 %transform.3 = (bf16[8,3,16,768]{3,2,1,0:T(8,128)(2,1)}, bf16[8,3,16,768]{3,2,1,0:T(8,128)(2,1)}, bf16[8,3,16,768]{3,2,1,0:T(8,128)(2,1)}, bf16[8,3,16,768]{3,2,1,0:T(8,128)(2,1)}) custom-call(bf16[4,128,320]{2,1,0:T(8,128)(2,1)} %constant.30.clone.band, bf16[3,512,768]{2,1,0:T(8,128)(2,1)} %bitcast.5, bf16[3,512,768]{2,1,0:T(8,128)(2,1)} %bitcast.6), custom_call_target="tpu_custom_call" | custom-call | flops 999999995904 | tf_op jit(solution)/shard_map/transform/pallas_call | solution.py:96
  12.8 4.2 %collective-permute-start = (bf16[8,3,16,768]{3,2,1,0:T(8,128)(2,1)}, bf16[8,3,16,768]{3,2,1,0:T(8,128)(2,1)}, u32[]{:S(2)}, u32[]{:S(2)}) collective-permute-start(bf16[8,3,16,768]{3,2,1,0:T(8,128)(2,1)} %get-tuple-element.21), channel_id=1, source_target_pairs={{0,1},{1,2},{2,3},{3,0},{4,5},{5,6},{6,7},{7,4},{8,9},{9,10},{10,1... | collective-permute-start | bytes 1769480 | tf_op jit(solution)/shard_map/ppermute | solution.py:286
  17.0 1.0 collective-permute-start.1
  18.0 3.5 %collective-permute-start.2 = (bf16[8,3,16,768]{3,2,1,0:T(8,128)(2,1)}, bf16[8,3,16,768]{3,2,1,0:T(8,128)(2,1)}, u32[]{:S(2)}, u32[]{:S(2)}) collective-permute-start(bf16[8,3,16,768]{3,2,1,0:T(8,128)(2,1)} %get-tuple-element.23), channel_id=1, source_target_pairs={{0,3},{1,0},{2,1},{3,2},{4,7},{5,4},{6,5},{7,6},{8,11},{9,8},{10,9... | collective-permute-start | bytes 1769480 | tf_op jit(solution)/shard_map/ppermute | solution.py:286
  21.5 0.0 copy-done.4
  21.5 0.0 collective-permute-done.3.moved
  21.5 0.0 copy-done.1
  21.5 0.0 copy-done.2
  21.5 0.0 copy-done.3
  21.5 3.5 %transform.5 = (bf16[5,3,16,768]{3,2,1,0:T(8,128)(2,1)S(1)}, bf16[5,3,16,768]{3,2,1,0:T(8,128)(2,1)}, bf16[5,3,16,768]{3,2,1,0:T(8,128)(2,1)}, bf16[5,3,16,768]{3,2,1,0:T(8,128)(2,1)}) custom-call(bf16[8,128,384]{2,1,0:T(8,128)(2,1)S(1)} %copy-done.3, bf16[3,512,768]{2,1,0:T(8,128)(2,1)S(1)} %bitcast.7, bf16[3,512,768]{2,1,0:T(8,128)(2,1)S(1)} %bitcast.8, ...), custom_call_target="tpu_custom_call" | custom-call | flops 999999995904 | tf_op jit(solution)/shard_map/transform/pallas_call | solution.py:96
  25.0 6.2 %collective-permute-start.7 = (bf16[5,3,16,768]{3,2,1,0:T(8,128)(2,1)}, bf16[5,3,16,768]{3,2,1,0:T(8,128)(2,1)}, u32[]{:S(2)}, u32[]{:S(2)}) collective-permute-start(bf16[5,3,16,768]{3,2,1,0:T(8,128)(2,1)} %get-tuple-element.29), channel_id=1, source_target_pairs={{0,1},{1,2},{2,3},{3,0},{4,5},{5,6},{6,7},{7,4},{8,9},{9,10},{10,1... | collective-permute-start | bytes 1105928 | tf_op jit(solution)/shard_map/ppermute | solution.py:286
  31.3 4.2 %collective-permute-start.8 = (bf16[5,3,16,768]{3,2,1,0:T(8,128)(2,1)}, bf16[5,3,16,768]{3,2,1,0:T(8,128)(2,1)}, u32[]{:S(2)}, u32[]{:S(2)}) collective-permute-start(bf16[5,3,16,768]{3,2,1,0:T(8,128)(2,1)} %get-tuple-element.30), channel_id=1, source_target_pairs={{0,2},{1,3},{2,0},{3,1},{4,6},{5,7},{6,4},{7,5},{8,10},{9,11},{10,... | collective-permute-start | bytes 1105928 | tf_op jit(solution)/shard_map/ppermute | solution.py:286
  35.5 11.8 %collective-permute-done.refs_1_ = bf16[8,3,16,768]{3,2,1,0:T(8,128)(2,1)} collective-permute-done((bf16[8,3,16,768]{3,2,1,0:T(8,128)(2,1)}, bf16[8,3,16,768]{3,2,1,0:T(8,128)(2,1)}, u32[]{:S(2)}, u32[]{:S(2)}) %collective-permute-start) | collective-permute-done | bytes 589856 | tf_op jit(solution)/shard_map/ppermute | solution.py:286
  47.3 0.0 collective-permute-start.9
  47.3 0.0 copy-start
  47.3 3.3 %transform.4 = (bf16[3,3,16,768]{3,2,1,0:T(8,128)(2,1)S(1)}, bf16[3,3,16,768]{3,2,1,0:T(8,128)(2,1)}, bf16[3,3,16,768]{3,2,1,0:T(8,128)(2,1)}, bf16[3,3,16,768]{3,2,1,0:T(8,128)(2,1)}) custom-call(bf16[8,128,384]{2,1,0:T(8,128)(2,1)S(1)} %copy-done.3, bf16[3,512,768]{2,1,0:T(8,128)(2,1)S(1)} %bitcast.9, bf16[3,512,768]{2,1,0:T(8,128)(2,1)S(1)} %bitcast.10, ...), custom_call_target="tpu_custom_call" | custom-call | flops 999999995904 | tf_op jit(solution)/shard_map/transform/pallas_call | solution.py:96
  50.6 23.7 %collective-permute-done.1.refs_2_ = bf16[8,3,16,768]{3,2,1,0:T(8,128)(2,1)} collective-permute-done((bf16[8,3,16,768]{3,2,1,0:T(8,128)(2,1)}, bf16[8,3,16,768]{3,2,1,0:T(8,128)(2,1)}, u32[]{:S(2)}, u32[]{:S(2)}) %collective-permute-start.1) | collective-permute-done | bytes 589856 | tf_op jit(solution)/shard_map/ppermute | solution.py:286
  74.4 10.2 %collective-permute-start.4 = (bf16[3,3,16,768]{3,2,1,0:T(8,128)(2,1)}, bf16[3,3,16,768]{3,2,1,0:T(8,128)(2,1)}, u32[]{:S(2)}, u32[]{:S(2)}) collective-permute-start(bf16[3,3,16,768]{3,2,1,0:T(8,128)(2,1)} %get-tuple-element.25), channel_id=1, source_target_pairs={{0,1},{1,2},{2,3},{3,0},{4,5},{5,6},{6,7},{7,4},{8,9},{9,10},{10,1... | collective-permute-start | bytes 663560 | tf_op jit(solution)/shard_map/ppermute | solution.py:286
  84.6 25.4 %collective-permute-done.2.refs_3_ = bf16[8,3,16,768]{3,2,1,0:T(8,128)(2,1)} collective-permute-done((bf16[8,3,16,768]{3,2,1,0:T(8,128)(2,1)}, bf16[8,3,16,768]{3,2,1,0:T(8,128)(2,1)}, u32[]{:S(2)}, u32[]{:S(2)}) %collective-permute-start.2) | collective-permute-done | bytes 589856 | tf_op jit(solution)/shard_map/ppermute | solution.py:286
  109.9 4.1 %collective-permute-start.5 = (bf16[3,3,16,768]{3,2,1,0:T(8,128)(2,1)}, bf16[3,3,16,768]{3,2,1,0:T(8,128)(2,1)}, u32[]{:S(2)}, u32[]{:S(2)}) collective-permute-start(bf16[3,3,16,768]{3,2,1,0:T(8,128)(2,1)} %get-tuple-element.26), channel_id=1, source_target_pairs={{0,2},{1,3},{2,0},{3,1},{4,6},{5,7},{6,4},{7,5},{8,10},{9,11},{10,... | collective-permute-start | bytes 663560 | tf_op jit(solution)/shard_map/ppermute | solution.py:286
  114.1 0.0 collective-permute-done.7.refs_5_
  114.1 1.0 collective-permute-start.6
  115.1 0.0 collective-permute-done.8.refs_6_
  115.1 2.7 %collective-permute-done.9.refs_7_ = bf16[5,3,16,768]{3,2,1,0:T(8,128)(2,1)} collective-permute-done((bf16[5,3,16,768]{3,2,1,0:T(8,128)(2,1)}, bf16[5,3,16,768]{3,2,1,0:T(8,128)(2,1)}, u32[]{:S(2)}, u32[]{:S(2)}) %collective-permute-start.9) | collective-permute-done | bytes 368672 | tf_op jit(solution)/shard_map/ppermute | solution.py:286
  117.8 0.0 copy-done
  117.8 4.7 %gram_terms.2 = (f32[8,32,128]{2,1,0:T(8,128)S(1)}, bf16[8,3,128,768]{3,2,1,0:T(8,128)(2,1)S(1)}) custom-call(bf16[8,3,16,768]{3,2,1,0:T(8,128)(2,1)S(1)} %copy-done, bf16[8,3,16,768]{3,2,1,0:T(8,128)(2,1)} %collective-permute-done.refs_1_, bf16[8,3,16,768]{3,2,1,0:T(8,128)(2,1)} %collective-permute-done.1.refs_2_, ...), custom_call_target="tpu_custom_call" | custom-call | flops 999999995904 | tf_op jit(solution)/shard_map/gram_terms/pallas_call | solution.py:164
  122.6 0.0 collective-permute-done.4.refs_5_
  122.6 0.2 collective-permute-done.5.refs_6_
  122.8 0.0 collective-permute-done.6.refs_7_
  122.8 3.2 %gram_terms.3 = (f32[8,32,128]{2,1,0:T(8,128)S(1)}, bf16[8,3,128,768]{3,2,1,0:T(8,128)(2,1)S(1)}) custom-call(bf16[8,3,16,768]{3,2,1,0:T(8,128)(2,1)S(1)} %copy-done, bf16[8,3,16,768]{3,2,1,0:T(8,128)(2,1)} %collective-permute-done.refs_1_, bf16[8,3,16,768]{3,2,1,0:T(8,128)(2,1)} %collective-permute-done.1.refs_2_, ...), custom_call_target="tpu_custom_call", output_to_operand_aliasing={{0}: (9, {}), {1}: (10, {})} | custom-call | tf_op jit(solution)/shard_map/gram_terms/pallas_call | solution.py:164
  125.9 2.6 %collective-permute-start.12 = (f32[8,32,128]{2,1,0:T(8,128)S(1)}, f32[8,32,128]{2,1,0:T(8,128)S(1)}, u32[]{:S(2)}, u32[]{:S(2)}) collective-permute-start(f32[8,32,128]{2,1,0:T(8,128)S(1)} %get-tuple-element.34), channel_id=1, source_target_pairs={{0,192},{4,196},{8,200},{12,204},{16,208},{20,212},{24,216},{28,22... | collective-permute-start | bytes 393224 | tf_op jit(solution)/shard_map/ppermute | solution.py:270
  128.5 0.5 collective-permute-start.11
  129.0 0.2 collective-permute-start.10
  129.3 3.6 %collective-permute-done.12 = f32[8,32,128]{2,1,0:T(8,128)S(1)} collective-permute-done((f32[8,32,128]{2,1,0:T(8,128)S(1)}, f32[8,32,128]{2,1,0:T(8,128)S(1)}, u32[]{:S(2)}, u32[]{:S(2)}) %collective-permute-start.12) | collective-permute-done | bytes 131104 | tf_op jit(solution)/shard_map/ppermute | solution.py:270
  132.8 1.1 collective-permute-done.11
  133.9 0.0 collective-permute-done.10
  134.0 2.8 %collective-permute-start.15 = (f32[8,32,128]{2,1,0:T(8,128)S(1)}, f32[8,32,128]{2,1,0:T(8,128)S(1)}, u32[]{:S(2)}, u32[]{:S(2)}) collective-permute-start(f32[8,32,128]{2,1,0:T(8,128)S(1)} %add_add_fusion.1), channel_id=1, source_target_pairs={{0,48},{4,52},{8,56},{12,60},{16,32},{20,36},{24,40},{28,44},{32,1... | collective-permute-start | bytes 393224 | tf_op jit(solution)/shard_map/ppermute | solution.py:270
  136.8 0.3 collective-permute-start.14
  137.2 0.3 collective-permute-start.13
  137.5 2.6 %collective-permute-done.15 = f32[8,32,128]{2,1,0:T(8,128)S(1)} collective-permute-done((f32[8,32,128]{2,1,0:T(8,128)S(1)}, f32[8,32,128]{2,1,0:T(8,128)S(1)}, u32[]{:S(2)}, u32[]{:S(2)}) %collective-permute-start.15) | collective-permute-done | bytes 131104 | tf_op jit(solution)/shard_map/ppermute | solution.py:270
  140.1 2.1 %collective-permute-done.14 = f32[8,32,128]{2,1,0:T(8,128)S(1)} collective-permute-done((f32[8,32,128]{2,1,0:T(8,128)S(1)}, f32[8,32,128]{2,1,0:T(8,128)S(1)}, u32[]{:S(2)}, u32[]{:S(2)}) %collective-permute-start.14) | collective-permute-done | bytes 131104 | tf_op jit(solution)/shard_map/ppermute | solution.py:270
  142.2 0.0 collective-permute-done.13
  142.2 0.1 collective-permute-start.18
  142.3 6.2 %collective-permute-start.17 = (f32[8,32,128]{2,1,0:T(8,128)S(1)}, f32[8,32,128]{2,1,0:T(8,128)S(1)}, u32[]{:S(2)}, u32[]{:S(2)}) collective-permute-start(f32[8,32,128]{2,1,0:T(8,128)S(1)} %add_add_fusion.t0), channel_id=1, source_target_pairs={{0,8},{4,12},{8,0},{12,4},{16,24},{20,28},{24,16},{28,20},{32,40},... | collective-permute-start | bytes 393224 | tf_op jit(solution)/shard_map/ppermute | solution.py:270
  148.5 0.0 collective-permute-start.16
  148.5 0.0 collective-permute-done.18.t3
  148.5 5.2 %collective-permute-done.17.t2 = f32[8,32,128]{2,1,0:T(8,128)S(1)} collective-permute-done((f32[8,32,128]{2,1,0:T(8,128)S(1)}, f32[8,32,128]{2,1,0:T(8,128)S(1)}, u32[]{:S(2)}, u32[]{:S(2)}) %collective-permute-start.17) | collective-permute-done | bytes 131104 | tf_op jit(solution)/shard_map/ppermute | solution.py:270
  153.6 0.0 collective-permute-done.16.t1
  153.6 5.4 %modes.1 = (f32[16,2,32,32]{3,2,1,0:T(8,128)}, bf16[16,2,3,32,768]{4,3,2,1,0:T(8,128)(2,1)}) custom-call(f32[8,32,128]{2,1,0:T(8,128)S(1)} %add_add_fusion.t0, f32[8,32,128]{2,1,0:T(8,128)S(1)} %collective-permute-done.16.t1, f32[8,32,128]{2,1,0:T(8,128)S(1)} %collective-permute-done.17.t2, f32[8,32,128]{2,1,0:T(8,128)S(1)} %collective-permute-done.18.t3, ...), custom_call_target="tpu_custom_call" | custom-call | tf_op jit(solution)/shard_map/modes/pallas_call | solution.py:243
  (3 shorter events, 0.1 us)
Async XLA Ops:
  2.3 19.1 %collective-permute-start.3 = (bf16[3,64,768]{2,1,0:T(8,128)(2,1)}, bf16[3,64,768]{2,1,0:T(8,128)(2,1)}, u32[]{:S(2)}, u32[]{:S(2)}) collective-permute-start(bf16[3,64,768]{2,1,0:T(8,128)(2,1)} %dynamic-slice_bitcast_fusion), channel_id=1, source_target_pairs={{1,0},{2,1},{3,2},{4,5},{5,6},{6,7},{7,4},{9,8},{10,9},{11,10},{12... | collective-permute-start | bytes 884744 | tf_op jit(solution)/shard_map/ppermute | solution.py:308
  8.1 13.4 %copy-start.4 = (f32[768]{0:T(1024)S(1)}, f32[768]{0:T(1024)}, u32[]{:S(2)}) copy-start(f32[768]{0:T(1024)} %param.7) | copy-start | bytes 9220
  8.1 13.4 %copy-start.1 = (bf16[512,3,768]{2,0,1:T(8,128)(2,1)S(1)}, bf16[512,3,768]{2,0,1:T(8,128)(2,1)}, u32[]{:S(2)}) copy-start(bf16[512,3,768]{2,0,1:T(8,128)(2,1)} %param.5) | copy-start | bytes 7077892
  8.1 13.4 %copy-start.2 = (bf16[64,3,768]{2,0,1:T(8,128)(2,1)S(1)}, bf16[64,3,768]{2,0,1:T(8,128)(2,1)}, u32[]{:S(2)}) copy-start(bf16[64,3,768]{2,0,1:T(8,128)(2,1)} %param.6) | copy-start | bytes 884740
  8.1 13.4 %copy-start.3 = (bf16[8,128,384]{2,1,0:T(8,128)(2,1)S(1)}, bf16[8,128,384]{2,1,0:T(8,128)(2,1)}, u32[]{:S(2)}) copy-start(bf16[8,128,384]{2,1,0:T(8,128)(2,1)} %constant.31.clone.band) | copy-start | bytes 2359300
  12.8 34.5 %collective-permute-start = (bf16[8,3,16,768]{3,2,1,0:T(8,128)(2,1)}, bf16[8,3,16,768]{3,2,1,0:T(8,128)(2,1)}, u32[]{:S(2)}, u32[]{:S(2)}) collective-permute-start(bf16[8,3,16,768]{3,2,1,0:T(8,128)(2,1)} %get-tuple-element.21), channel_id=1, source_target_pairs={{0,1},{1,2},{2,3},{3,0},{4,5},{5,6},{6,7},{7,4},{8,9},{9,10},{10,1... | collective-permute-start | bytes 1769480 | tf_op jit(solution)/shard_map/ppermute | solution.py:286
  17.0 57.4 %collective-permute-start.1 = (bf16[8,3,16,768]{3,2,1,0:T(8,128)(2,1)}, bf16[8,3,16,768]{3,2,1,0:T(8,128)(2,1)}, u32[]{:S(2)}, u32[]{:S(2)}) collective-permute-start(bf16[8,3,16,768]{3,2,1,0:T(8,128)(2,1)} %get-tuple-element.22), channel_id=1, source_target_pairs={{0,2},{1,3},{2,0},{3,1},{4,6},{5,7},{6,4},{7,5},{8,10},{9,11},{10,... | collective-permute-start | bytes 1769480 | tf_op jit(solution)/shard_map/ppermute | solution.py:286
  18.0 92.0 %collective-permute-start.2 = (bf16[8,3,16,768]{3,2,1,0:T(8,128)(2,1)}, bf16[8,3,16,768]{3,2,1,0:T(8,128)(2,1)}, u32[]{:S(2)}, u32[]{:S(2)}) collective-permute-start(bf16[8,3,16,768]{3,2,1,0:T(8,128)(2,1)} %get-tuple-element.23), channel_id=1, source_target_pairs={{0,3},{1,0},{2,1},{3,2},{4,7},{5,4},{6,5},{7,6},{8,11},{9,8},{10,9... | collective-permute-start | bytes 1769480 | tf_op jit(solution)/shard_map/ppermute | solution.py:286
  25.0 89.0 %collective-permute-start.7 = (bf16[5,3,16,768]{3,2,1,0:T(8,128)(2,1)}, bf16[5,3,16,768]{3,2,1,0:T(8,128)(2,1)}, u32[]{:S(2)}, u32[]{:S(2)}) collective-permute-start(bf16[5,3,16,768]{3,2,1,0:T(8,128)(2,1)} %get-tuple-element.29), channel_id=1, source_target_pairs={{0,1},{1,2},{2,3},{3,0},{4,5},{5,6},{6,7},{7,4},{8,9},{9,10},{10,1... | collective-permute-start | bytes 1105928 | tf_op jit(solution)/shard_map/ppermute | solution.py:286
  31.3 83.8 %collective-permute-start.8 = (bf16[5,3,16,768]{3,2,1,0:T(8,128)(2,1)}, bf16[5,3,16,768]{3,2,1,0:T(8,128)(2,1)}, u32[]{:S(2)}, u32[]{:S(2)}) collective-permute-start(bf16[5,3,16,768]{3,2,1,0:T(8,128)(2,1)} %get-tuple-element.30), channel_id=1, source_target_pairs={{0,2},{1,3},{2,0},{3,1},{4,6},{5,7},{6,4},{7,5},{8,10},{9,11},{10,... | collective-permute-start | bytes 1105928 | tf_op jit(solution)/shard_map/ppermute | solution.py:286
  47.3 70.6 %collective-permute-start.9 = (bf16[5,3,16,768]{3,2,1,0:T(8,128)(2,1)}, bf16[5,3,16,768]{3,2,1,0:T(8,128)(2,1)}, u32[]{:S(2)}, u32[]{:S(2)}) collective-permute-start(bf16[5,3,16,768]{3,2,1,0:T(8,128)(2,1)} %get-tuple-element.31), channel_id=1, source_target_pairs={{0,3},{1,0},{2,1},{3,2},{4,7},{5,4},{6,5},{7,6},{8,11},{9,8},{10,9... | collective-permute-start | bytes 1105928 | tf_op jit(solution)/shard_map/ppermute | solution.py:286
  47.3 70.6 %copy-start = (bf16[8,3,16,768]{3,2,1,0:T(8,128)(2,1)S(1)}, bf16[8,3,16,768]{3,2,1,0:T(8,128)(2,1)}, u32[]{:S(2)}) copy-start(bf16[8,3,16,768]{3,2,1,0:T(8,128)(2,1)} %get-tuple-element.20.refs_0_) | copy-start | bytes 1769476
  74.4 48.2 %collective-permute-start.4 = (bf16[3,3,16,768]{3,2,1,0:T(8,128)(2,1)}, bf16[3,3,16,768]{3,2,1,0:T(8,128)(2,1)}, u32[]{:S(2)}, u32[]{:S(2)}) collective-permute-start(bf16[3,3,16,768]{3,2,1,0:T(8,128)(2,1)} %get-tuple-element.25), channel_id=1, source_target_pairs={{0,1},{1,2},{2,3},{3,0},{4,5},{5,6},{6,7},{7,4},{8,9},{9,10},{10,1... | collective-permute-start | bytes 663560 | tf_op jit(solution)/shard_map/ppermute | solution.py:286
  109.9 12.8 %collective-permute-start.5 = (bf16[3,3,16,768]{3,2,1,0:T(8,128)(2,1)}, bf16[3,3,16,768]{3,2,1,0:T(8,128)(2,1)}, u32[]{:S(2)}, u32[]{:S(2)}) collective-permute-start(bf16[3,3,16,768]{3,2,1,0:T(8,128)(2,1)} %get-tuple-element.26), channel_id=1, source_target_pairs={{0,2},{1,3},{2,0},{3,1},{4,6},{5,7},{6,4},{7,5},{8,10},{9,11},{10,... | collective-permute-start | bytes 663560 | tf_op jit(solution)/shard_map/ppermute | solution.py:286
  114.1 8.7 %collective-permute-start.6 = (bf16[3,3,16,768]{3,2,1,0:T(8,128)(2,1)}, bf16[3,3,16,768]{3,2,1,0:T(8,128)(2,1)}, u32[]{:S(2)}, u32[]{:S(2)}) collective-permute-start(bf16[3,3,16,768]{3,2,1,0:T(8,128)(2,1)} %get-tuple-element.27), channel_id=1, source_target_pairs={{0,3},{1,0},{2,1},{3,2},{4,7},{5,4},{6,5},{7,6},{8,11},{9,8},{10,9... | collective-permute-start | bytes 663560 | tf_op jit(solution)/shard_map/ppermute | solution.py:286
  125.9 6.9 %collective-permute-start.12 = (f32[8,32,128]{2,1,0:T(8,128)S(1)}, f32[8,32,128]{2,1,0:T(8,128)S(1)}, u32[]{:S(2)}, u32[]{:S(2)}) collective-permute-start(f32[8,32,128]{2,1,0:T(8,128)S(1)} %get-tuple-element.34), channel_id=1, source_target_pairs={{0,192},{4,196},{8,200},{12,204},{16,208},{20,212},{24,216},{28,22... | collective-permute-start | bytes 393224 | tf_op jit(solution)/shard_map/ppermute | solution.py:270
  128.5 5.4 %collective-permute-start.11 = (f32[8,32,128]{2,1,0:T(8,128)S(1)}, f32[8,32,128]{2,1,0:T(8,128)S(1)}, u32[]{:S(2)}, u32[]{:S(2)}) collective-permute-start(f32[8,32,128]{2,1,0:T(8,128)S(1)} %get-tuple-element.34), channel_id=1, source_target_pairs={{0,128},{4,132},{8,136},{12,140},{16,144},{20,148},{24,152},{28,15... | collective-permute-start | bytes 393224 | tf_op jit(solution)/shard_map/ppermute | solution.py:270
  129.0 4.9 %collective-permute-start.10 = (f32[8,32,128]{2,1,0:T(8,128)S(1)}, f32[8,32,128]{2,1,0:T(8,128)S(1)}, u32[]{:S(2)}, u32[]{:S(2)}) collective-permute-start(f32[8,32,128]{2,1,0:T(8,128)S(1)} %get-tuple-element.34), channel_id=1, source_target_pairs={{0,64},{4,68},{8,72},{12,76},{16,80},{20,84},{24,88},{28,92},{32,9... | collective-permute-start | bytes 393224 | tf_op jit(solution)/shard_map/ppermute | solution.py:270
  134.0 6.1 %collective-permute-start.15 = (f32[8,32,128]{2,1,0:T(8,128)S(1)}, f32[8,32,128]{2,1,0:T(8,128)S(1)}, u32[]{:S(2)}, u32[]{:S(2)}) collective-permute-start(f32[8,32,128]{2,1,0:T(8,128)S(1)} %add_add_fusion.1), channel_id=1, source_target_pairs={{0,48},{4,52},{8,56},{12,60},{16,32},{20,36},{24,40},{28,44},{32,1... | collective-permute-start | bytes 393224 | tf_op jit(solution)/shard_map/ppermute | solution.py:270
  136.8 5.4 %collective-permute-start.14 = (f32[8,32,128]{2,1,0:T(8,128)S(1)}, f32[8,32,128]{2,1,0:T(8,128)S(1)}, u32[]{:S(2)}, u32[]{:S(2)}) collective-permute-start(f32[8,32,128]{2,1,0:T(8,128)S(1)} %add_add_fusion.1), channel_id=1, source_target_pairs={{0,32},{4,36},{8,40},{12,44},{16,48},{20,52},{24,56},{28,60},{32,0... | collective-permute-start | bytes 393224 | tf_op jit(solution)/shard_map/ppermute | solution.py:270
  137.2 5.0 %collective-permute-start.13 = (f32[8,32,128]{2,1,0:T(8,128)S(1)}, f32[8,32,128]{2,1,0:T(8,128)S(1)}, u32[]{:S(2)}, u32[]{:S(2)}) collective-permute-start(f32[8,32,128]{2,1,0:T(8,128)S(1)} %add_add_fusion.1), channel_id=1, source_target_pairs={{0,16},{4,20},{8,24},{12,28},{16,0},{20,4},{24,8},{28,12},{32,48},... | collective-permute-start | bytes 393224 | tf_op jit(solution)/shard_map/ppermute | solution.py:270
  142.2 6.3 %collective-permute-start.18 = (f32[8,32,128]{2,1,0:T(8,128)S(1)}, f32[8,32,128]{2,1,0:T(8,128)S(1)}, u32[]{:S(2)}, u32[]{:S(2)}) collective-permute-start(f32[8,32,128]{2,1,0:T(8,128)S(1)} %add_add_fusion.t0), channel_id=1, source_target_pairs={{0,12},{4,8},{8,4},{12,0},{16,28},{20,24},{24,20},{28,16},{32,44},... | collective-permute-start | bytes 393224 | tf_op jit(solution)/shard_map/ppermute | solution.py:270
  142.3 11.3 %collective-permute-start.17 = (f32[8,32,128]{2,1,0:T(8,128)S(1)}, f32[8,32,128]{2,1,0:T(8,128)S(1)}, u32[]{:S(2)}, u32[]{:S(2)}) collective-permute-start(f32[8,32,128]{2,1,0:T(8,128)S(1)} %add_add_fusion.t0), channel_id=1, source_target_pairs={{0,8},{4,12},{8,0},{12,4},{16,24},{20,28},{24,16},{28,20},{32,40},... | collective-permute-start | bytes 393224 | tf_op jit(solution)/shard_map/ppermute | solution.py:270
  148.5 5.2 %collective-permute-start.16 = (f32[8,32,128]{2,1,0:T(8,128)S(1)}, f32[8,32,128]{2,1,0:T(8,128)S(1)}, u32[]{:S(2)}, u32[]{:S(2)}) collective-permute-start(f32[8,32,128]{2,1,0:T(8,128)S(1)} %add_add_fusion.t0), channel_id=1, source_target_pairs={{0,4},{4,0},{8,12},{12,8},{16,20},{20,16},{24,28},{28,24},{32,36},... | collective-permute-start | bytes 393224 | tf_op jit(solution)/shard_map/ppermute | solution.py:270

commit v4 on v3

--- a/solution.py
+++ b/solution.py
@@ -21,7 +21,8 @@
 HERE = SLOTS // TM
 BODY = HALF * HOP
 ALL = (0, HERE // 2)
-PARTS = ((0, 5), (5, HERE // 2))
+QUADS = HERE // 4
+PARTS = ((0, 3), (3, QUADS))
 LONG = 10**12
 F32, BF16 = jnp.float32, jnp.bfloat16
 ANY = pl.BlockSpec(memory_space=pl.ANY)
@@ -106,9 +107,8 @@
     )(band, *(array for array, _, _ in blocks))
 
 
-def zero_lanes(first_pair, pair):
-    is_zero = (lax.axis_index("tm") == 0) & (pair + first_pair == 0)
-    return jnp.where(is_zero, 2 * NB, 0)
+def zero_lanes(is_first, lanes):
+    return jnp.where((lax.axis_index("tm") == 0) & is_first, lanes, 0)
 
 
 def lane_masks():
@@ -116,26 +116,44 @@
     return lane, lane < 2 * NB, (lane % (2 * NB)) < NB
 
 
-def gram_kernel(first_pair, *refs):
-    early, late, volume = refs[:TM], refs[TM : 2 * TM], refs[2 * TM]
-    terms, spec, held = refs[-3:]
+def triangle():
+    row = lax.broadcasted_iota(jnp.int32, (NB, 4 * NB), 0)
+    return row, lax.broadcasted_iota(jnp.int32, (NB, 4 * NB), 1) % NB
+
+
+def by_quarter(parts):
+    lane, _, _ = lane_masks()
+    out = parts[3]
+    for at in (2, 1, 0):
+        out = jnp.where(lane < (at + 1) * NB, parts[at], out)
+    return out
+
+
+def turn(x, quarters):
+    return pltpu.roll(x, (quarters % 4) * NB, 1) if quarters % 4 else x
+
+
+def transposed(four):
+    flipped = jnp.concatenate([four] * 4, 0).T
+    return by_quarter([flipped[g * NB : (g + 1) * NB] for g in range(4)])
+
+
+def pair_terms(early, late, volume, spec, pair, is_first):
     rank = lax.axis_index("tm")
-    for k in range(TM):
-        held[(rank + TM - k) % TM, 0] = early[k][0]
-        held[(rank + TM - k) % TM, 1] = late[k][0]
-    weights = volume[...]
     row = lax.broadcasted_iota(jnp.int32, (OWN, PDEV), 0)
     upper = row < HALF
     moved = (row % HALF) >= jnp.where(core() == 1, HALF - 1, HALF)
+    weights = volume[...]
     total = jnp.zeros((4 * NB, 4 * NB), F32)
     for c in range(3):
         rows = []
         for s in range(2):
+            half = slice(s * OWN, (s + 1) * OWN)
             real, imag = [], []
             for q in range(TM):
-                a = held[q, 0, c].astype(F32)[s * OWN : (s + 1) * OWN]
-                b = held[q, 1, c].astype(F32)[s * OWN : (s + 1) * OWN]
-                after = held[(q + 1) % TM, 1, c].astype(F32)[s * OWN : (s + 1) * OWN]
+                a = early[q, pair, c].astype(F32)[half]
+                b = late[q, pair, c].astype(F32)[half]
+                after = late[(q + 1) % TM, pair, c].astype(F32)[half]
                 b = jnp.where(moved, after, b)
                 real.append(jnp.where(upper, a, pltpu.roll(b, HALF, 0)))
                 imag.append(jnp.where(upper, pltpu.roll(a, HALF, 0), b))
@@ -143,53 +161,83 @@
         both = jnp.concatenate(rows, 0)
         plain = both.astype(BF16)
         weighted = (both * weights).astype(BF16)
-        spec[0, c] = plain
+        spec[pair, c] = plain
         total += lax.dot_general(
             weighted, plain, (((1,), (1,)), ((), ())), preferred_element_type=F32
         )
     lane, first, low = lane_masks()
     top = jnp.where(first, total[:NB], total[2 * NB : 3 * NB])
     bottom = jnp.where(first, total[NB : 2 * NB], total[3 * NB :])
-    summed = top + jnp.where(low, pltpu.roll(bottom, 3 * NB, 1), 0.0)
+    summed = top + jnp.where(low, turn(bottom, 3), 0.0)
+    if pair:
+        return summed
     apart = jnp.where(lane < NB, top, bottom)
-    terms[0] = jnp.where(lane < zero_lanes(first_pair, pl.program_id(0)), apart, summed)
-
-
-def gram_terms(group, pairs, early, late, volume, before=(), wait=(), cost=0):
-    count = pairs[1] - pairs[0]
-    skip = pairs[0] - group[0]
-    size = group[1] - group[0]
-    late_piece = pl.BlockSpec((1, 3, 4 * HALF, PDEV), lambda p: (p, 0, 0, 0))
-    early_piece = pl.BlockSpec((1, 3, 4 * HALF, PDEV), lambda p: (p + skip, 0, 0, 0))
+    return jnp.where(lane < zero_lanes(is_first, 2 * NB), apart, summed)
+
+
+def gram_kernel(quads, *refs):
+    pieces, volume = refs[: 2 * TM], refs[2 * TM]
+    terms, spec, early, late = refs[-4:]
+    step = pl.program_id(0)
+    rank = lax.axis_index("tm")
+    for k in range(TM):
+        early[(rank + TM - k) % TM] = pieces[k][...]
+        late[(rank + TM - k) % TM] = pieces[TM + k][...]
+
+    is_first = step + quads[0] == 0
+    if quads[0]:
+
+        @pl.when(step == 0)
+        def _():
+            terms[...] = refs[2 * TM + 1][...]
+
+    one, two = (pair_terms(early, late, volume, spec, p, is_first) for p in range(2))
+    sums = by_quarter([one, turn(one, -1), turn(two, 2), turn(two, 1)])
+    cross = by_quarter([turn(one, -1), turn(one, -2), turn(two, 1), two])
+    lane, _, _ = lane_masks()
+    zero = lane < zero_lanes(is_first, NB)
+    row, column = triangle()
+    below = jnp.where(zero, cross, cross - transposed(cross))
+    at = pl.multiple_of((step + quads[0]) * NB, NB)
+    terms[pl.ds(at, NB)] = jnp.where(row <= column, sums, below)
+    if not quads[0]:
+
+        @pl.when(step == 0)
+        def _():
+            diagonal = jnp.sum(jnp.where(row == column, cross, 0.0), 0, keepdims=True)
+            terms[QUADS * NB :] = jnp.broadcast_to(diagonal, (8, 4 * NB))
+
+
+def gram_terms(quads, early, late, volume, before=(), cost=0):
+    count, skip = quads[1] - quads[0], quads[0]
+    block = (2, 3, 4 * HALF, PDEV)
+    whole = ((QUADS * NB + 8), 4 * NB)
     return pl.pallas_call(
-        functools.partial(gram_kernel, pairs[0]),
+        functools.partial(gram_kernel, quads),
         grid=(count,),
-        in_specs=[early_piece] * TM
-        + [late_piece] * TM
+        in_specs=[pl.BlockSpec(block, lambda p: (p + skip, 0, 0, 0))] * TM
+        + [pl.BlockSpec(block, lambda p: (p, 0, 0, 0))] * TM
         + [pl.BlockSpec((1, PDEV), lambda p: (0, 0))]
-        + [ANY] * (len(before) + len(wait)),
+        + [pl.BlockSpec(whole, lambda p: (0, 0)), ANY][: len(before)],
         out_specs=[
-            pl.BlockSpec((1, NB, 4 * NB), lambda p: (p + skip, 0, 0)),
-            pl.BlockSpec((1, 3, 4 * NB, PDEV), lambda p: (p + skip, 0, 0, 0)),
+            pl.BlockSpec(whole, lambda p: (0, 0)),
+            pl.BlockSpec((2, 3, 4 * NB, PDEV), lambda p: (p + skip, 0, 0, 0)),
         ],
         out_shape=[
-            jax.ShapeDtypeStruct((size, NB, 4 * NB), F32),
-            jax.ShapeDtypeStruct((size, 3, 4 * NB, PDEV), BF16),
-        ],
-        scratch_shapes=[pltpu.VMEM((TM, 2, 3, 4 * HALF, PDEV), BF16)],
-        input_output_aliases={2 * TM + 1 + i: i for i in range(len(before))},
+            jax.ShapeDtypeStruct(whole, F32),
+            jax.ShapeDtypeStruct((2 * QUADS, 3, 4 * NB, PDEV), BF16),
+        ],
+        scratch_shapes=[pltpu.VMEM((TM,) + block, BF16)] * 2,
+        input_output_aliases={2 * TM + 2: 1} if before else {},
         compiler_params=pltpu.CompilerParams(vmem_limit_bytes=PART),
         cost_estimate=pl.CostEstimate(flops=cost, bytes_accessed=0, transcendentals=0),
         name="gram_terms",
-    )(*early, *late, volume, *before, *wait)
-
-
-def mix(first_pair, pair, total):
+    )(*early, *late, volume, *before)
+
+
+def mix(mat, is_first):
     lane, first, low = lane_masks()
-    zero = lane < zero_lanes(first_pair, pair)
-    flipped = jnp.concatenate([total] * 4, 0).T
-    cross_t = jnp.where(first, flipped[NB : 2 * NB], flipped[3 * NB :])
-    mat = jnp.where(low, total, jnp.where(zero, total, total - cross_t))
+    zero = lane < zero_lanes(is_first, 2 * NB)
     squares = mat * mat
 
     def part_sum(keep):
@@ -201,7 +249,7 @@
     norm_a = jnp.sqrt(jnp.where(zero_here, e0, e0 + e1) + 1e-06)
     norm_b = jnp.sqrt(jnp.where(zero_here, e1, e0 + e1) + 1e-06)
     norm_rest = jnp.sqrt(rest_sum + 1e-06)
-    turned = jnp.where(low, -pltpu.roll(mat, 3 * NB, 1), pltpu.roll(mat, NB, 1))
+    turned = jnp.where(low, -turn(mat, 3), turn(mat, 1))
     part_a = jnp.where(zero, jnp.where(low, mat, 0.0), mat)
     part_b = jnp.where(zero, jnp.where(low, 0.0, mat), turned)
     part_a = part_a / jnp.where(first, norm_a, norm_rest)
@@ -215,18 +263,30 @@
         ],
         0,
     )
-    return mat, mixing.astype(BF16)
-
-
-def modes_kernel(pairs, t0, t1, t2, t3, spec, *rest):
-    gram, modes, mats, mixings = rest[-4:]
+    return mixing.astype(BF16)
+
+
+def modes_kernel(t0, t1, t2, t3, spec, gram, modes, mats, mixings):
     pair = pl.program_id(0)
 
     @pl.when(pair == 0)
     def _():
-        for p in range(pairs[1] - pairs[0]):
-            total = ((t0[p] + t1[p]) + (t2[p] + t3[p])) / (NB * 3 * NPOINTS)
-            mats[p], mixings[p] = mix(pairs[0], p, total)
+        total = ((t0[...] + t1[...]) + (t2[...] + t3[...])) / (NB * 3 * NPOINTS)
+        row, column = triangle()
+        lane, _, _ = lane_masks()
+        for u in range(QUADS):
+            packed = total[u * NB : (u + 1) * NB]
+            other = transposed(packed)
+            even = jnp.where(row <= column, packed, other)
+            odd = jnp.where(row > column, packed, jnp.where(row < column, -other, 0.0))
+            if u == 0:
+                diagonal = total[QUADS * NB : QUADS * NB + 1]
+                alone = jnp.where(row < column, other, jnp.where(row > column, packed, diagonal))
+                odd = jnp.where(lane < zero_lanes(True, NB), alone, odd)
+            one = by_quarter([even, turn(odd, 1), turn(even, 1), turn(odd, 2)])
+            two = by_quarter([turn(even, 2), turn(odd, -1), turn(even, -1), odd])
+            mats[2 * u], mats[2 * u + 1] = one, two
+            mixings[2 * u], mixings[2 * u + 1] = mix(one, u == 0), mix(two, False)
 
     mat = mats[pair]
     for s in range(2):
@@ -238,31 +298,28 @@
         modes[:, :, c] = got.astype(BF16).reshape(2, 2, NB, PDEV)
 
 
-def project(pairs, totals, spec, before):
-    first, count = pairs[0], pairs[1] - pairs[0]
+def project(totals, spec):
     return pl.pallas_call(
-        functools.partial(modes_kernel, pairs),
-        grid=(count,),
-        in_specs=[pl.BlockSpec((count, NB, 4 * NB), lambda p: (0, 0, 0))] * 4
-        + [pl.BlockSpec((1, 3, 4 * NB, PDEV), lambda p: (p, 0, 0, 0))]
-        + [ANY] * len(before),
+        modes_kernel,
+        grid=(2 * QUADS,),
+        in_specs=[pl.BlockSpec(totals[0].shape, lambda p: (0, 0))] * 4
+        + [pl.BlockSpec((1, 3, 4 * NB, PDEV), lambda p: (p, 0, 0, 0))],
         out_specs=[
-            pl.BlockSpec((2, 2, NB, NB), lambda p: (p + first, 0, 0, 0)),
-            pl.BlockSpec((2, 2, 3, NB, PDEV), lambda p: (p + first, 0, 0, 0, 0)),
+            pl.BlockSpec((2, 2, NB, NB), lambda p: (p, 0, 0, 0)),
+            pl.BlockSpec((2, 2, 3, NB, PDEV), lambda p: (p, 0, 0, 0, 0)),
         ],
         out_shape=[
             jax.ShapeDtypeStruct((HERE, 2, NB, NB), F32),
             jax.ShapeDtypeStruct((HERE, 2, 3, NB, PDEV), BF16),
         ],
         scratch_shapes=[
-            pltpu.VMEM((count, NB, 4 * NB), F32),
-            pltpu.VMEM((count, 4 * NB, 4 * NB), BF16),
-        ],
-        input_output_aliases={5 + i: i for i in range(len(before))},
+            pltpu.VMEM((2 * QUADS, NB, 4 * NB), F32),
+            pltpu.VMEM((2 * QUADS, 4 * NB, 4 * NB), BF16),
+        ],
         compiler_params=pltpu.CompilerParams(vmem_limit_bytes=PART),
         cost_estimate=pl.CostEstimate(flops=0, bytes_accessed=0, transcendentals=0),
         name="modes",
-    )(*totals, spec, *before)
+    )(*totals, spec)
 
 
 def over_space(block, mask):
@@ -309,11 +366,11 @@
     blocks = [(snaps, BODY, 0), (snaps, HOP, HALF)]
     early = to_owners(transform(early_kernel, ALL, early_band, blocks, WHOLE))
     blocks = [(snaps, BODY, 1), (snaps, HOP, 0), (moved, HOP, 0), (tail, HOP, 0)]
-    late = [transform(late_kernel, part, late_band, blocks, PART) for part in PARTS]
+    late = [transform(late_kernel, (2 * a, 2 * b), late_band, blocks, PART) for a, b in PARTS]
     late = [to_owners(pieces) for pieces in late]
-    sums = gram_terms(ALL, PARTS[0], early, late[0], weights, cost=LONG)
-    terms, spec = gram_terms(ALL, PARTS[1], early, late[1], weights, sums)
-    gram, modes = project(ALL, sum_over_space(terms), spec, ())
+    sums = gram_terms(PARTS[0], early, late[0], weights, cost=LONG)
+    terms, spec = gram_terms(PARTS[1], early, late[1], weights, sums)
+    gram, modes = project(sum_over_space(terms), spec)
     return gram, jnp.transpose(modes, (0, 1, 3, 2, 4))
 
 

time: 161 us -> 155 us (0.963); the launches traced: 159 us -> 155 us
  waiting for transfers between devices: 78.3 us -> 76.4 us
    ppermute x9, waiting for transfers between devices: 14.5 us -> 11.3 us  [over_space(): return lax.ppermute(block, 'space', route)]
  transfers between devices with their start and end apart: 19 -> 19, of which waited for: 10 -> 9; matrix products, arithmetic and copies ran while one was open for 0% -> 0% of each run, Pallas kernels for 10% -> 10%
where the time goes in v4:
time: 155 us
  waiting for transfers between devices  76.4 us (49%)
  starting transfers between devices  52.2 us (34%)
  Pallas kernels  23.7 us (15%)
  local copies, waits for them, and re-layouts  1.74 us (1%)
    ppermute x9, waiting for transfers between devices, from_behind(): return lax.ppermute(block, 'tm', route)  65 us
    ppermute x9, starting transfers between devices, from_behind(): return lax.ppermute(block, 'tm', route)  34.7 us
    ppermute x9, starting transfers between devices, over_space(): return lax.ppermute(block, 'space', route)  11.8 us
    pallas_call x3, Pallas kernels, transform(): pl.pallas_call(functools.partial(kernel, pairs), grid=(3,), in_specs=[pl....  11.5 us
    ppermute x9, waiting for transfers between devices, over_space(): return lax.ppermute(block, 'space', route)  11.3 us
    pallas_call x2, Pallas kernels, gram_terms(): pl.pallas_call(functools.partial(gram_kernel, quads), grid=(count,), in_s...  6.69 us
    ppermute x1, starting transfers between devices, body(): moved = lax.ppermute(edge, ('space', 'tm'), half_block_route())  5.72 us
    pallas_call x1, Pallas kernels, project(): pl.pallas_call(modes_kernel, grid=(2 * QUADS,), in_specs=[pl.BlockSpec(to...  5.59 us
  transfers between devices with their start and end apart: 19, of which 9 were waited for; matrix products, arithmetic and copies ran while one was open for 0% of the time, Pallas kernels for 10%

profile of v4, /device:TPU:1, one launch (start us, length us, event | category | flops | bytes accessed | tf_op | source)
XLA Modules:
  0.0 154.9 jit_solution(5124293107653783018)
XLA Ops:
  0.6 1.7 %dynamic-slice_bitcast_fusion = bf16[3,64,768]{2,1,0:T(8,128)(2,1)} fusion(bf16[512,3,768]{2,0,1:T(8,128)(2,1)} %param.5, s32[]{:T(128)S(6)} %select_n.11), kind=kLoop, calls=%fused_computation | loop fusion | bytes 589828 | tf_op jit(solution)/shard_map/dynamic_slice | solution.py:364
  2.3 5.7 %collective-permute-start.3 = (bf16[3,64,768]{2,1,0:T(8,128)(2,1)}, bf16[3,64,768]{2,1,0:T(8,128)(2,1)}, u32[]{:S(2)}, u32[]{:S(2)}) collective-permute-start(bf16[3,64,768]{2,1,0:T(8,128)(2,1)} %dynamic-slice_bitcast_fusion), channel_id=1, source_target_pairs={{1,0},{2,1},{3,2},{4,5},{5,6},{6,7},{7,4},{9,8},{10,9},{11,10},{12... | collective-permute-start | bytes 884744 | tf_op jit(solution)/shard_map/ppermute | solution.py:365
  8.1 0.0 copy-start.4
  8.1 0.0 copy-start.1
  8.1 0.0 copy-start.2
  8.1 0.0 copy-start.3
  8.1 4.7 %transform.3 = (bf16[8,3,16,768]{3,2,1,0:T(8,128)(2,1)}, bf16[8,3,16,768]{3,2,1,0:T(8,128)(2,1)}, bf16[8,3,16,768]{3,2,1,0:T(8,128)(2,1)}, bf16[8,3,16,768]{3,2,1,0:T(8,128)(2,1)}) custom-call(bf16[4,128,320]{2,1,0:T(8,128)(2,1)} %constant.30.clone.band, bf16[3,512,768]{2,1,0:T(8,128)(2,1)} %bitcast.5, bf16[3,512,768]{2,1,0:T(8,128)(2,1)} %bitcast.6), custom_call_target="tpu_custom_call" | custom-call | flops 999999995904 | tf_op jit(solution)/shard_map/transform/pallas_call | solution.py:97
  12.8 4.2 %collective-permute-start = (bf16[8,3,16,768]{3,2,1,0:T(8,128)(2,1)}, bf16[8,3,16,768]{3,2,1,0:T(8,128)(2,1)}, u32[]{:S(2)}, u32[]{:S(2)}) collective-permute-start(bf16[8,3,16,768]{3,2,1,0:T(8,128)(2,1)} %get-tuple-element.21), channel_id=1, source_target_pairs={{0,1},{1,2},{2,3},{3,0},{4,5},{5,6},{6,7},{7,4},{8,9},{9,10},{10,1... | collective-permute-start | bytes 1769480 | tf_op jit(solution)/shard_map/ppermute | solution.py:343
  17.0 1.0 collective-permute-start.1
  18.0 3.5 %collective-permute-start.2 = (bf16[8,3,16,768]{3,2,1,0:T(8,128)(2,1)}, bf16[8,3,16,768]{3,2,1,0:T(8,128)(2,1)}, u32[]{:S(2)}, u32[]{:S(2)}) collective-permute-start(bf16[8,3,16,768]{3,2,1,0:T(8,128)(2,1)} %get-tuple-element.23), channel_id=1, source_target_pairs={{0,3},{1,0},{2,1},{3,2},{4,7},{5,4},{6,5},{7,6},{8,11},{9,8},{10,9... | collective-permute-start | bytes 1769480 | tf_op jit(solution)/shard_map/ppermute | solution.py:343
  21.5 0.0 copy-done.4
  21.5 0.0 collective-permute-done.3.moved
  21.5 0.0 copy-done.1
  21.5 0.0 copy-done.2
  21.5 0.0 copy-done.3
  21.5 3.7 %transform.5 = (bf16[6,3,16,768]{3,2,1,0:T(8,128)(2,1)S(1)}, bf16[6,3,16,768]{3,2,1,0:T(8,128)(2,1)}, bf16[6,3,16,768]{3,2,1,0:T(8,128)(2,1)}, bf16[6,3,16,768]{3,2,1,0:T(8,128)(2,1)}) custom-call(bf16[8,128,384]{2,1,0:T(8,128)(2,1)S(1)} %copy-done.3, bf16[3,512,768]{2,1,0:T(8,128)(2,1)S(1)} %bitcast.7, bf16[3,512,768]{2,1,0:T(8,128)(2,1)S(1)} %bitcast.8, ...), custom_call_target="tpu_custom_call" | custom-call | flops 999999995904 | tf_op jit(solution)/shard_map/transform/pallas_call | solution.py:97
  25.2 6.3 %collective-permute-start.7 = (bf16[6,3,16,768]{3,2,1,0:T(8,128)(2,1)}, bf16[6,3,16,768]{3,2,1,0:T(8,128)(2,1)}, u32[]{:S(2)}, u32[]{:S(2)}) collective-permute-start(bf16[6,3,16,768]{3,2,1,0:T(8,128)(2,1)} %get-tuple-element.29), channel_id=1, source_target_pairs={{0,1},{1,2},{2,3},{3,0},{4,5},{5,6},{6,7},{7,4},{8,9},{9,10},{10,1... | collective-permute-start | bytes 1327112 | tf_op jit(solution)/shard_map/ppermute | solution.py:343
  31.4 4.2 %collective-permute-start.8 = (bf16[6,3,16,768]{3,2,1,0:T(8,128)(2,1)}, bf16[6,3,16,768]{3,2,1,0:T(8,128)(2,1)}, u32[]{:S(2)}, u32[]{:S(2)}) collective-permute-start(bf16[6,3,16,768]{3,2,1,0:T(8,128)(2,1)} %get-tuple-element.30), channel_id=1, source_target_pairs={{0,2},{1,3},{2,0},{3,1},{4,6},{5,7},{6,4},{7,5},{8,10},{9,11},{10,... | collective-permute-start | bytes 1327112 | tf_op jit(solution)/shard_map/ppermute | solution.py:343
  35.6 11.7 %collective-permute-done.refs_1_ = bf16[8,3,16,768]{3,2,1,0:T(8,128)(2,1)} collective-permute-done((bf16[8,3,16,768]{3,2,1,0:T(8,128)(2,1)}, bf16[8,3,16,768]{3,2,1,0:T(8,128)(2,1)}, u32[]{:S(2)}, u32[]{:S(2)}) %collective-permute-start) | collective-permute-done | bytes 589856 | tf_op jit(solution)/shard_map/ppermute | solution.py:343
  47.3 0.0 collective-permute-start.9
  47.3 0.0 copy-start
  47.3 3.2 %transform.4 = (bf16[2,3,16,768]{3,2,1,0:T(8,128)(2,1)S(1)}, bf16[2,3,16,768]{3,2,1,0:T(8,128)(2,1)}, bf16[2,3,16,768]{3,2,1,0:T(8,128)(2,1)}, bf16[2,3,16,768]{3,2,1,0:T(8,128)(2,1)}) custom-call(bf16[8,128,384]{2,1,0:T(8,128)(2,1)S(1)} %copy-done.3, bf16[3,512,768]{2,1,0:T(8,128)(2,1)S(1)} %bitcast.9, bf16[3,512,768]{2,1,0:T(8,128)(2,1)S(1)} %bitcast.10, ...), custom_call_target="tpu_custom_call" | custom-call | flops 999999995904 | tf_op jit(solution)/shard_map/transform/pallas_call | solution.py:97
  50.5 23.7 %collective-permute-done.1.refs_2_ = bf16[8,3,16,768]{3,2,1,0:T(8,128)(2,1)} collective-permute-done((bf16[8,3,16,768]{3,2,1,0:T(8,128)(2,1)}, bf16[8,3,16,768]{3,2,1,0:T(8,128)(2,1)}, u32[]{:S(2)}, u32[]{:S(2)}) %collective-permute-start.1) | collective-permute-done | bytes 589856 | tf_op jit(solution)/shard_map/ppermute | solution.py:343
  74.1 10.4 %collective-permute-start.4 = (bf16[2,3,16,768]{3,2,1,0:T(8,128)(2,1)}, bf16[2,3,16,768]{3,2,1,0:T(8,128)(2,1)}, u32[]{:S(2)}, u32[]{:S(2)}) collective-permute-start(bf16[2,3,16,768]{3,2,1,0:T(8,128)(2,1)} %get-tuple-element.25), channel_id=1, source_target_pairs={{0,1},{1,2},{2,3},{3,0},{4,5},{5,6},{6,7},{7,4},{8,9},{9,10},{10,1... | collective-permute-start | bytes 442376 | tf_op jit(solution)/shard_map/ppermute | solution.py:343
  84.6 25.4 %collective-permute-done.2.refs_3_ = bf16[8,3,16,768]{3,2,1,0:T(8,128)(2,1)} collective-permute-done((bf16[8,3,16,768]{3,2,1,0:T(8,128)(2,1)}, bf16[8,3,16,768]{3,2,1,0:T(8,128)(2,1)}, u32[]{:S(2)}, u32[]{:S(2)}) %collective-permute-start.2) | collective-permute-done | bytes 589856 | tf_op jit(solution)/shard_map/ppermute | solution.py:343
  109.9 4.1 %collective-permute-start.5 = (bf16[2,3,16,768]{3,2,1,0:T(8,128)(2,1)}, bf16[2,3,16,768]{3,2,1,0:T(8,128)(2,1)}, u32[]{:S(2)}, u32[]{:S(2)}) collective-permute-start(bf16[2,3,16,768]{3,2,1,0:T(8,128)(2,1)} %get-tuple-element.26), channel_id=1, source_target_pairs={{0,2},{1,3},{2,0},{3,1},{4,6},{5,7},{6,4},{7,5},{8,10},{9,11},{10,... | collective-permute-start | bytes 442376 | tf_op jit(solution)/shard_map/ppermute | solution.py:343
  114.1 0.0 collective-permute-done.7.refs_5_
  114.1 1.0 collective-permute-start.6
  115.1 0.0 collective-permute-done.8.refs_6_
  115.1 4.3 %collective-permute-done.9.refs_7_ = bf16[6,3,16,768]{3,2,1,0:T(8,128)(2,1)} collective-permute-done((bf16[6,3,16,768]{3,2,1,0:T(8,128)(2,1)}, bf16[6,3,16,768]{3,2,1,0:T(8,128)(2,1)}, u32[]{:S(2)}, u32[]{:S(2)}) %collective-permute-start.9) | collective-permute-done | bytes 442400 | tf_op jit(solution)/shard_map/ppermute | solution.py:343
  119.4 0.0 copy-done
  119.4 4.5 %gram_terms.2 = (f32[136,128]{1,0:T(8,128)S(1)}, bf16[8,3,128,768]{3,2,1,0:T(8,128)(2,1)S(1)}) custom-call(bf16[8,3,16,768]{3,2,1,0:T(8,128)(2,1)S(1)} %copy-done, bf16[8,3,16,768]{3,2,1,0:T(8,128)(2,1)} %collective-permute-done.refs_1_, bf16[8,3,16,768]{3,2,1,0:T(8,128)(2,1)} %collective-permute-done.1.refs_2_, ...), custom_call_target="tpu_custom_call" | custom-call | flops 999999995904 | tf_op jit(solution)/shard_map/gram_terms/pallas_call | solution.py:215
  123.9 0.0 collective-permute-done.4.refs_5_
  123.9 0.0 collective-permute-done.5.refs_6_
  123.9 0.0 collective-permute-done.6.refs_7_
  123.9 2.2 %gram_terms.3 = (f32[136,128]{1,0:T(8,128)S(1)}, bf16[8,3,128,768]{3,2,1,0:T(8,128)(2,1)S(1)}) custom-call(bf16[8,3,16,768]{3,2,1,0:T(8,128)(2,1)S(1)} %copy-done, bf16[8,3,16,768]{3,2,1,0:T(8,128)(2,1)} %collective-permute-done.refs_1_, bf16[8,3,16,768]{3,2,1,0:T(8,128)(2,1)} %collective-permute-done.1.refs_2_, ...), custom_call_target="tpu_custom_call", output_to_operand_aliasing={{1}: (10, {})} | custom-call | tf_op jit(solution)/shard_map/gram_terms/pallas_call | solution.py:215
  126.2 2.6 %collective-permute-start.12 = (f32[136,128]{1,0:T(8,128)S(1)}, f32[136,128]{1,0:T(8,128)S(1)}, u32[]{:S(2)}, u32[]{:S(2)}) collective-permute-start(f32[136,128]{1,0:T(8,128)S(1)} %get-tuple-element.34), channel_id=1, source_target_pairs={{0,192},{4,196},{8,200},{12,204},{16,208},{20,212},{24,216},{28,22... | collective-permute-start | bytes 208904 | tf_op jit(solution)/shard_map/ppermute | solution.py:327
  128.7 0.5 collective-permute-start.11
  129.3 0.3 collective-permute-start.10
  129.5 1.1 collective-permute-done.12
  130.6 2.8 %collective-permute-done.11 = f32[136,128]{1,0:T(8,128)S(1)} collective-permute-done((f32[136,128]{1,0:T(8,128)S(1)}, f32[136,128]{1,0:T(8,128)S(1)}, u32[]{:S(2)}, u32[]{:S(2)}) %collective-permute-start.11) | collective-permute-done | bytes 69664 | tf_op jit(solution)/shard_map/ppermute | solution.py:327
  133.4 0.0 collective-permute-done.10
  133.4 2.8 %collective-permute-start.15 = (f32[136,128]{1,0:T(8,128)S(1)}, f32[136,128]{1,0:T(8,128)S(1)}, u32[]{:S(2)}, u32[]{:S(2)}) collective-permute-start(f32[136,128]{1,0:T(8,128)S(1)} %add_add_fusion.1), channel_id=1, source_target_pairs={{0,48},{4,52},{8,56},{12,60},{16,32},{20,36},{24,40},{28,44},{32,1... | collective-permute-start | bytes 208904 | tf_op jit(solution)/shard_map/ppermute | solution.py:327
  136.2 0.4 collective-permute-start.14
  136.6 0.3 collective-permute-start.13
  136.9 1.3 collective-permute-done.15
  138.2 2.8 %collective-permute-done.14 = f32[136,128]{1,0:T(8,128)S(1)} collective-permute-done((f32[136,128]{1,0:T(8,128)S(1)}, f32[136,128]{1,0:T(8,128)S(1)}, u32[]{:S(2)}, u32[]{:S(2)}) %collective-permute-start.14) | collective-permute-done | bytes 69664 | tf_op jit(solution)/shard_map/ppermute | solution.py:327
  141.0 0.0 collective-permute-done.13
  141.0 0.1 collective-permute-start.18
  141.1 4.8 %collective-permute-start.17 = (f32[136,128]{1,0:T(8,128)S(1)}, f32[136,128]{1,0:T(8,128)S(1)}, u32[]{:S(2)}, u32[]{:S(2)}) collective-permute-start(f32[136,128]{1,0:T(8,128)S(1)} %add_add_fusion.t0), channel_id=1, source_target_pairs={{0,8},{4,12},{8,0},{12,4},{16,24},{20,28},{24,16},{28,20},{32,40},... | collective-permute-start | bytes 208904 | tf_op jit(solution)/shard_map/ppermute | solution.py:327
  146.0 0.0 collective-permute-start.16
  146.0 0.0 collective-permute-done.18.t3
  146.0 3.4 %collective-permute-done.17.t2 = f32[136,128]{1,0:T(8,128)S(1)} collective-permute-done((f32[136,128]{1,0:T(8,128)S(1)}, f32[136,128]{1,0:T(8,128)S(1)}, u32[]{:S(2)}, u32[]{:S(2)}) %collective-permute-start.17) | collective-permute-done | bytes 69664 | tf_op jit(solution)/shard_map/ppermute | solution.py:327
  149.3 0.0 collective-permute-done.16.t1
  149.3 5.6 %modes.1 = (f32[16,2,32,32]{3,2,1,0:T(8,128)}, bf16[16,2,3,32,768]{4,3,2,1,0:T(8,128)(2,1)}) custom-call(f32[136,128]{1,0:T(8,128)S(1)} %add_add_fusion.t0, f32[136,128]{1,0:T(8,128)S(1)} %collective-permute-done.16.t1, f32[136,128]{1,0:T(8,128)S(1)} %collective-permute-done.17.t2, f32[136,128]{1,0:T(8,128)S(1)} %collective-permute-done.18.t3, ...), custom_call_target="tpu_custom_call" | custom-call | tf_op jit(solution)/shard_map/modes/pallas_call | solution.py:302
  (3 shorter events, 0.0 us)
Async XLA Ops:
  2.3 19.1 %collective-permute-start.3 = (bf16[3,64,768]{2,1,0:T(8,128)(2,1)}, bf16[3,64,768]{2,1,0:T(8,128)(2,1)}, u32[]{:S(2)}, u32[]{:S(2)}) collective-permute-start(bf16[3,64,768]{2,1,0:T(8,128)(2,1)} %dynamic-slice_bitcast_fusion), channel_id=1, source_target_pairs={{1,0},{2,1},{3,2},{4,5},{5,6},{6,7},{7,4},{9,8},{10,9},{11,10},{12... | collective-permute-start | bytes 884744 | tf_op jit(solution)/shard_map/ppermute | solution.py:365
  8.1 13.4 %copy-start.4 = (f32[768]{0:T(1024)S(1)}, f32[768]{0:T(1024)}, u32[]{:S(2)}) copy-start(f32[768]{0:T(1024)} %param.7) | copy-start | bytes 9220
  8.1 13.4 %copy-start.1 = (bf16[512,3,768]{2,0,1:T(8,128)(2,1)S(1)}, bf16[512,3,768]{2,0,1:T(8,128)(2,1)}, u32[]{:S(2)}) copy-start(bf16[512,3,768]{2,0,1:T(8,128)(2,1)} %param.5) | copy-start | bytes 7077892
  8.1 13.4 %copy-start.2 = (bf16[64,3,768]{2,0,1:T(8,128)(2,1)S(1)}, bf16[64,3,768]{2,0,1:T(8,128)(2,1)}, u32[]{:S(2)}) copy-start(bf16[64,3,768]{2,0,1:T(8,128)(2,1)} %param.6) | copy-start | bytes 884740
  8.1 13.4 %copy-start.3 = (bf16[8,128,384]{2,1,0:T(8,128)(2,1)S(1)}, bf16[8,128,384]{2,1,0:T(8,128)(2,1)}, u32[]{:S(2)}) copy-start(bf16[8,128,384]{2,1,0:T(8,128)(2,1)} %constant.31.clone.band) | copy-start | bytes 2359300
  12.8 34.5 %collective-permute-start = (bf16[8,3,16,768]{3,2,1,0:T(8,128)(2,1)}, bf16[8,3,16,768]{3,2,1,0:T(8,128)(2,1)}, u32[]{:S(2)}, u32[]{:S(2)}) collective-permute-start(bf16[8,3,16,768]{3,2,1,0:T(8,128)(2,1)} %get-tuple-element.21), channel_id=1, source_target_pairs={{0,1},{1,2},{2,3},{3,0},{4,5},{5,6},{6,7},{7,4},{8,9},{9,10},{10,1... | collective-permute-start | bytes 1769480 | tf_op jit(solution)/shard_map/ppermute | solution.py:343
  17.0 57.2 %collective-permute-start.1 = (bf16[8,3,16,768]{3,2,1,0:T(8,128)(2,1)}, bf16[8,3,16,768]{3,2,1,0:T(8,128)(2,1)}, u32[]{:S(2)}, u32[]{:S(2)}) collective-permute-start(bf16[8,3,16,768]{3,2,1,0:T(8,128)(2,1)} %get-tuple-element.22), channel_id=1, source_target_pairs={{0,2},{1,3},{2,0},{3,1},{4,6},{5,7},{6,4},{7,5},{8,10},{9,11},{10,... | collective-permute-start | bytes 1769480 | tf_op jit(solution)/shard_map/ppermute | solution.py:343
  18.0 92.0 %collective-permute-start.2 = (bf16[8,3,16,768]{3,2,1,0:T(8,128)(2,1)}, bf16[8,3,16,768]{3,2,1,0:T(8,128)(2,1)}, u32[]{:S(2)}, u32[]{:S(2)}) collective-permute-start(bf16[8,3,16,768]{3,2,1,0:T(8,128)(2,1)} %get-tuple-element.23), channel_id=1, source_target_pairs={{0,3},{1,0},{2,1},{3,2},{4,7},{5,4},{6,5},{7,6},{8,11},{9,8},{10,9... | collective-permute-start | bytes 1769480 | tf_op jit(solution)/shard_map/ppermute | solution.py:343
  25.2 88.9 %collective-permute-start.7 = (bf16[6,3,16,768]{3,2,1,0:T(8,128)(2,1)}, bf16[6,3,16,768]{3,2,1,0:T(8,128)(2,1)}, u32[]{:S(2)}, u32[]{:S(2)}) collective-permute-start(bf16[6,3,16,768]{3,2,1,0:T(8,128)(2,1)} %get-tuple-element.29), channel_id=1, source_target_pairs={{0,1},{1,2},{2,3},{3,0},{4,5},{5,6},{6,7},{7,4},{8,9},{9,10},{10,1... | collective-permute-start | bytes 1327112 | tf_op jit(solution)/shard_map/ppermute | solution.py:343
  31.4 83.7 %collective-permute-start.8 = (bf16[6,3,16,768]{3,2,1,0:T(8,128)(2,1)}, bf16[6,3,16,768]{3,2,1,0:T(8,128)(2,1)}, u32[]{:S(2)}, u32[]{:S(2)}) collective-permute-start(bf16[6,3,16,768]{3,2,1,0:T(8,128)(2,1)} %get-tuple-element.30), channel_id=1, source_target_pairs={{0,2},{1,3},{2,0},{3,1},{4,6},{5,7},{6,4},{7,5},{8,10},{9,11},{10,... | collective-permute-start | bytes 1327112 | tf_op jit(solution)/shard_map/ppermute | solution.py:343
  47.3 72.1 %collective-permute-start.9 = (bf16[6,3,16,768]{3,2,1,0:T(8,128)(2,1)}, bf16[6,3,16,768]{3,2,1,0:T(8,128)(2,1)}, u32[]{:S(2)}, u32[]{:S(2)}) collective-permute-start(bf16[6,3,16,768]{3,2,1,0:T(8,128)(2,1)} %get-tuple-element.31), channel_id=1, source_target_pairs={{0,3},{1,0},{2,1},{3,2},{4,7},{5,4},{6,5},{7,6},{8,11},{9,8},{10,9... | collective-permute-start | bytes 1327112 | tf_op jit(solution)/shard_map/ppermute | solution.py:343
  47.3 72.1 %copy-start = (bf16[8,3,16,768]{3,2,1,0:T(8,128)(2,1)S(1)}, bf16[8,3,16,768]{3,2,1,0:T(8,128)(2,1)}, u32[]{:S(2)}) copy-start(bf16[8,3,16,768]{3,2,1,0:T(8,128)(2,1)} %get-tuple-element.20.refs_0_) | copy-start | bytes 1769476
  74.1 49.8 %collective-permute-start.4 = (bf16[2,3,16,768]{3,2,1,0:T(8,128)(2,1)}, bf16[2,3,16,768]{3,2,1,0:T(8,128)(2,1)}, u32[]{:S(2)}, u32[]{:S(2)}) collective-permute-start(bf16[2,3,16,768]{3,2,1,0:T(8,128)(2,1)} %get-tuple-element.25), channel_id=1, source_target_pairs={{0,1},{1,2},{2,3},{3,0},{4,5},{5,6},{6,7},{7,4},{8,9},{9,10},{10,1... | collective-permute-start | bytes 442376 | tf_op jit(solution)/shard_map/ppermute | solution.py:343
  109.9 14.0 %collective-permute-start.5 = (bf16[2,3,16,768]{3,2,1,0:T(8,128)(2,1)}, bf16[2,3,16,768]{3,2,1,0:T(8,128)(2,1)}, u32[]{:S(2)}, u32[]{:S(2)}) collective-permute-start(bf16[2,3,16,768]{3,2,1,0:T(8,128)(2,1)} %get-tuple-element.26), channel_id=1, source_target_pairs={{0,2},{1,3},{2,0},{3,1},{4,6},{5,7},{6,4},{7,5},{8,10},{9,11},{10,... | collective-permute-start | bytes 442376 | tf_op jit(solution)/shard_map/ppermute | solution.py:343
  114.1 9.9 %collective-permute-start.6 = (bf16[2,3,16,768]{3,2,1,0:T(8,128)(2,1)}, bf16[2,3,16,768]{3,2,1,0:T(8,128)(2,1)}, u32[]{:S(2)}, u32[]{:S(2)}) collective-permute-start(bf16[2,3,16,768]{3,2,1,0:T(8,128)(2,1)} %get-tuple-element.27), channel_id=1, source_target_pairs={{0,3},{1,0},{2,1},{3,2},{4,7},{5,4},{6,5},{7,6},{8,11},{9,8},{10,9... | collective-permute-start | bytes 442376 | tf_op jit(solution)/shard_map/ppermute | solution.py:343
  126.2 4.5 %collective-permute-start.12 = (f32[136,128]{1,0:T(8,128)S(1)}, f32[136,128]{1,0:T(8,128)S(1)}, u32[]{:S(2)}, u32[]{:S(2)}) collective-permute-start(f32[136,128]{1,0:T(8,128)S(1)} %get-tuple-element.34), channel_id=1, source_target_pairs={{0,192},{4,196},{8,200},{12,204},{16,208},{20,212},{24,216},{28,22... | collective-permute-start | bytes 208904 | tf_op jit(solution)/shard_map/ppermute | solution.py:327
  128.7 4.7 %collective-permute-start.11 = (f32[136,128]{1,0:T(8,128)S(1)}, f32[136,128]{1,0:T(8,128)S(1)}, u32[]{:S(2)}, u32[]{:S(2)}) collective-permute-start(f32[136,128]{1,0:T(8,128)S(1)} %get-tuple-element.34), channel_id=1, source_target_pairs={{0,128},{4,132},{8,136},{12,140},{16,144},{20,148},{24,152},{28,15... | collective-permute-start | bytes 208904 | tf_op jit(solution)/shard_map/ppermute | solution.py:327
  129.3 4.1 %collective-permute-start.10 = (f32[136,128]{1,0:T(8,128)S(1)}, f32[136,128]{1,0:T(8,128)S(1)}, u32[]{:S(2)}, u32[]{:S(2)}) collective-permute-start(f32[136,128]{1,0:T(8,128)S(1)} %get-tuple-element.34), channel_id=1, source_target_pairs={{0,64},{4,68},{8,72},{12,76},{16,80},{20,84},{24,88},{28,92},{32,9... | collective-permute-start | bytes 208904 | tf_op jit(solution)/shard_map/ppermute | solution.py:327
  133.4 4.8 %collective-permute-start.15 = (f32[136,128]{1,0:T(8,128)S(1)}, f32[136,128]{1,0:T(8,128)S(1)}, u32[]{:S(2)}, u32[]{:S(2)}) collective-permute-start(f32[136,128]{1,0:T(8,128)S(1)} %add_add_fusion.1), channel_id=1, source_target_pairs={{0,48},{4,52},{8,56},{12,60},{16,32},{20,36},{24,40},{28,44},{32,1... | collective-permute-start | bytes 208904 | tf_op jit(solution)/shard_map/ppermute | solution.py:327
  136.2 4.8 %collective-permute-start.14 = (f32[136,128]{1,0:T(8,128)S(1)}, f32[136,128]{1,0:T(8,128)S(1)}, u32[]{:S(2)}, u32[]{:S(2)}) collective-permute-start(f32[136,128]{1,0:T(8,128)S(1)} %add_add_fusion.1), channel_id=1, source_target_pairs={{0,32},{4,36},{8,40},{12,44},{16,48},{20,52},{24,56},{28,60},{32,0... | collective-permute-start | bytes 208904 | tf_op jit(solution)/shard_map/ppermute | solution.py:327
  136.6 4.4 %collective-permute-start.13 = (f32[136,128]{1,0:T(8,128)S(1)}, f32[136,128]{1,0:T(8,128)S(1)}, u32[]{:S(2)}, u32[]{:S(2)}) collective-permute-start(f32[136,128]{1,0:T(8,128)S(1)} %add_add_fusion.1), channel_id=1, source_target_pairs={{0,16},{4,20},{8,24},{12,28},{16,0},{20,4},{24,8},{28,12},{32,48},... | collective-permute-start | bytes 208904 | tf_op jit(solution)/shard_map/ppermute | solution.py:327
  141.0 4.9 %collective-permute-start.18 = (f32[136,128]{1,0:T(8,128)S(1)}, f32[136,128]{1,0:T(8,128)S(1)}, u32[]{:S(2)}, u32[]{:S(2)}) collective-permute-start(f32[136,128]{1,0:T(8,128)S(1)} %add_add_fusion.t0), channel_id=1, source_target_pairs={{0,12},{4,8},{8,4},{12,0},{16,28},{20,24},{24,20},{28,16},{32,44},... | collective-permute-start | bytes 208904 | tf_op jit(solution)/shard_map/ppermute | solution.py:327
  141.1 8.2 %collective-permute-start.17 = (f32[136,128]{1,0:T(8,128)S(1)}, f32[136,128]{1,0:T(8,128)S(1)}, u32[]{:S(2)}, u32[]{:S(2)}) collective-permute-start(f32[136,128]{1,0:T(8,128)S(1)} %add_add_fusion.t0), channel_id=1, source_target_pairs={{0,8},{4,12},{8,0},{12,4},{16,24},{20,28},{24,16},{28,20},{32,40},... | collective-permute-start | bytes 208904 | tf_op jit(solution)/shard_map/ppermute | solution.py:327
  146.0 3.4 %collective-permute-start.16 = (f32[136,128]{1,0:T(8,128)S(1)}, f32[136,128]{1,0:T(8,128)S(1)}, u32[]{:S(2)}, u32[]{:S(2)}) collective-permute-start(f32[136,128]{1,0:T(8,128)S(1)} %add_add_fusion.t0), channel_id=1, source_target_pairs={{0,4},{4,0},{8,12},{12,8},{16,20},{20,16},{24,28},{28,24},{32,36},... | collective-permute-start | bytes 208904 | tf_op jit(solution)/shard_map/ppermute | solution.py:327

commit v5 on v4

v5 whole, which is shorter than its diff:
```python
import functools

import jax
import jax.numpy as jnp
import ml_dtypes
import numpy as np
from jax import lax
from jax.experimental import pallas as pl
from jax.experimental.pallas import tpu as pltpu
from jax.sharding import PartitionSpec as P

NB = 32
NFFT = 128
HOP = 64
SLOTS = 64
PDEV = 768
NPOINTS = 49152
TM = 4
OWN = NB // TM
HALF = OWN // 2
HERE = SLOTS // TM
BODY = HALF * HOP
ALL = (0, HERE // 2)
PAIRS, QUADS = HERE // 2, HERE // 4
LANES = 256
LONG = 10**12
F32, BF16 = jnp.float32, jnp.bfloat16
HELD = pl.BlockSpec(memory_space=pltpu.VMEM)
WHOLE, PART = 60 << 20, 16 << 20


def transform_table():
    f32 = np.float32
    times = np.arange(NFFT, dtype=f32)
    freq = np.arange(SLOTS, dtype=f32)[:, None]
    window = f32(0.5) - f32(0.5) * np.cos(f32(2.0 * np.pi) * times / f32(NFFT))
    window = window / np.sqrt(np.sum(window * window))
    angles = f32(2.0 * np.pi) * freq * times[None, :] / f32(NFFT)
    real_rows = window * np.cos(angles)
    imag_rows = -window * np.sin(angles)
    nyquist = window * np.cos(f32(np.pi) * times)
    imag_rows = np.where(freq == 0, nyquist[None, :], imag_rows)
    return np.stack([real_rows, imag_rows], axis=1).astype(ml_dtypes.bfloat16)


def banded_tables():
    table = transform_table()

    def band(starts, span):
        rows = np.zeros((SLOTS, 2, HALF, span), ml_dtypes.bfloat16)
        for b, start in enumerate(starts):
            rows[:, :, b, start : start + NFFT] = table
        return rows.reshape(TM, HERE * 2 * HALF, span)

    starts = [b * HOP for b in range(HALF)]
    late = [band(starts, BODY + 2 * HOP), band(starts[:-1] + [BODY], BODY + 2 * HOP)]
    return band(starts, BODY + HOP), np.concatenate(late, 0)


def orders():
    arrived = np.arange(4 * NB)
    piece, s, ri, b = arrived // 16, arrived // 8 % 2, arrived // 4 % 2, arrived % 4
    late, distance = piece // TM, piece % TM
    out = np.zeros((2 * TM, 4 * NB, 4 * NB), ml_dtypes.bfloat16)
    for rank in range(TM):
        for which in range(2):
            moved = which * late * (b == HALF - 1)
            source = (rank - distance - moved) % TM
            natural = s * 64 + ri * NB + source * OWN + late * HALF + b
            out[2 * rank + which, natural, arrived] = 1
    return out


def core():
    return lax.axis_index("space") % 2


def pick(flag, yes, no):
    chosen = jnp.full(yes.shape, flag.astype(jnp.int32), jnp.int32) > 0
    return jnp.where(chosen, yes.astype(F32), no.astype(F32)).astype(BF16)


def apply_band(pairs, band, base, main, after, outs):
    rank = lax.axis_index("tm")
    first, stop = (4 * HALF * p for p in pairs)
    rows = jnp.concatenate([band[base + (rank + k) % TM, first:stop] for k in range(TM)], 0)
    got = jnp.dot(rows[:, :BODY], main, preferred_element_type=F32)
    got += jnp.dot(rows[:, BODY:], after, preferred_element_type=F32)
    got = got.astype(BF16).reshape(TM, pairs[1] - pairs[0], 4 * HALF, PDEV)
    for k, out in enumerate(outs):
        out[:, pl.program_id(0)] = got[k]


def early_kernel(pairs, band, main, after, *outs):
    apply_band(pairs, band, 0, main[0], after[0], outs)


def late_kernel(pairs, band, main, head, moved, tail, *outs):
    rank = lax.axis_index("tm")
    half = pick((rank == TM - 1) & (core() == 0), tail[0], moved[0])
    start = pick((rank == 0) & (core() == 1), tail[0], head[0])
    apply_band(pairs, band, TM * core(), main[0], jnp.concatenate([half, start], 0), outs)


def transform(kernel, pairs, band, blocks, limit):
    count = pairs[1] - pairs[0]

    def block(span, at):
        return pl.BlockSpec((1, span, PDEV), lambda c: (c, at, 0))

    return pl.pallas_call(
        functools.partial(kernel, pairs),
        grid=(3,),
        in_specs=[pl.BlockSpec(band.shape, lambda c: (0, 0, 0))]
        + [block(span, at) for _, span, at in blocks],
        out_specs=[HELD] * TM,
        out_shape=[jax.ShapeDtypeStruct((count, 3, 4 * HALF, PDEV), BF16)] * TM,
        compiler_params=pltpu.CompilerParams(vmem_limit_bytes=limit),
        cost_estimate=pl.CostEstimate(flops=LONG, bytes_accessed=0, transcendentals=0),
        name="transform",
    )(band, *(array for array, _, _ in blocks))


def zero_lanes(is_first, lanes):
    return jnp.where((lax.axis_index("tm") == 0) & is_first, lanes, 0)


def lane_masks():
    lane = lax.broadcasted_iota(jnp.int32, (NB, 4 * NB), 1)
    return lane, lane < 2 * NB, (lane % (2 * NB)) < NB


def triangle():
    row = lax.broadcasted_iota(jnp.int32, (NB, 4 * NB), 0)
    return row, lax.broadcasted_iota(jnp.int32, (NB, 4 * NB), 1) % NB


def by_quarter(parts):
    lane, _, _ = lane_masks()
    out = parts[3]
    for at in (2, 1, 0):
        out = jnp.where(lane < (at + 1) * NB, parts[at], out)
    return out


def turn(x, quarters):
    return pltpu.roll(x, (quarters % 4) * NB, 1) if quarters % 4 else x


def transposed(four):
    flipped = jnp.concatenate([four] * 4, 0).T
    return by_quarter([flipped[g * NB : (g + 1) * NB] for g in range(4)])


def rows_of(pieces, pair, c, lanes=slice(None)):
    return [p[pair, c, :, lanes] for p in pieces]


def in_three(x):
    high = x.astype(BF16)
    rest = x - high.astype(F32)
    middle = rest.astype(BF16)
    return [high, middle, (rest - middle.astype(F32)).astype(BF16)]


def reorder(x, order):
    n = x.shape[0]
    got = lax.dot_general(
        jnp.concatenate(in_three(x), 0),
        order,
        (((1,), (1,)), ((), ())),
        preferred_element_type=F32,
    )
    x = (got[:n] + got[n : 2 * n]) + got[2 * n :]
    x = jnp.concatenate([x[at : at + 4 * NB] for at in range(0, n, 4 * NB)], 1)
    got = jnp.dot(order, jnp.concatenate(in_three(x), 1), preferred_element_type=F32)
    return (got[:, :n] + got[:, n : 2 * n]) + got[:, 2 * n :]


def pair_terms(total, is_zero):
    lane, first, low = lane_masks()
    top = jnp.where(first, total[:NB], total[2 * NB : 3 * NB])
    bottom = jnp.where(first, total[NB : 2 * NB], total[3 * NB :])
    summed = top + jnp.where(low, turn(bottom, 3), 0.0)
    if not is_zero:
        return summed
    apart = jnp.where(lane < NB, top, bottom)
    return jnp.where(lane < zero_lanes(True, 2 * NB), apart, summed)


def gram_kernel(*refs):
    pieces, (volume, orders, terms, sums) = refs[: 2 * TM], refs[2 * TM :]
    quad, n = pl.program_id(0), 4 * NB
    total = jnp.zeros((2 * n, 2 * n), F32)
    for c in range(3):
        for start in range(0, PDEV, LANES):
            lanes = slice(start, start + LANES)
            weights = volume[:, lanes]
            rows = rows_of(pieces, 2 * quad, c, lanes) + rows_of(pieces, 2 * quad + 1, c, lanes)
            weighted = [(r.astype(F32) * weights).astype(BF16) for r in rows]
            total += lax.dot_general(
                jnp.concatenate(weighted, 0),
                jnp.concatenate(rows, 0),
                (((1,), (1,)), ((), ())),
                preferred_element_type=F32,
            )
    sums[2 * quad] = total[:n, :n]
    sums[2 * quad + 1] = total[n:, n:]

    @pl.when(quad == QUADS - 1)
    def _():
        order = orders[2 * lax.axis_index("tm") + core()]
        every = reorder(sums[...].reshape(PAIRS * n, n), order)
        lane, _, _ = lane_masks()
        row, column = triangle()
        for u in range(QUADS):
            one, two = (
                pair_terms(every[:, p * n : (p + 1) * n], p == 0) for p in (2 * u, 2 * u + 1)
            )
            plus = by_quarter([one, turn(one, -1), turn(two, 2), turn(two, 1)])
            cross = by_quarter([turn(one, -1), turn(one, -2), turn(two, 1), two])
            below = cross - transposed(cross)
            if u == 0:
                below = jnp.where(lane < zero_lanes(True, NB), cross, below)
                diagonal = jnp.sum(jnp.where(row == column, cross, 0.0), 0, keepdims=True)
                terms[QUADS * NB :] = jnp.broadcast_to(diagonal, (8, 4 * NB))
            terms[u * NB : (u + 1) * NB] = jnp.where(row <= column, plus, below)


def gram_terms(pieces, volume, order):
    return pl.pallas_call(
        gram_kernel,
        grid=(QUADS,),
        in_specs=[HELD] * (2 * TM + 2),
        out_specs=HELD,
        out_shape=jax.ShapeDtypeStruct((QUADS * NB + 8, 4 * NB), F32),
        scratch_shapes=[pltpu.VMEM((PAIRS, 4 * NB, 4 * NB), F32)],
        compiler_params=pltpu.CompilerParams(vmem_limit_bytes=PART),
        cost_estimate=pl.CostEstimate(flops=0, bytes_accessed=0, transcendentals=0),
        name="gram_terms",
    )(*pieces, volume, order)


def mix(mat, is_first):
    lane, first, low = lane_masks()
    zero = lane < (zero_lanes(True, 2 * NB) if is_first else 0)
    squares = mat * mat

    def part_sum(keep):
        return jnp.sum(jnp.where(keep, squares, 0.0), keepdims=True)

    e0, e1 = part_sum(lane < NB), part_sum(first & ~low)
    rest_sum = part_sum(~first)
    zero_here = zero[:1, :1]
    norm_a = jnp.sqrt(jnp.where(zero_here, e0, e0 + e1) + 1e-06)
    norm_b = jnp.sqrt(jnp.where(zero_here, e1, e0 + e1) + 1e-06)
    norm_rest = jnp.sqrt(rest_sum + 1e-06)
    turned = jnp.where(low, -turn(mat, 3), turn(mat, 1))
    part_a = jnp.where(zero, jnp.where(low, mat, 0.0), mat)
    part_b = jnp.where(zero, jnp.where(low, 0.0, mat), turned)
    part_a = part_a / jnp.where(first, norm_a, norm_rest)
    part_b = part_b / jnp.where(first, norm_b, norm_rest)
    mixing = jnp.concatenate(
        [
            jnp.where(first, part_a, 0.0),
            jnp.where(first, part_b, 0.0),
            jnp.where(first, 0.0, part_a),
            jnp.where(first, 0.0, part_b),
        ],
        0,
    )
    return mixing.astype(BF16)


def modes_kernel(t0, t1, t2, t3, orders, *refs):
    pieces = refs[: 2 * TM]
    gram_out, modes_out, gram, modes, sems = refs[2 * TM :]
    order = orders[2 * lax.axis_index("tm") + core()]
    total = ((t0[...] + t1[...]) + (t2[...] + t3[...])) / (NB * 3 * NPOINTS)
    row, column = triangle()
    lane, _, _ = lane_masks()
    copies = []
    for u in range(QUADS):
        packed = total[u * NB : (u + 1) * NB]
        other = transposed(packed)
        even = jnp.where(row <= column, packed, other)
        odd = jnp.where(row > column, packed, jnp.where(row < column, -other, 0.0))
        if u == 0:
            diagonal = total[QUADS * NB : QUADS * NB + 1]
            alone = jnp.where(row < column, other, jnp.where(row > column, packed, diagonal))
            odd = jnp.where(lane < zero_lanes(True, NB), alone, odd)
        one = by_quarter([even, turn(odd, 1), turn(even, 1), turn(odd, 2)])
        two = by_quarter([turn(even, 2), turn(odd, -1), turn(even, -1), odd])
        for pair, mat in ((2 * u, one), (2 * u + 1, two)):
            for s in range(2):
                for part in range(2):
                    at = (2 * s + part) * NB
                    gram[2 * pair + s, part] = mat[:, at : at + NB]
            mixing = mix(mat, True if pair == 0 else False)
            mixing = jnp.dot(mixing, order, preferred_element_type=F32).astype(BF16)
            slots = pl.ds(2 * pair, 2)
            for c in range(3):
                rows = jnp.concatenate(rows_of(pieces, pair, c), 0)
                got = jnp.dot(mixing, rows, preferred_element_type=F32)
                modes[slots, :, c] = got.astype(BF16).reshape(2, 2, NB, PDEV)
            copies.append(pltpu.make_async_copy(modes.at[slots], modes_out.at[slots], sems.at[pair]))
            copies[-1].start()
    copies.append(pltpu.make_async_copy(gram, gram_out, sems.at[PAIRS]))
    copies[-1].start()
    for copy in copies:
        copy.wait()


def project(totals, order, pieces):
    gram = jax.ShapeDtypeStruct((HERE, 2, NB, NB), F32)
    modes = jax.ShapeDtypeStruct((HERE, 2, 3, NB, PDEV), BF16)
    return pl.pallas_call(
        modes_kernel,
        in_specs=[HELD] * (5 + 2 * TM),
        out_specs=[pl.BlockSpec(memory_space=pl.ANY)] * 2,
        out_shape=[gram, modes],
        scratch_shapes=[
            pltpu.VMEM(gram.shape, F32),
            pltpu.VMEM(modes.shape, BF16),
            pltpu.SemaphoreType.DMA((PAIRS + 1,)),
        ],
        compiler_params=pltpu.CompilerParams(vmem_limit_bytes=PART),
        cost_estimate=pl.CostEstimate(flops=0, bytes_accessed=0, transcendentals=0),
        name="modes",
    )(*totals, order, *pieces)


def over_space(block, mask):
    route = [(i, i ^ mask) for i in range(lax.axis_size("space"))]
    return lax.ppermute(block, "space", route)


def half_block_route():
    route = []
    for s in range(lax.axis_size("space")):
        for t in range(TM):
            if s % 2 == 1:
                route.append((s * TM + t, s * TM + (t + 1) % TM))
            elif t:
                route.append((s * TM + t, s * TM + t - 1))
    return route


def from_behind(block, distance):
    route = [(i, (i + distance) % TM) for i in range(TM)]
    return lax.ppermute(block, "tm", route)


def to_owners(pieces):
    far = from_behind(pieces[2], 2)
    return [pieces[0], from_behind(pieces[1], 1), far, from_behind(pieces[3], 3)]


def sum_over_space(terms):
    for shift in (4, 2, 0):
        got = [terms] + [over_space(terms, m << shift) for m in (1, 2, 3)]
        if shift:
            terms = (got[0] + got[1]) + (got[2] + got[3])
    return got


def body(snapshots, tail, volume):
    snaps = jnp.transpose(snapshots, (1, 0, 2))
    tail = jnp.transpose(tail, (1, 0, 2))
    weights = volume.reshape(1, PDEV)
    early_band, late_band = (jnp.asarray(b) for b in banded_tables())
    edge = lax.dynamic_slice_in_dim(snaps, core() * (OWN - 1) * HOP, HOP, 1)
    moved = lax.ppermute(edge, ("space", "tm"), half_block_route())
    blocks = [(snaps, BODY, 0), (snaps, HOP, HALF)]
    early = to_owners(transform(early_kernel, ALL, early_band, blocks, WHOLE))
    blocks = [(snaps, BODY, 1), (snaps, HOP, 0), (moved, HOP, 0), (tail, HOP, 0)]
    late = to_owners(transform(late_kernel, ALL, late_band, blocks, PART))
    pieces = early + late
    order = jnp.asarray(orders())
    terms = gram_terms(pieces, weights, order)
    gram, modes = project(sum_over_space(terms), order, pieces)
    return gram, jnp.transpose(modes, (0, 1, 3, 2, 4))


def solution(mesh):
    placed = (P("tm", None, "space"), P(None, None, "space"), P("space"))
    return jax.shard_map(
        body,
        mesh=mesh,
        in_specs=placed,
        out_specs=(P("tm", None, None, None), P("tm", None, None, None, "space")),
        check_vma=False,
    )
```

time: 155 us -> 156 us (level)
  waiting for transfers between devices: 76.4 us -> 98.7 us
  starting transfers between devices: 52.2 us -> 36.7 us
  Pallas kernels: 23.7 us -> 18 us
    ppermute x9 -> x6, waiting for transfers between devices: 65 us -> 87.3 us  [from_behind(): return lax.ppermute(block, 'tm', route)]
    ppermute x9 -> x6, starting transfers between devices: 34.7 us -> 19.2 us  [from_behind(): return lax.ppermute(block, 'tm', route)]
    pallas_call x3 -> x2, Pallas kernels: 11.5 us -> 7.81 us  [transform(): pl.pallas_call(functools.partial(kernel, pairs), grid=(3,), in_specs=[pl....]
    pallas_call x3 -> x2, Pallas kernels: 12.3 us -> 10.2 us  [the longest x1 5.43 us: project(): pl.pallas_call(modes_kernel, in_specs=[HELD] * (5 + 2 * TM), out_specs=[p...]
  transfers between devices with their start and end apart: 19 -> 16, of which waited for: 9 -> 10; matrix products, arithmetic and copies ran while one was open for 0% -> 0% of each run, Pallas kernels for 10% -> 5%
where the time goes in v5:
time: 156 us
  waiting for transfers between devices  98.7 us (63%)
  starting transfers between devices  36.7 us (24%)
  Pallas kernels  18 us (12%)
  local copies, waits for them, and re-layouts  1.75 us (1%)
    ppermute x6, waiting for transfers between devices, from_behind(): return lax.ppermute(block, 'tm', route)  87.3 us
    ppermute x6, starting transfers between devices, from_behind(): return lax.ppermute(block, 'tm', route)  19.2 us
    ppermute x9, starting transfers between devices, over_space(): return lax.ppermute(block, 'space', route)  11.8 us
    ppermute x9, waiting for transfers between devices, over_space(): return lax.ppermute(block, 'space', route)  11.3 us
    pallas_call x2, Pallas kernels, transform(): pl.pallas_call(functools.partial(kernel, pairs), grid=(3,), in_specs=[pl....  7.81 us
    ppermute x1, starting transfers between devices, body(): moved = lax.ppermute(edge, ('space', 'tm'), half_block_route())  5.72 us
    pallas_call x1, Pallas kernels, project(): pl.pallas_call(modes_kernel, in_specs=[HELD] * (5 + 2 * TM), out_specs=[p...  5.43 us
    pallas_call x1, Pallas kernels, gram_terms(): pl.pallas_call(gram_kernel, grid=(QUADS,), in_specs=[HELD] * (2 * TM + 2)...  4.79 us
  transfers between devices with their start and end apart: 16, of which 10 were waited for; matrix products, arithmetic and copies ran while one was open for 0% of the time, Pallas kernels for 5%

profile of v5, /device:TPU:1, one launch (start us, length us, event | category | flops | bytes accessed | tf_op | source)
XLA Modules:
  0.0 155.9 jit_solution(14057650548340393243)
XLA Ops:
  0.6 1.7 %dynamic-slice_bitcast_fusion = bf16[3,64,768]{2,1,0:T(8,128)(2,1)} fusion(bf16[512,3,768]{2,0,1:T(8,128)(2,1)} %param.6, s32[]{:T(128)S(6)} %select_n.11), kind=kLoop, calls=%fused_computation | loop fusion | bytes 589828 | tf_op jit(solution)/shard_map/dynamic_slice | solution.py:372
  2.3 5.7 %collective-permute-start.3 = (bf16[3,64,768]{2,1,0:T(8,128)(2,1)}, bf16[3,64,768]{2,1,0:T(8,128)(2,1)}, u32[]{:S(2)}, u32[]{:S(2)}) collective-permute-start(bf16[3,64,768]{2,1,0:T(8,128)(2,1)} %dynamic-slice_bitcast_fusion), channel_id=1, source_target_pairs={{1,0},{2,1},{3,2},{4,5},{5,6},{6,7},{7,4},{9,8},{10,9},{11,10},{12... | collective-permute-start | bytes 884744 | tf_op jit(solution)/shard_map/ppermute | solution.py:373
  8.1 0.0 copy-start.2
  8.1 0.0 copy-start.3
  8.1 0.0 copy-start.4
  8.1 4.8 %transform.2 = (bf16[8,3,16,768]{3,2,1,0:T(8,128)(2,1)}, bf16[8,3,16,768]{3,2,1,0:T(8,128)(2,1)}, bf16[8,3,16,768]{3,2,1,0:T(8,128)(2,1)}, bf16[8,3,16,768]{3,2,1,0:T(8,128)(2,1)}) custom-call(bf16[4,128,320]{2,1,0:T(8,128)(2,1)} %constant.32.clone.band, bf16[3,512,768]{2,1,0:T(8,128)(2,1)} %bitcast.5, bf16[3,512,768]{2,1,0:T(8,128)(2,1)} %bitcast.6), custom_call_target="tpu_custom_call" | custom-call | flops 999999995904 | tf_op jit(solution)/shard_map/transform/pallas_call | solution.py:111
  12.9 4.2 %collective-permute-start = (bf16[8,3,16,768]{3,2,1,0:T(8,128)(2,1)}, bf16[8,3,16,768]{3,2,1,0:T(8,128)(2,1)}, u32[]{:S(2)}, u32[]{:S(2)}) collective-permute-start(bf16[8,3,16,768]{3,2,1,0:T(8,128)(2,1)} %get-tuple-element.13), channel_id=1, source_target_pairs={{0,1},{1,2},{2,3},{3,0},{4,5},{5,6},{6,7},{7,4},{8,9},{9,10},{10,1... | collective-permute-start | bytes 1769480 | tf_op jit(solution)/shard_map/ppermute | solution.py:351
  17.1 0.9 collective-permute-start.1
  18.0 3.6 %collective-permute-start.2 = (bf16[8,3,16,768]{3,2,1,0:T(8,128)(2,1)}, bf16[8,3,16,768]{3,2,1,0:T(8,128)(2,1)}, u32[]{:S(2)}, u32[]{:S(2)}) collective-permute-start(bf16[8,3,16,768]{3,2,1,0:T(8,128)(2,1)} %get-tuple-element.15), channel_id=1, source_target_pairs={{0,3},{1,0},{2,1},{3,2},{4,7},{5,4},{6,5},{7,6},{8,11},{9,8},{10,9... | collective-permute-start | bytes 1769480 | tf_op jit(solution)/shard_map/ppermute | solution.py:351
  21.6 0.0 collective-permute-done.3.moved
  21.6 0.0 copy-done.2
  21.6 0.0 copy-done.3
  21.6 0.0 copy-done.4
  21.6 0.0 copy-start.5
  21.6 0.0 copy-start
  21.6 0.0 copy-start.1
  21.6 3.1 %transform.3 = (bf16[8,3,16,768]{3,2,1,0:T(8,128)(2,1)S(1)}, bf16[8,3,16,768]{3,2,1,0:T(8,128)(2,1)S(1)}, bf16[8,3,16,768]{3,2,1,0:T(8,128)(2,1)S(1)}, bf16[8,3,16,768]{3,2,1,0:T(8,128)(2,1)S(1)}) custom-call(bf16[8,128,384]{2,1,0:T(8,128)(2,1)S(1)} %copy-done.4, bf16[3,512,768]{2,1,0:T(8,128)(2,1)S(1)} %bitcast.7, bf16[3,512,768]{2,1,0:T(8,128)(2,1)S(1)} %bitcast.8, ...), custom_call_target="tpu_custom_call" | custom-call | flops 999999995904 | tf_op jit(solution)/shard_map/transform/pallas_call | solution.py:111
  24.7 6.2 %collective-permute-start.4 = (bf16[8,3,16,768]{3,2,1,0:T(8,128)(2,1)S(1)}, bf16[8,3,16,768]{3,2,1,0:T(8,128)(2,1)S(1)}, u32[]{:S(2)}, u32[]{:S(2)}) collective-permute-start(bf16[8,3,16,768]{3,2,1,0:T(8,128)(2,1)S(1)} %get-tuple-element.17), channel_id=1, source_target_pairs={{0,1},{1,2},{2,3},{3,0},{4,5},{5,6},{6,7},{7,4},{8,9},{9,10},{10,1... | collective-permute-start | bytes 1769480 | tf_op jit(solution)/shard_map/ppermute | solution.py:351
  30.9 4.3 %collective-permute-start.5 = (bf16[8,3,16,768]{3,2,1,0:T(8,128)(2,1)S(1)}, bf16[8,3,16,768]{3,2,1,0:T(8,128)(2,1)S(1)}, u32[]{:S(2)}, u32[]{:S(2)}) collective-permute-start(bf16[8,3,16,768]{3,2,1,0:T(8,128)(2,1)S(1)} %get-tuple-element.18), channel_id=1, source_target_pairs={{0,2},{1,3},{2,0},{3,1},{4,6},{5,7},{6,4},{7,5},{8,10},{9,11},{10,... | collective-permute-start | bytes 1769480 | tf_op jit(solution)/shard_map/ppermute | solution.py:351
  35.2 11.8 %collective-permute-done.refs_1_ = bf16[8,3,16,768]{3,2,1,0:T(8,128)(2,1)} collective-permute-done((bf16[8,3,16,768]{3,2,1,0:T(8,128)(2,1)}, bf16[8,3,16,768]{3,2,1,0:T(8,128)(2,1)}, u32[]{:S(2)}, u32[]{:S(2)}) %collective-permute-start) | collective-permute-done | bytes 589856 | tf_op jit(solution)/shard_map/ppermute | solution.py:351
  47.0 0.0 collective-permute-start.6
  47.0 0.0 copy-done.5
  47.0 26.8 %collective-permute-done.1.refs_2_ = bf16[8,3,16,768]{3,2,1,0:T(8,128)(2,1)} collective-permute-done((bf16[8,3,16,768]{3,2,1,0:T(8,128)(2,1)}, bf16[8,3,16,768]{3,2,1,0:T(8,128)(2,1)}, u32[]{:S(2)}, u32[]{:S(2)}) %collective-permute-start.1) | collective-permute-done | bytes 589856 | tf_op jit(solution)/shard_map/ppermute | solution.py:351
  73.8 36.2 %collective-permute-done.2.refs_3_ = bf16[8,3,16,768]{3,2,1,0:T(8,128)(2,1)} collective-permute-done((bf16[8,3,16,768]{3,2,1,0:T(8,128)(2,1)}, bf16[8,3,16,768]{3,2,1,0:T(8,128)(2,1)}, u32[]{:S(2)}, u32[]{:S(2)}) %collective-permute-start.2) | collective-permute-done | bytes 589856 | tf_op jit(solution)/shard_map/ppermute | solution.py:351
  110.0 0.0 collective-permute-done.4.refs_5_
  110.0 0.4 collective-permute-done.5.refs_6_
  110.4 12.1 %collective-permute-done.6.refs_7_ = bf16[8,3,16,768]{3,2,1,0:T(8,128)(2,1)S(1)} collective-permute-done((bf16[8,3,16,768]{3,2,1,0:T(8,128)(2,1)S(1)}, bf16[8,3,16,768]{3,2,1,0:T(8,128)(2,1)S(1)}, u32[]{:S(2)}, u32[]{:S(2)}) %collective-permute-start.6) | collective-permute-done | bytes 589856 | tf_op jit(solution)/shard_map/ppermute | solution.py:351
  122.5 0.0 copy-done
  122.5 0.0 copy-done.1
  122.5 4.8 %gram_terms.1 = f32[136,128]{1,0:T(8,128)S(1)} custom-call(bf16[8,3,16,768]{3,2,1,0:T(8,128)(2,1)S(1)} %copy-done, bf16[8,3,16,768]{3,2,1,0:T(8,128)(2,1)} %collective-permute-done.refs_1_, bf16[8,3,16,768]{3,2,1,0:T(8,128)(2,1)} %collective-permute-done.1.refs_2_, bf16[8,3,16,768]{3,2,1,0:T(8,128)(2,1)} %collective-permute-done.2.refs_3_, ...), custom_call_target="tpu_custom_call" | custom-call | tf_op jit(solution)/shard_map/gram_terms/pallas_call | solution.py:231
  127.3 2.6 %collective-permute-start.9 = (f32[136,128]{1,0:T(8,128)S(1)}, f32[136,128]{1,0:T(8,128)S(1)}, u32[]{:S(2)}, u32[]{:S(2)}) collective-permute-start(f32[136,128]{1,0:T(8,128)S(1)} %gram_terms.1), channel_id=1, source_target_pairs={{0,192},{4,196},{8,200},{12,204},{16,208},{20,212},{24,216},{28,22... | collective-permute-start | bytes 208904 | tf_op jit(solution)/shard_map/ppermute | solution.py:335
  129.9 0.5 collective-permute-start.8
  130.4 0.3 collective-permute-start.7
  130.7 1.1 collective-permute-done.9
  131.8 2.8 %collective-permute-done.8 = f32[136,128]{1,0:T(8,128)S(1)} collective-permute-done((f32[136,128]{1,0:T(8,128)S(1)}, f32[136,128]{1,0:T(8,128)S(1)}, u32[]{:S(2)}, u32[]{:S(2)}) %collective-permute-start.8) | collective-permute-done | bytes 69664 | tf_op jit(solution)/shard_map/ppermute | solution.py:335
  134.6 0.0 collective-permute-done.7
  134.6 2.8 %collective-permute-start.12 = (f32[136,128]{1,0:T(8,128)S(1)}, f32[136,128]{1,0:T(8,128)S(1)}, u32[]{:S(2)}, u32[]{:S(2)}) collective-permute-start(f32[136,128]{1,0:T(8,128)S(1)} %add_add_fusion.1), channel_id=1, source_target_pairs={{0,48},{4,52},{8,56},{12,60},{16,32},{20,36},{24,40},{28,44},{32,1... | collective-permute-start | bytes 208904 | tf_op jit(solution)/shard_map/ppermute | solution.py:335
  137.4 0.3 collective-permute-start.11
  137.8 0.3 collective-permute-start.10
  138.1 1.3 collective-permute-done.12
  139.4 2.8 %collective-permute-done.11 = f32[136,128]{1,0:T(8,128)S(1)} collective-permute-done((f32[136,128]{1,0:T(8,128)S(1)}, f32[136,128]{1,0:T(8,128)S(1)}, u32[]{:S(2)}, u32[]{:S(2)}) %collective-permute-start.11) | collective-permute-done | bytes 69664 | tf_op jit(solution)/shard_map/ppermute | solution.py:335
  142.2 0.0 collective-permute-done.10
  142.2 0.1 collective-permute-start.15
  142.3 4.8 %collective-permute-start.14 = (f32[136,128]{1,0:T(8,128)S(1)}, f32[136,128]{1,0:T(8,128)S(1)}, u32[]{:S(2)}, u32[]{:S(2)}) collective-permute-start(f32[136,128]{1,0:T(8,128)S(1)} %add_add_fusion.t0), channel_id=1, source_target_pairs={{0,8},{4,12},{8,0},{12,4},{16,24},{20,28},{24,16},{28,20},{32,40},... | collective-permute-start | bytes 208904 | tf_op jit(solution)/shard_map/ppermute | solution.py:335
  147.2 0.0 collective-permute-start.13
  147.2 0.0 collective-permute-done.15.t3
  147.2 3.4 %collective-permute-done.14.t2 = f32[136,128]{1,0:T(8,128)S(1)} collective-permute-done((f32[136,128]{1,0:T(8,128)S(1)}, f32[136,128]{1,0:T(8,128)S(1)}, u32[]{:S(2)}, u32[]{:S(2)}) %collective-permute-start.14) | collective-permute-done | bytes 69664 | tf_op jit(solution)/shard_map/ppermute | solution.py:335
  150.5 0.0 collective-permute-done.13.t1
  150.5 5.4 %modes.1 = (f32[16,2,32,32]{3,2,1,0:T(8,128)}, bf16[16,2,3,32,768]{4,3,2,1,0:T(8,128)(2,1)}) custom-call(f32[136,128]{1,0:T(8,128)S(1)} %add_add_fusion.t0, f32[136,128]{1,0:T(8,128)S(1)} %collective-permute-done.13.t1, f32[136,128]{1,0:T(8,128)S(1)} %collective-permute-done.14.t2, f32[136,128]{1,0:T(8,128)S(1)} %collective-permute-done.15.t3, ...), custom_call_target="tpu_custom_call" | custom-call | tf_op jit(solution)/shard_map/modes/pallas_call | solution.py:317
  (3 shorter events, 0.0 us)
Async XLA Ops:
  2.3 19.2 %collective-permute-start.3 = (bf16[3,64,768]{2,1,0:T(8,128)(2,1)}, bf16[3,64,768]{2,1,0:T(8,128)(2,1)}, u32[]{:S(2)}, u32[]{:S(2)}) collective-permute-start(bf16[3,64,768]{2,1,0:T(8,128)(2,1)} %dynamic-slice_bitcast_fusion), channel_id=1, source_target_pairs={{1,0},{2,1},{3,2},{4,5},{5,6},{6,7},{7,4},{9,8},{10,9},{11,10},{12... | collective-permute-start | bytes 884744 | tf_op jit(solution)/shard_map/ppermute | solution.py:373
  8.1 13.5 %copy-start.2 = (bf16[512,3,768]{2,0,1:T(8,128)(2,1)S(1)}, bf16[512,3,768]{2,0,1:T(8,128)(2,1)}, u32[]{:S(2)}) copy-start(bf16[512,3,768]{2,0,1:T(8,128)(2,1)} %param.6) | copy-start | bytes 7077892
  8.1 13.5 %copy-start.3 = (bf16[64,3,768]{2,0,1:T(8,128)(2,1)S(1)}, bf16[64,3,768]{2,0,1:T(8,128)(2,1)}, u32[]{:S(2)}) copy-start(bf16[64,3,768]{2,0,1:T(8,128)(2,1)} %param.7) | copy-start | bytes 884740
  8.1 13.5 %copy-start.4 = (bf16[8,128,384]{2,1,0:T(8,128)(2,1)S(1)}, bf16[8,128,384]{2,1,0:T(8,128)(2,1)}, u32[]{:S(2)}) copy-start(bf16[8,128,384]{2,1,0:T(8,128)(2,1)} %constant.33.clone.band) | copy-start | bytes 2359300
  12.9 34.1 %collective-permute-start = (bf16[8,3,16,768]{3,2,1,0:T(8,128)(2,1)}, bf16[8,3,16,768]{3,2,1,0:T(8,128)(2,1)}, u32[]{:S(2)}, u32[]{:S(2)}) collective-permute-start(bf16[8,3,16,768]{3,2,1,0:T(8,128)(2,1)} %get-tuple-element.13), channel_id=1, source_target_pairs={{0,1},{1,2},{2,3},{3,0},{4,5},{5,6},{6,7},{7,4},{8,9},{9,10},{10,1... | collective-permute-start | bytes 1769480 | tf_op jit(solution)/shard_map/ppermute | solution.py:351
  17.1 56.7 %collective-permute-start.1 = (bf16[8,3,16,768]{3,2,1,0:T(8,128)(2,1)}, bf16[8,3,16,768]{3,2,1,0:T(8,128)(2,1)}, u32[]{:S(2)}, u32[]{:S(2)}) collective-permute-start(bf16[8,3,16,768]{3,2,1,0:T(8,128)(2,1)} %get-tuple-element.14), channel_id=1, source_target_pairs={{0,2},{1,3},{2,0},{3,1},{4,6},{5,7},{6,4},{7,5},{8,10},{9,11},{10,... | collective-permute-start | bytes 1769480 | tf_op jit(solution)/shard_map/ppermute | solution.py:351
  18.0 92.0 %collective-permute-start.2 = (bf16[8,3,16,768]{3,2,1,0:T(8,128)(2,1)}, bf16[8,3,16,768]{3,2,1,0:T(8,128)(2,1)}, u32[]{:S(2)}, u32[]{:S(2)}) collective-permute-start(bf16[8,3,16,768]{3,2,1,0:T(8,128)(2,1)} %get-tuple-element.15), channel_id=1, source_target_pairs={{0,3},{1,0},{2,1},{3,2},{4,7},{5,4},{6,5},{7,6},{8,11},{9,8},{10,9... | collective-permute-start | bytes 1769480 | tf_op jit(solution)/shard_map/ppermute | solution.py:351
  21.6 25.4 %copy-start.5 = (f32[768]{0:T(1024)S(1)}, f32[768]{0:T(1024)}, u32[]{:S(2)}) copy-start(f32[768]{0:T(1024)} %param.8) | copy-start | bytes 9220
  21.6 100.9 %copy-start = (bf16[8,3,16,768]{3,2,1,0:T(8,128)(2,1)S(1)}, bf16[8,3,16,768]{3,2,1,0:T(8,128)(2,1)}, u32[]{:S(2)}) copy-start(bf16[8,3,16,768]{3,2,1,0:T(8,128)(2,1)} %get-tuple-element.12.refs_0_) | copy-start | bytes 1769476
  21.6 100.9 %copy-start.1 = (bf16[8,128,128]{2,1,0:T(8,128)(2,1)S(1)}, bf16[8,128,128]{2,1,0:T(8,128)(2,1)}, u32[]{:S(2)}) copy-start(bf16[8,128,128]{2,1,0:T(8,128)(2,1)} %constant.34.clone.refs_9_.orders) | copy-start | bytes 786436
  24.7 85.3 %collective-permute-start.4 = (bf16[8,3,16,768]{3,2,1,0:T(8,128)(2,1)S(1)}, bf16[8,3,16,768]{3,2,1,0:T(8,128)(2,1)S(1)}, u32[]{:S(2)}, u32[]{:S(2)}) collective-permute-start(bf16[8,3,16,768]{3,2,1,0:T(8,128)(2,1)S(1)} %get-tuple-element.17), channel_id=1, source_target_pairs={{0,1},{1,2},{2,3},{3,0},{4,5},{5,6},{6,7},{7,4},{8,9},{9,10},{10,1... | collective-permute-start | bytes 1769480 | tf_op jit(solution)/shard_map/ppermute | solution.py:351
  30.9 79.6 %collective-permute-start.5 = (bf16[8,3,16,768]{3,2,1,0:T(8,128)(2,1)S(1)}, bf16[8,3,16,768]{3,2,1,0:T(8,128)(2,1)S(1)}, u32[]{:S(2)}, u32[]{:S(2)}) collective-permute-start(bf16[8,3,16,768]{3,2,1,0:T(8,128)(2,1)S(1)} %get-tuple-element.18), channel_id=1, source_target_pairs={{0,2},{1,3},{2,0},{3,1},{4,6},{5,7},{6,4},{7,5},{8,10},{9,11},{10,... | collective-permute-start | bytes 1769480 | tf_op jit(solution)/shard_map/ppermute | solution.py:351
  47.0 75.5 %collective-permute-start.6 = (bf16[8,3,16,768]{3,2,1,0:T(8,128)(2,1)S(1)}, bf16[8,3,16,768]{3,2,1,0:T(8,128)(2,1)S(1)}, u32[]{:S(2)}, u32[]{:S(2)}) collective-permute-start(bf16[8,3,16,768]{3,2,1,0:T(8,128)(2,1)S(1)} %get-tuple-element.19), channel_id=1, source_target_pairs={{0,3},{1,0},{2,1},{3,2},{4,7},{5,4},{6,5},{7,6},{8,11},{9,8},{10,9... | collective-permute-start | bytes 1769480 | tf_op jit(solution)/shard_map/ppermute | solution.py:351
  127.3 4.5 %collective-permute-start.9 = (f32[136,128]{1,0:T(8,128)S(1)}, f32[136,128]{1,0:T(8,128)S(1)}, u32[]{:S(2)}, u32[]{:S(2)}) collective-permute-start(f32[136,128]{1,0:T(8,128)S(1)} %gram_terms.1), channel_id=1, source_target_pairs={{0,192},{4,196},{8,200},{12,204},{16,208},{20,212},{24,216},{28,22... | collective-permute-start | bytes 208904 | tf_op jit(solution)/shard_map/ppermute | solution.py:335
  129.9 4.7 %collective-permute-start.8 = (f32[136,128]{1,0:T(8,128)S(1)}, f32[136,128]{1,0:T(8,128)S(1)}, u32[]{:S(2)}, u32[]{:S(2)}) collective-permute-start(f32[136,128]{1,0:T(8,128)S(1)} %gram_terms.1), channel_id=1, source_target_pairs={{0,128},{4,132},{8,136},{12,140},{16,144},{20,148},{24,152},{28,15... | collective-permute-start | bytes 208904 | tf_op jit(solution)/shard_map/ppermute | solution.py:335
  130.4 4.1 %collective-permute-start.7 = (f32[136,128]{1,0:T(8,128)S(1)}, f32[136,128]{1,0:T(8,128)S(1)}, u32[]{:S(2)}, u32[]{:S(2)}) collective-permute-start(f32[136,128]{1,0:T(8,128)S(1)} %gram_terms.1), channel_id=1, source_target_pairs={{0,64},{4,68},{8,72},{12,76},{16,80},{20,84},{24,88},{28,92},{32,9... | collective-permute-start | bytes 208904 | tf_op jit(solution)/shard_map/ppermute | solution.py:335
  134.6 4.8 %collective-permute-start.12 = (f32[136,128]{1,0:T(8,128)S(1)}, f32[136,128]{1,0:T(8,128)S(1)}, u32[]{:S(2)}, u32[]{:S(2)}) collective-permute-start(f32[136,128]{1,0:T(8,128)S(1)} %add_add_fusion.1), channel_id=1, source_target_pairs={{0,48},{4,52},{8,56},{12,60},{16,32},{20,36},{24,40},{28,44},{32,1... | collective-permute-start | bytes 208904 | tf_op jit(solution)/shard_map/ppermute | solution.py:335
  137.4 4.8 %collective-permute-start.11 = (f32[136,128]{1,0:T(8,128)S(1)}, f32[136,128]{1,0:T(8,128)S(1)}, u32[]{:S(2)}, u32[]{:S(2)}) collective-permute-start(f32[136,128]{1,0:T(8,128)S(1)} %add_add_fusion.1), channel_id=1, source_target_pairs={{0,32},{4,36},{8,40},{12,44},{16,48},{20,52},{24,56},{28,60},{32,0... | collective-permute-start | bytes 208904 | tf_op jit(solution)/shard_map/ppermute | solution.py:335
  137.8 4.4 %collective-permute-start.10 = (f32[136,128]{1,0:T(8,128)S(1)}, f32[136,128]{1,0:T(8,128)S(1)}, u32[]{:S(2)}, u32[]{:S(2)}) collective-permute-start(f32[136,128]{1,0:T(8,128)S(1)} %add_add_fusion.1), channel_id=1, source_target_pairs={{0,16},{4,20},{8,24},{12,28},{16,0},{20,4},{24,8},{28,12},{32,48},... | collective-permute-start | bytes 208904 | tf_op jit(solution)/shard_map/ppermute | solution.py:335
  142.2 4.9 %collective-permute-start.15 = (f32[136,128]{1,0:T(8,128)S(1)}, f32[136,128]{1,0:T(8,128)S(1)}, u32[]{:S(2)}, u32[]{:S(2)}) collective-permute-start(f32[136,128]{1,0:T(8,128)S(1)} %add_add_fusion.t0), channel_id=1, source_target_pairs={{0,12},{4,8},{8,4},{12,0},{16,28},{20,24},{24,20},{28,16},{32,44},... | collective-permute-start | bytes 208904 | tf_op jit(solution)/shard_map/ppermute | solution.py:335
  142.3 8.2 %collective-permute-start.14 = (f32[136,128]{1,0:T(8,128)S(1)}, f32[136,128]{1,0:T(8,128)S(1)}, u32[]{:S(2)}, u32[]{:S(2)}) collective-permute-start(f32[136,128]{1,0:T(8,128)S(1)} %add_add_fusion.t0), channel_id=1, source_target_pairs={{0,8},{4,12},{8,0},{12,4},{16,24},{20,28},{24,16},{28,20},{32,40},... | collective-permute-start | bytes 208904 | tf_op jit(solution)/shard_map/ppermute | solution.py:335
  147.2 3.4 %collective-permute-start.13 = (f32[136,128]{1,0:T(8,128)S(1)}, f32[136,128]{1,0:T(8,128)S(1)}, u32[]{:S(2)}, u32[]{:S(2)}) collective-permute-start(f32[136,128]{1,0:T(8,128)S(1)} %add_add_fusion.t0), channel_id=1, source_target_pairs={{0,4},{4,0},{8,12},{12,8},{16,20},{20,16},{24,28},{28,24},{32,36},... | collective-permute-start | bytes 208904 | tf_op jit(solution)/shard_map/ppermute | solution.py:335

commit v6 on v4

--- a/solution.py
+++ b/solution.py
@@ -21,10 +21,11 @@
 HERE = SLOTS // TM
 BODY = HALF * HOP
 ALL = (0, HERE // 2)
-QUADS = HERE // 4
+PAIRS, QUADS = HERE // 2, HERE // 4
 PARTS = ((0, 3), (3, QUADS))
 LONG = 10**12
 F32, BF16 = jnp.float32, jnp.bfloat16
+HELD = pl.BlockSpec(memory_space=pltpu.VMEM)
 ANY = pl.BlockSpec(memory_space=pl.ANY)
 WHOLE, PART = 60 << 20, 16 << 20
 
@@ -237,7 +238,7 @@
 
 def mix(mat, is_first):
     lane, first, low = lane_masks()
-    zero = lane < zero_lanes(is_first, 2 * NB)
+    zero = lane < (zero_lanes(True, 2 * NB) if is_first else 0)
     squares = mat * mat
 
     def part_sum(keep):
@@ -266,55 +267,54 @@
     return mixing.astype(BF16)
 
 
-def modes_kernel(t0, t1, t2, t3, spec, gram, modes, mats, mixings):
-    pair = pl.program_id(0)
-
-    @pl.when(pair == 0)
-    def _():
-        total = ((t0[...] + t1[...]) + (t2[...] + t3[...])) / (NB * 3 * NPOINTS)
-        row, column = triangle()
-        lane, _, _ = lane_masks()
-        for u in range(QUADS):
-            packed = total[u * NB : (u + 1) * NB]
-            other = transposed(packed)
-            even = jnp.where(row <= column, packed, other)
-            odd = jnp.where(row > column, packed, jnp.where(row < column, -other, 0.0))
-            if u == 0:
-                diagonal = total[QUADS * NB : QUADS * NB + 1]
-                alone = jnp.where(row < column, other, jnp.where(row > column, packed, diagonal))
-                odd = jnp.where(lane < zero_lanes(True, NB), alone, odd)
-            one = by_quarter([even, turn(odd, 1), turn(even, 1), turn(odd, 2)])
-            two = by_quarter([turn(even, 2), turn(odd, -1), turn(even, -1), odd])
-            mats[2 * u], mats[2 * u + 1] = one, two
-            mixings[2 * u], mixings[2 * u + 1] = mix(one, u == 0), mix(two, False)
-
-    mat = mats[pair]
-    for s in range(2):
-        for part in range(2):
-            at = (2 * s + part) * NB
-            gram[s, part] = mat[:, at : at + NB]
-    for c in range(3):
-        got = jnp.dot(mixings[pair], spec[0, c], preferred_element_type=F32)
-        modes[:, :, c] = got.astype(BF16).reshape(2, 2, NB, PDEV)
+def modes_kernel(t0, t1, t2, t3, spec, gram_out, modes_out, gram, modes, sems):
+    total = ((t0[...] + t1[...]) + (t2[...] + t3[...])) / (NB * 3 * NPOINTS)
+    row, column = triangle()
+    lane, _, _ = lane_masks()
+    mats = []
+    for u in range(QUADS):
+        packed = total[u * NB : (u + 1) * NB]
+        other = transposed(packed)
+        even = jnp.where(row <= column, packed, other)
+        odd = jnp.where(row > column, packed, jnp.where(row < column, -other, 0.0))
+        if u == 0:
+            diagonal = total[QUADS * NB : QUADS * NB + 1]
+            alone = jnp.where(row < column, other, jnp.where(row > column, packed, diagonal))
+            odd = jnp.where(lane < zero_lanes(True, NB), alone, odd)
+        mats.append(by_quarter([even, turn(odd, 1), turn(even, 1), turn(odd, 2)]))
+        mats.append(by_quarter([turn(even, 2), turn(odd, -1), turn(even, -1), odd]))
+    mixings = [mix(mat, pair == 0) for pair, mat in enumerate(mats)]
+    copies = []
+    for pair in range(PAIRS):
+        slots = pl.ds(2 * pair, 2)
+        for c in range(3):
+            got = jnp.dot(mixings[pair], spec[pair, c], preferred_element_type=F32)
+            modes[slots, :, c] = got.astype(BF16).reshape(2, 2, NB, PDEV)
+        copies.append(pltpu.make_async_copy(modes.at[slots], modes_out.at[slots], sems.at[pair]))
+        copies[-1].start()
+    for pair, mat in enumerate(mats):
+        for s in range(2):
+            for part in range(2):
+                at = (2 * s + part) * NB
+                gram[2 * pair + s, part] = mat[:, at : at + NB]
+    copies.append(pltpu.make_async_copy(gram, gram_out, sems.at[PAIRS]))
+    copies[-1].start()
+    for copy in copies:
+        copy.wait()
 
 
 def project(totals, spec):
+    gram = jax.ShapeDtypeStruct((HERE, 2, NB, NB), F32)
+    modes = jax.ShapeDtypeStruct((HERE, 2, 3, NB, PDEV), BF16)
     return pl.pallas_call(
         modes_kernel,
-        grid=(2 * QUADS,),
-        in_specs=[pl.BlockSpec(totals[0].shape, lambda p: (0, 0))] * 4
-        + [pl.BlockSpec((1, 3, 4 * NB, PDEV), lambda p: (p, 0, 0, 0))],
-        out_specs=[
-            pl.BlockSpec((2, 2, NB, NB), lambda p: (p, 0, 0, 0)),
-            pl.BlockSpec((2, 2, 3, NB, PDEV), lambda p: (p, 0, 0, 0, 0)),
-        ],
-        out_shape=[
-            jax.ShapeDtypeStruct((HERE, 2, NB, NB), F32),
-            jax.ShapeDtypeStruct((HERE, 2, 3, NB, PDEV), BF16),
-        ],
+        in_specs=[HELD] * 5,
+        out_specs=[pl.BlockSpec(memory_space=pl.ANY)] * 2,
+        out_shape=[gram, modes],
         scratch_shapes=[
-            pltpu.VMEM((2 * QUADS, NB, 4 * NB), F32),
-            pltpu.VMEM((2 * QUADS, 4 * NB, 4 * NB), BF16),
+            pltpu.VMEM(gram.shape, F32),
+            pltpu.VMEM(modes.shape, BF16),
+            pltpu.SemaphoreType.DMA((PAIRS + 1,)),
         ],
         compiler_params=pltpu.CompilerParams(vmem_limit_bytes=PART),
         cost_estimate=pl.CostEstimate(flops=0, bytes_accessed=0, transcendentals=0),

time: 155 us -> 154 us (level)
  Pallas kernels: 23.7 us -> 22 us
    pallas_call x1, Pallas kernels: 5.59 us -> 3.87 us  [project(): pl.pallas_call(modes_kernel, in_specs=[HELD] * 5, out_specs=[pl.BlockSpec...]
where the time goes in v6:
time: 154 us; the launch traced here: 153 us
  waiting for transfers between devices  76.4 us (50%)
  starting transfers between devices  52.2 us (34%)
  Pallas kernels  22 us (14%)
  local copies, waits for them, and re-layouts  1.74 us (1%)
    ppermute x9, waiting for transfers between devices, from_behind(): return lax.ppermute(block, 'tm', route)  65 us
    ppermute x9, starting transfers between devices, from_behind(): return lax.ppermute(block, 'tm', route)  34.7 us
    ppermute x9, starting transfers between devices, over_space(): return lax.ppermute(block, 'space', route)  11.8 us
    pallas_call x3, Pallas kernels, transform(): pl.pallas_call(functools.partial(kernel, pairs), grid=(3,), in_specs=[pl....  11.5 us
    ppermute x9, waiting for transfers between devices, over_space(): return lax.ppermute(block, 'space', route)  11.3 us
    pallas_call x2, Pallas kernels, gram_terms(): pl.pallas_call(functools.partial(gram_kernel, quads), grid=(count,), in_s...  6.69 us
    ppermute x1, starting transfers between devices, body(): moved = lax.ppermute(edge, ('space', 'tm'), half_block_route())  5.72 us
    pallas_call x1, Pallas kernels, project(): pl.pallas_call(modes_kernel, in_specs=[HELD] * 5, out_specs=[pl.BlockSpec...  3.87 us
  transfers between devices with their start and end apart: 19, of which 9 were waited for; matrix products, arithmetic and copies ran while one was open for 0% of the time, Pallas kernels for 10%

profile of v6, /device:TPU:1, one launch (start us, length us, event | category | flops | bytes accessed | tf_op | source)
XLA Modules:
  0.0 153.4 jit_solution(804198294617368725)
XLA Ops:
  0.6 1.7 %dynamic-slice_bitcast_fusion = bf16[3,64,768]{2,1,0:T(8,128)(2,1)} fusion(bf16[512,3,768]{2,0,1:T(8,128)(2,1)} %param.5, s32[]{:T(128)S(6)} %select_n.11), kind=kLoop, calls=%fused_computation | loop fusion | bytes 589828 | tf_op jit(solution)/shard_map/dynamic_slice | solution.py:364
  2.3 5.7 %collective-permute-start.3 = (bf16[3,64,768]{2,1,0:T(8,128)(2,1)}, bf16[3,64,768]{2,1,0:T(8,128)(2,1)}, u32[]{:S(2)}, u32[]{:S(2)}) collective-permute-start(bf16[3,64,768]{2,1,0:T(8,128)(2,1)} %dynamic-slice_bitcast_fusion), channel_id=1, source_target_pairs={{1,0},{2,1},{3,2},{4,5},{5,6},{6,7},{7,4},{9,8},{10,9},{11,10},{12... | collective-permute-start | bytes 884744 | tf_op jit(solution)/shard_map/ppermute | solution.py:365
  8.1 0.0 copy-start.4
  8.1 0.0 copy-start.1
  8.1 0.0 copy-start.2
  8.1 0.0 copy-start.3
  8.1 4.7 %transform.3 = (bf16[8,3,16,768]{3,2,1,0:T(8,128)(2,1)}, bf16[8,3,16,768]{3,2,1,0:T(8,128)(2,1)}, bf16[8,3,16,768]{3,2,1,0:T(8,128)(2,1)}, bf16[8,3,16,768]{3,2,1,0:T(8,128)(2,1)}) custom-call(bf16[4,128,320]{2,1,0:T(8,128)(2,1)} %constant.30.clone.band, bf16[3,512,768]{2,1,0:T(8,128)(2,1)} %bitcast.5, bf16[3,512,768]{2,1,0:T(8,128)(2,1)} %bitcast.6), custom_call_target="tpu_custom_call" | custom-call | flops 999999995904 | tf_op jit(solution)/shard_map/transform/pallas_call | solution.py:98
  12.8 4.2 %collective-permute-start = (bf16[8,3,16,768]{3,2,1,0:T(8,128)(2,1)}, bf16[8,3,16,768]{3,2,1,0:T(8,128)(2,1)}, u32[]{:S(2)}, u32[]{:S(2)}) collective-permute-start(bf16[8,3,16,768]{3,2,1,0:T(8,128)(2,1)} %get-tuple-element.21), channel_id=1, source_target_pairs={{0,1},{1,2},{2,3},{3,0},{4,5},{5,6},{6,7},{7,4},{8,9},{9,10},{10,1... | collective-permute-start | bytes 1769480 | tf_op jit(solution)/shard_map/ppermute | solution.py:343
  17.0 1.0 collective-permute-start.1
  18.0 3.5 %collective-permute-start.2 = (bf16[8,3,16,768]{3,2,1,0:T(8,128)(2,1)}, bf16[8,3,16,768]{3,2,1,0:T(8,128)(2,1)}, u32[]{:S(2)}, u32[]{:S(2)}) collective-permute-start(bf16[8,3,16,768]{3,2,1,0:T(8,128)(2,1)} %get-tuple-element.23), channel_id=1, source_target_pairs={{0,3},{1,0},{2,1},{3,2},{4,7},{5,4},{6,5},{7,6},{8,11},{9,8},{10,9... | collective-permute-start | bytes 1769480 | tf_op jit(solution)/shard_map/ppermute | solution.py:343
  21.5 0.0 copy-done.4
  21.5 0.0 collective-permute-done.3.moved
  21.5 0.0 copy-done.1
  21.5 0.0 copy-done.2
  21.5 0.0 copy-done.3
  21.5 3.7 %transform.5 = (bf16[6,3,16,768]{3,2,1,0:T(8,128)(2,1)S(1)}, bf16[6,3,16,768]{3,2,1,0:T(8,128)(2,1)}, bf16[6,3,16,768]{3,2,1,0:T(8,128)(2,1)}, bf16[6,3,16,768]{3,2,1,0:T(8,128)(2,1)}) custom-call(bf16[8,128,384]{2,1,0:T(8,128)(2,1)S(1)} %copy-done.3, bf16[3,512,768]{2,1,0:T(8,128)(2,1)S(1)} %bitcast.7, bf16[3,512,768]{2,1,0:T(8,128)(2,1)S(1)} %bitcast.8, ...), custom_call_target="tpu_custom_call" | custom-call | flops 999999995904 | tf_op jit(solution)/shard_map/transform/pallas_call | solution.py:98
  25.2 6.3 %collective-permute-start.7 = (bf16[6,3,16,768]{3,2,1,0:T(8,128)(2,1)}, bf16[6,3,16,768]{3,2,1,0:T(8,128)(2,1)}, u32[]{:S(2)}, u32[]{:S(2)}) collective-permute-start(bf16[6,3,16,768]{3,2,1,0:T(8,128)(2,1)} %get-tuple-element.29), channel_id=1, source_target_pairs={{0,1},{1,2},{2,3},{3,0},{4,5},{5,6},{6,7},{7,4},{8,9},{9,10},{10,1... | collective-permute-start | bytes 1327112 | tf_op jit(solution)/shard_map/ppermute | solution.py:343
  31.4 4.2 %collective-permute-start.8 = (bf16[6,3,16,768]{3,2,1,0:T(8,128)(2,1)}, bf16[6,3,16,768]{3,2,1,0:T(8,128)(2,1)}, u32[]{:S(2)}, u32[]{:S(2)}) collective-permute-start(bf16[6,3,16,768]{3,2,1,0:T(8,128)(2,1)} %get-tuple-element.30), channel_id=1, source_target_pairs={{0,2},{1,3},{2,0},{3,1},{4,6},{5,7},{6,4},{7,5},{8,10},{9,11},{10,... | collective-permute-start | bytes 1327112 | tf_op jit(solution)/shard_map/ppermute | solution.py:343
  35.6 11.7 %collective-permute-done.refs_1_ = bf16[8,3,16,768]{3,2,1,0:T(8,128)(2,1)} collective-permute-done((bf16[8,3,16,768]{3,2,1,0:T(8,128)(2,1)}, bf16[8,3,16,768]{3,2,1,0:T(8,128)(2,1)}, u32[]{:S(2)}, u32[]{:S(2)}) %collective-permute-start) | collective-permute-done | bytes 589856 | tf_op jit(solution)/shard_map/ppermute | solution.py:343
  47.3 0.0 collective-permute-start.9
  47.3 0.0 copy-start
  47.3 3.2 %transform.4 = (bf16[2,3,16,768]{3,2,1,0:T(8,128)(2,1)S(1)}, bf16[2,3,16,768]{3,2,1,0:T(8,128)(2,1)}, bf16[2,3,16,768]{3,2,1,0:T(8,128)(2,1)}, bf16[2,3,16,768]{3,2,1,0:T(8,128)(2,1)}) custom-call(bf16[8,128,384]{2,1,0:T(8,128)(2,1)S(1)} %copy-done.3, bf16[3,512,768]{2,1,0:T(8,128)(2,1)S(1)} %bitcast.9, bf16[3,512,768]{2,1,0:T(8,128)(2,1)S(1)} %bitcast.10, ...), custom_call_target="tpu_custom_call" | custom-call | flops 999999995904 | tf_op jit(solution)/shard_map/transform/pallas_call | solution.py:98
  50.5 23.7 %collective-permute-done.1.refs_2_ = bf16[8,3,16,768]{3,2,1,0:T(8,128)(2,1)} collective-permute-done((bf16[8,3,16,768]{3,2,1,0:T(8,128)(2,1)}, bf16[8,3,16,768]{3,2,1,0:T(8,128)(2,1)}, u32[]{:S(2)}, u32[]{:S(2)}) %collective-permute-start.1) | collective-permute-done | bytes 589856 | tf_op jit(solution)/shard_map/ppermute | solution.py:343
  74.1 10.4 %collective-permute-start.4 = (bf16[2,3,16,768]{3,2,1,0:T(8,128)(2,1)}, bf16[2,3,16,768]{3,2,1,0:T(8,128)(2,1)}, u32[]{:S(2)}, u32[]{:S(2)}) collective-permute-start(bf16[2,3,16,768]{3,2,1,0:T(8,128)(2,1)} %get-tuple-element.25), channel_id=1, source_target_pairs={{0,1},{1,2},{2,3},{3,0},{4,5},{5,6},{6,7},{7,4},{8,9},{9,10},{10,1... | collective-permute-start | bytes 442376 | tf_op jit(solution)/shard_map/ppermute | solution.py:343
  84.6 25.4 %collective-permute-done.2.refs_3_ = bf16[8,3,16,768]{3,2,1,0:T(8,128)(2,1)} collective-permute-done((bf16[8,3,16,768]{3,2,1,0:T(8,128)(2,1)}, bf16[8,3,16,768]{3,2,1,0:T(8,128)(2,1)}, u32[]{:S(2)}, u32[]{:S(2)}) %collective-permute-start.2) | collective-permute-done | bytes 589856 | tf_op jit(solution)/shard_map/ppermute | solution.py:343
  109.9 4.1 %collective-permute-start.5 = (bf16[2,3,16,768]{3,2,1,0:T(8,128)(2,1)}, bf16[2,3,16,768]{3,2,1,0:T(8,128)(2,1)}, u32[]{:S(2)}, u32[]{:S(2)}) collective-permute-start(bf16[2,3,16,768]{3,2,1,0:T(8,128)(2,1)} %get-tuple-element.26), channel_id=1, source_target_pairs={{0,2},{1,3},{2,0},{3,1},{4,6},{5,7},{6,4},{7,5},{8,10},{9,11},{10,... | collective-permute-start | bytes 442376 | tf_op jit(solution)/shard_map/ppermute | solution.py:343
  114.1 0.0 collective-permute-done.7.refs_5_
  114.1 1.0 collective-permute-start.6
  115.1 0.0 collective-permute-done.8.refs_6_
  115.1 4.3 %collective-permute-done.9.refs_7_ = bf16[6,3,16,768]{3,2,1,0:T(8,128)(2,1)} collective-permute-done((bf16[6,3,16,768]{3,2,1,0:T(8,128)(2,1)}, bf16[6,3,16,768]{3,2,1,0:T(8,128)(2,1)}, u32[]{:S(2)}, u32[]{:S(2)}) %collective-permute-start.9) | collective-permute-done | bytes 442400 | tf_op jit(solution)/shard_map/ppermute | solution.py:343
  119.4 0.0 copy-done
  119.4 4.5 %gram_terms.2 = (f32[136,128]{1,0:T(8,128)S(1)}, bf16[8,3,128,768]{3,2,1,0:T(8,128)(2,1)S(1)}) custom-call(bf16[8,3,16,768]{3,2,1,0:T(8,128)(2,1)S(1)} %copy-done, bf16[8,3,16,768]{3,2,1,0:T(8,128)(2,1)} %collective-permute-done.refs_1_, bf16[8,3,16,768]{3,2,1,0:T(8,128)(2,1)} %collective-permute-done.1.refs_2_, ...), custom_call_target="tpu_custom_call" | custom-call | flops 999999995904 | tf_op jit(solution)/shard_map/gram_terms/pallas_call | solution.py:216
  123.9 0.0 collective-permute-done.4.refs_5_
  123.9 0.0 collective-permute-done.5.refs_6_
  123.9 0.0 collective-permute-done.6.refs_7_
  123.9 2.2 %gram_terms.3 = (f32[136,128]{1,0:T(8,128)S(1)}, bf16[8,3,128,768]{3,2,1,0:T(8,128)(2,1)S(1)}) custom-call(bf16[8,3,16,768]{3,2,1,0:T(8,128)(2,1)S(1)} %copy-done, bf16[8,3,16,768]{3,2,1,0:T(8,128)(2,1)} %collective-permute-done.refs_1_, bf16[8,3,16,768]{3,2,1,0:T(8,128)(2,1)} %collective-permute-done.1.refs_2_, ...), custom_call_target="tpu_custom_call", output_to_operand_aliasing={{1}: (10, {})} | custom-call | tf_op jit(solution)/shard_map/gram_terms/pallas_call | solution.py:216
  126.2 2.6 %collective-permute-start.12 = (f32[136,128]{1,0:T(8,128)S(1)}, f32[136,128]{1,0:T(8,128)S(1)}, u32[]{:S(2)}, u32[]{:S(2)}) collective-permute-start(f32[136,128]{1,0:T(8,128)S(1)} %get-tuple-element.34), channel_id=1, source_target_pairs={{0,192},{4,196},{8,200},{12,204},{16,208},{20,212},{24,216},{28,22... | collective-permute-start | bytes 208904 | tf_op jit(solution)/shard_map/ppermute | solution.py:327
  128.7 0.5 collective-permute-start.11
  129.3 0.3 collective-permute-start.10
  129.5 1.1 collective-permute-done.12
  130.6 2.8 %collective-permute-done.11 = f32[136,128]{1,0:T(8,128)S(1)} collective-permute-done((f32[136,128]{1,0:T(8,128)S(1)}, f32[136,128]{1,0:T(8,128)S(1)}, u32[]{:S(2)}, u32[]{:S(2)}) %collective-permute-start.11) | collective-permute-done | bytes 69664 | tf_op jit(solution)/shard_map/ppermute | solution.py:327
  133.4 0.0 collective-permute-done.10
  133.4 2.8 %collective-permute-start.15 = (f32[136,128]{1,0:T(8,128)S(1)}, f32[136,128]{1,0:T(8,128)S(1)}, u32[]{:S(2)}, u32[]{:S(2)}) collective-permute-start(f32[136,128]{1,0:T(8,128)S(1)} %add_add_fusion.1), channel_id=1, source_target_pairs={{0,48},{4,52},{8,56},{12,60},{16,32},{20,36},{24,40},{28,44},{32,1... | collective-permute-start | bytes 208904 | tf_op jit(solution)/shard_map/ppermute | solution.py:327
  136.2 0.4 collective-permute-start.14
  136.6 0.3 collective-permute-start.13
  136.9 1.3 collective-permute-done.15
  138.2 2.8 %collective-permute-done.14 = f32[136,128]{1,0:T(8,128)S(1)} collective-permute-done((f32[136,128]{1,0:T(8,128)S(1)}, f32[136,128]{1,0:T(8,128)S(1)}, u32[]{:S(2)}, u32[]{:S(2)}) %collective-permute-start.14) | collective-permute-done | bytes 69664 | tf_op jit(solution)/shard_map/ppermute | solution.py:327
  141.0 0.0 collective-permute-done.13
  141.0 0.1 collective-permute-start.18
  141.1 4.8 %collective-permute-start.17 = (f32[136,128]{1,0:T(8,128)S(1)}, f32[136,128]{1,0:T(8,128)S(1)}, u32[]{:S(2)}, u32[]{:S(2)}) collective-permute-start(f32[136,128]{1,0:T(8,128)S(1)} %add_add_fusion.t0), channel_id=1, source_target_pairs={{0,8},{4,12},{8,0},{12,4},{16,24},{20,28},{24,16},{28,20},{32,40},... | collective-permute-start | bytes 208904 | tf_op jit(solution)/shard_map/ppermute | solution.py:327
  146.0 0.0 collective-permute-start.16
  146.0 0.0 collective-permute-done.18.t3
  146.0 3.4 %collective-permute-done.17.t2 = f32[136,128]{1,0:T(8,128)S(1)} collective-permute-done((f32[136,128]{1,0:T(8,128)S(1)}, f32[136,128]{1,0:T(8,128)S(1)}, u32[]{:S(2)}, u32[]{:S(2)}) %collective-permute-start.17) | collective-permute-done | bytes 69664 | tf_op jit(solution)/shard_map/ppermute | solution.py:327
  149.3 0.0 collective-permute-done.16.t1
  149.3 3.9 %modes.1 = (f32[16,2,32,32]{3,2,1,0:T(8,128)}, bf16[16,2,3,32,768]{4,3,2,1,0:T(8,128)(2,1)}) custom-call(f32[136,128]{1,0:T(8,128)S(1)} %add_add_fusion.t0, f32[136,128]{1,0:T(8,128)S(1)} %collective-permute-done.16.t1, f32[136,128]{1,0:T(8,128)S(1)} %collective-permute-done.17.t2, f32[136,128]{1,0:T(8,128)S(1)} %collective-permute-done.18.t3, ...), custom_call_target="tpu_custom_call" | custom-call | tf_op jit(solution)/shard_map/modes/pallas_call | solution.py:309
  (3 shorter events, 0.0 us)
Async XLA Ops:
  2.3 19.1 %collective-permute-start.3 = (bf16[3,64,768]{2,1,0:T(8,128)(2,1)}, bf16[3,64,768]{2,1,0:T(8,128)(2,1)}, u32[]{:S(2)}, u32[]{:S(2)}) collective-permute-start(bf16[3,64,768]{2,1,0:T(8,128)(2,1)} %dynamic-slice_bitcast_fusion), channel_id=1, source_target_pairs={{1,0},{2,1},{3,2},{4,5},{5,6},{6,7},{7,4},{9,8},{10,9},{11,10},{12... | collective-permute-start | bytes 884744 | tf_op jit(solution)/shard_map/ppermute | solution.py:365
  8.1 13.4 %copy-start.4 = (f32[768]{0:T(1024)S(1)}, f32[768]{0:T(1024)}, u32[]{:S(2)}) copy-start(f32[768]{0:T(1024)} %param.7) | copy-start | bytes 9220
  8.1 13.4 %copy-start.1 = (bf16[512,3,768]{2,0,1:T(8,128)(2,1)S(1)}, bf16[512,3,768]{2,0,1:T(8,128)(2,1)}, u32[]{:S(2)}) copy-start(bf16[512,3,768]{2,0,1:T(8,128)(2,1)} %param.5) | copy-start | bytes 7077892
  8.1 13.4 %copy-start.2 = (bf16[64,3,768]{2,0,1:T(8,128)(2,1)S(1)}, bf16[64,3,768]{2,0,1:T(8,128)(2,1)}, u32[]{:S(2)}) copy-start(bf16[64,3,768]{2,0,1:T(8,128)(2,1)} %param.6) | copy-start | bytes 884740
  8.1 13.4 %copy-start.3 = (bf16[8,128,384]{2,1,0:T(8,128)(2,1)S(1)}, bf16[8,128,384]{2,1,0:T(8,128)(2,1)}, u32[]{:S(2)}) copy-start(bf16[8,128,384]{2,1,0:T(8,128)(2,1)} %constant.31.clone.band) | copy-start | bytes 2359300
  12.8 34.5 %collective-permute-start = (bf16[8,3,16,768]{3,2,1,0:T(8,128)(2,1)}, bf16[8,3,16,768]{3,2,1,0:T(8,128)(2,1)}, u32[]{:S(2)}, u32[]{:S(2)}) collective-permute-start(bf16[8,3,16,768]{3,2,1,0:T(8,128)(2,1)} %get-tuple-element.21), channel_id=1, source_target_pairs={{0,1},{1,2},{2,3},{3,0},{4,5},{5,6},{6,7},{7,4},{8,9},{9,10},{10,1... | collective-permute-start | bytes 1769480 | tf_op jit(solution)/shard_map/ppermute | solution.py:343
  17.0 57.2 %collective-permute-start.1 = (bf16[8,3,16,768]{3,2,1,0:T(8,128)(2,1)}, bf16[8,3,16,768]{3,2,1,0:T(8,128)(2,1)}, u32[]{:S(2)}, u32[]{:S(2)}) collective-permute-start(bf16[8,3,16,768]{3,2,1,0:T(8,128)(2,1)} %get-tuple-element.22), channel_id=1, source_target_pairs={{0,2},{1,3},{2,0},{3,1},{4,6},{5,7},{6,4},{7,5},{8,10},{9,11},{10,... | collective-permute-start | bytes 1769480 | tf_op jit(solution)/shard_map/ppermute | solution.py:343
  18.0 92.0 %collective-permute-start.2 = (bf16[8,3,16,768]{3,2,1,0:T(8,128)(2,1)}, bf16[8,3,16,768]{3,2,1,0:T(8,128)(2,1)}, u32[]{:S(2)}, u32[]{:S(2)}) collective-permute-start(bf16[8,3,16,768]{3,2,1,0:T(8,128)(2,1)} %get-tuple-element.23), channel_id=1, source_target_pairs={{0,3},{1,0},{2,1},{3,2},{4,7},{5,4},{6,5},{7,6},{8,11},{9,8},{10,9... | collective-permute-start | bytes 1769480 | tf_op jit(solution)/shard_map/ppermute | solution.py:343
  25.2 88.9 %collective-permute-start.7 = (bf16[6,3,16,768]{3,2,1,0:T(8,128)(2,1)}, bf16[6,3,16,768]{3,2,1,0:T(8,128)(2,1)}, u32[]{:S(2)}, u32[]{:S(2)}) collective-permute-start(bf16[6,3,16,768]{3,2,1,0:T(8,128)(2,1)} %get-tuple-element.29), channel_id=1, source_target_pairs={{0,1},{1,2},{2,3},{3,0},{4,5},{5,6},{6,7},{7,4},{8,9},{9,10},{10,1... | collective-permute-start | bytes 1327112 | tf_op jit(solution)/shard_map/ppermute | solution.py:343
  31.4 83.7 %collective-permute-start.8 = (bf16[6,3,16,768]{3,2,1,0:T(8,128)(2,1)}, bf16[6,3,16,768]{3,2,1,0:T(8,128)(2,1)}, u32[]{:S(2)}, u32[]{:S(2)}) collective-permute-start(bf16[6,3,16,768]{3,2,1,0:T(8,128)(2,1)} %get-tuple-element.30), channel_id=1, source_target_pairs={{0,2},{1,3},{2,0},{3,1},{4,6},{5,7},{6,4},{7,5},{8,10},{9,11},{10,... | collective-permute-start | bytes 1327112 | tf_op jit(solution)/shard_map/ppermute | solution.py:343
  47.3 72.1 %collective-permute-start.9 = (bf16[6,3,16,768]{3,2,1,0:T(8,128)(2,1)}, bf16[6,3,16,768]{3,2,1,0:T(8,128)(2,1)}, u32[]{:S(2)}, u32[]{:S(2)}) collective-permute-start(bf16[6,3,16,768]{3,2,1,0:T(8,128)(2,1)} %get-tuple-element.31), channel_id=1, source_target_pairs={{0,3},{1,0},{2,1},{3,2},{4,7},{5,4},{6,5},{7,6},{8,11},{9,8},{10,9... | collective-permute-start | bytes 1327112 | tf_op jit(solution)/shard_map/ppermute | solution.py:343
  47.3 72.1 %copy-start = (bf16[8,3,16,768]{3,2,1,0:T(8,128)(2,1)S(1)}, bf16[8,3,16,768]{3,2,1,0:T(8,128)(2,1)}, u32[]{:S(2)}) copy-start(bf16[8,3,16,768]{3,2,1,0:T(8,128)(2,1)} %get-tuple-element.20.refs_0_) | copy-start | bytes 1769476
  74.1 49.8 %collective-permute-start.4 = (bf16[2,3,16,768]{3,2,1,0:T(8,128)(2,1)}, bf16[2,3,16,768]{3,2,1,0:T(8,128)(2,1)}, u32[]{:S(2)}, u32[]{:S(2)}) collective-permute-start(bf16[2,3,16,768]{3,2,1,0:T(8,128)(2,1)} %get-tuple-element.25), channel_id=1, source_target_pairs={{0,1},{1,2},{2,3},{3,0},{4,5},{5,6},{6,7},{7,4},{8,9},{9,10},{10,1... | collective-permute-start | bytes 442376 | tf_op jit(solution)/shard_map/ppermute | solution.py:343
  109.9 14.0 %collective-permute-start.5 = (bf16[2,3,16,768]{3,2,1,0:T(8,128)(2,1)}, bf16[2,3,16,768]{3,2,1,0:T(8,128)(2,1)}, u32[]{:S(2)}, u32[]{:S(2)}) collective-permute-start(bf16[2,3,16,768]{3,2,1,0:T(8,128)(2,1)} %get-tuple-element.26), channel_id=1, source_target_pairs={{0,2},{1,3},{2,0},{3,1},{4,6},{5,7},{6,4},{7,5},{8,10},{9,11},{10,... | collective-permute-start | bytes 442376 | tf_op jit(solution)/shard_map/ppermute | solution.py:343
  114.1 9.9 %collective-permute-start.6 = (bf16[2,3,16,768]{3,2,1,0:T(8,128)(2,1)}, bf16[2,3,16,768]{3,2,1,0:T(8,128)(2,1)}, u32[]{:S(2)}, u32[]{:S(2)}) collective-permute-start(bf16[2,3,16,768]{3,2,1,0:T(8,128)(2,1)} %get-tuple-element.27), channel_id=1, source_target_pairs={{0,3},{1,0},{2,1},{3,2},{4,7},{5,4},{6,5},{7,6},{8,11},{9,8},{10,9... | collective-permute-start | bytes 442376 | tf_op jit(solution)/shard_map/ppermute | solution.py:343
  126.2 4.5 %collective-permute-start.12 = (f32[136,128]{1,0:T(8,128)S(1)}, f32[136,128]{1,0:T(8,128)S(1)}, u32[]{:S(2)}, u32[]{:S(2)}) collective-permute-start(f32[136,128]{1,0:T(8,128)S(1)} %get-tuple-element.34), channel_id=1, source_target_pairs={{0,192},{4,196},{8,200},{12,204},{16,208},{20,212},{24,216},{28,22... | collective-permute-start | bytes 208904 | tf_op jit(solution)/shard_map/ppermute | solution.py:327
  128.7 4.7 %collective-permute-start.11 = (f32[136,128]{1,0:T(8,128)S(1)}, f32[136,128]{1,0:T(8,128)S(1)}, u32[]{:S(2)}, u32[]{:S(2)}) collective-permute-start(f32[136,128]{1,0:T(8,128)S(1)} %get-tuple-element.34), channel_id=1, source_target_pairs={{0,128},{4,132},{8,136},{12,140},{16,144},{20,148},{24,152},{28,15... | collective-permute-start | bytes 208904 | tf_op jit(solution)/shard_map/ppermute | solution.py:327
  129.3 4.1 %collective-permute-start.10 = (f32[136,128]{1,0:T(8,128)S(1)}, f32[136,128]{1,0:T(8,128)S(1)}, u32[]{:S(2)}, u32[]{:S(2)}) collective-permute-start(f32[136,128]{1,0:T(8,128)S(1)} %get-tuple-element.34), channel_id=1, source_target_pairs={{0,64},{4,68},{8,72},{12,76},{16,80},{20,84},{24,88},{28,92},{32,9... | collective-permute-start | bytes 208904 | tf_op jit(solution)/shard_map/ppermute | solution.py:327
  133.4 4.8 %collective-permute-start.15 = (f32[136,128]{1,0:T(8,128)S(1)}, f32[136,128]{1,0:T(8,128)S(1)}, u32[]{:S(2)}, u32[]{:S(2)}) collective-permute-start(f32[136,128]{1,0:T(8,128)S(1)} %add_add_fusion.1), channel_id=1, source_target_pairs={{0,48},{4,52},{8,56},{12,60},{16,32},{20,36},{24,40},{28,44},{32,1... | collective-permute-start | bytes 208904 | tf_op jit(solution)/shard_map/ppermute | solution.py:327
  136.2 4.8 %collective-permute-start.14 = (f32[136,128]{1,0:T(8,128)S(1)}, f32[136,128]{1,0:T(8,128)S(1)}, u32[]{:S(2)}, u32[]{:S(2)}) collective-permute-start(f32[136,128]{1,0:T(8,128)S(1)} %add_add_fusion.1), channel_id=1, source_target_pairs={{0,32},{4,36},{8,40},{12,44},{16,48},{20,52},{24,56},{28,60},{32,0... | collective-permute-start | bytes 208904 | tf_op jit(solution)/shard_map/ppermute | solution.py:327
  136.6 4.4 %collective-permute-start.13 = (f32[136,128]{1,0:T(8,128)S(1)}, f32[136,128]{1,0:T(8,128)S(1)}, u32[]{:S(2)}, u32[]{:S(2)}) collective-permute-start(f32[136,128]{1,0:T(8,128)S(1)} %add_add_fusion.1), channel_id=1, source_target_pairs={{0,16},{4,20},{8,24},{12,28},{16,0},{20,4},{24,8},{28,12},{32,48},... | collective-permute-start | bytes 208904 | tf_op jit(solution)/shard_map/ppermute | solution.py:327
  141.0 4.9 %collective-permute-start.18 = (f32[136,128]{1,0:T(8,128)S(1)}, f32[136,128]{1,0:T(8,128)S(1)}, u32[]{:S(2)}, u32[]{:S(2)}) collective-permute-start(f32[136,128]{1,0:T(8,128)S(1)} %add_add_fusion.t0), channel_id=1, source_target_pairs={{0,12},{4,8},{8,4},{12,0},{16,28},{20,24},{24,20},{28,16},{32,44},... | collective-permute-start | bytes 208904 | tf_op jit(solution)/shard_map/ppermute | solution.py:327
  141.1 8.2 %collective-permute-start.17 = (f32[136,128]{1,0:T(8,128)S(1)}, f32[136,128]{1,0:T(8,128)S(1)}, u32[]{:S(2)}, u32[]{:S(2)}) collective-permute-start(f32[136,128]{1,0:T(8,128)S(1)} %add_add_fusion.t0), channel_id=1, source_target_pairs={{0,8},{4,12},{8,0},{12,4},{16,24},{20,28},{24,16},{28,20},{32,40},... | collective-permute-start | bytes 208904 | tf_op jit(solution)/shard_map/ppermute | solution.py:327
  146.0 3.4 %collective-permute-start.16 = (f32[136,128]{1,0:T(8,128)S(1)}, f32[136,128]{1,0:T(8,128)S(1)}, u32[]{:S(2)}, u32[]{:S(2)}) collective-permute-start(f32[136,128]{1,0:T(8,128)S(1)} %add_add_fusion.t0), channel_id=1, source_target_pairs={{0,4},{4,0},{8,12},{12,8},{16,20},{20,16},{24,28},{28,24},{32,36},... | collective-permute-start | bytes 208904 | tf_op jit(solution)/shard_map/ppermute | solution.py:327

commit v7 on v6

--- a/solution.py
+++ b/solution.py
@@ -349,9 +349,9 @@
 
 
 def sum_over_space(terms):
-    for shift in (4, 2, 0):
-        got = [terms] + [over_space(terms, m << shift) for m in (1, 2, 3)]
-        if shift:
+    for first, second in ((1, 2), (16, 32), (4, 8)):
+        got = [terms] + [over_space(terms, m) for m in (first, second, first ^ second)]
+        if (first, second) != (4, 8):
             terms = (got[0] + got[1]) + (got[2] + got[3])
     return got
 

time: 154 us -> 153 us (level)
  starting transfers between devices: 52.2 us -> 49.5 us
    ppermute x9, starting transfers between devices: 11.8 us -> 9.05 us  [over_space(): return lax.ppermute(block, 'space', route)]
  transfers between devices with their start and end apart: 19 -> 19, of which waited for: 9 -> 10; matrix products, arithmetic and copies ran while one was open for 0% -> 0% of each run, Pallas kernels for 10% -> 11%
where the time goes in v7:
time: 153 us; the launch traced here: 151 us
  waiting for transfers between devices  77 us (50%)
  starting transfers between devices  49.5 us (32%)
  Pallas kernels  22 us (14%)
  local copies, waits for them, and re-layouts  1.74 us (1%)
    ppermute x9, waiting for transfers between devices, from_behind(): return lax.ppermute(block, 'tm', route)  65 us
    ppermute x9, starting transfers between devices, from_behind(): return lax.ppermute(block, 'tm', route)  34.7 us
    ppermute x9, waiting for transfers between devices, over_space(): return lax.ppermute(block, 'space', route)  11.9 us
    pallas_call x3, Pallas kernels, transform(): pl.pallas_call(functools.partial(kernel, pairs), grid=(3,), in_specs=[pl....  11.5 us
    ppermute x9, starting transfers between devices, over_space(): return lax.ppermute(block, 'space', route)  9.05 us
    pallas_call x2, Pallas kernels, gram_terms(): pl.pallas_call(functools.partial(gram_kernel, quads), grid=(count,), in_s...  6.69 us
    ppermute x1, starting transfers between devices, body(): moved = lax.ppermute(edge, ('space', 'tm'), half_block_route())  5.72 us
    pallas_call x1, Pallas kernels, project(): pl.pallas_call(modes_kernel, in_specs=[HELD] * 5, out_specs=[pl.BlockSpec...  3.86 us
  transfers between devices with their start and end apart: 19, of which 10 were waited for; matrix products, arithmetic and copies ran while one was open for 0% of the time, Pallas kernels for 11%

profile of v7, /device:TPU:1, one launch (start us, length us, event | category | flops | bytes accessed | tf_op | source)
XLA Modules:
  0.0 151.2 jit_solution(16606372665225211214)
XLA Ops:
  0.6 1.7 %dynamic-slice_bitcast_fusion = bf16[3,64,768]{2,1,0:T(8,128)(2,1)} fusion(bf16[512,3,768]{2,0,1:T(8,128)(2,1)} %param.5, s32[]{:T(128)S(6)} %select_n.11), kind=kLoop, calls=%fused_computation | loop fusion | bytes 589828 | tf_op jit(solution)/shard_map/dynamic_slice | solution.py:364
  2.3 5.7 %collective-permute-start.3 = (bf16[3,64,768]{2,1,0:T(8,128)(2,1)}, bf16[3,64,768]{2,1,0:T(8,128)(2,1)}, u32[]{:S(2)}, u32[]{:S(2)}) collective-permute-start(bf16[3,64,768]{2,1,0:T(8,128)(2,1)} %dynamic-slice_bitcast_fusion), channel_id=1, source_target_pairs={{1,0},{2,1},{3,2},{4,5},{5,6},{6,7},{7,4},{9,8},{10,9},{11,10},{12... | collective-permute-start | bytes 884744 | tf_op jit(solution)/shard_map/ppermute | solution.py:365
  8.1 0.0 copy-start.4
  8.1 0.0 copy-start.1
  8.1 0.0 copy-start.2
  8.1 0.0 copy-start.3
  8.1 4.7 %transform.3 = (bf16[8,3,16,768]{3,2,1,0:T(8,128)(2,1)}, bf16[8,3,16,768]{3,2,1,0:T(8,128)(2,1)}, bf16[8,3,16,768]{3,2,1,0:T(8,128)(2,1)}, bf16[8,3,16,768]{3,2,1,0:T(8,128)(2,1)}) custom-call(bf16[4,128,320]{2,1,0:T(8,128)(2,1)} %constant.30.clone.band, bf16[3,512,768]{2,1,0:T(8,128)(2,1)} %bitcast.5, bf16[3,512,768]{2,1,0:T(8,128)(2,1)} %bitcast.6), custom_call_target="tpu_custom_call" | custom-call | flops 999999995904 | tf_op jit(solution)/shard_map/transform/pallas_call | solution.py:98
  12.8 4.2 %collective-permute-start = (bf16[8,3,16,768]{3,2,1,0:T(8,128)(2,1)}, bf16[8,3,16,768]{3,2,1,0:T(8,128)(2,1)}, u32[]{:S(2)}, u32[]{:S(2)}) collective-permute-start(bf16[8,3,16,768]{3,2,1,0:T(8,128)(2,1)} %get-tuple-element.21), channel_id=1, source_target_pairs={{0,1},{1,2},{2,3},{3,0},{4,5},{5,6},{6,7},{7,4},{8,9},{9,10},{10,1... | collective-permute-start | bytes 1769480 | tf_op jit(solution)/shard_map/ppermute | solution.py:343
  17.0 1.0 collective-permute-start.1
  18.0 3.5 %collective-permute-start.2 = (bf16[8,3,16,768]{3,2,1,0:T(8,128)(2,1)}, bf16[8,3,16,768]{3,2,1,0:T(8,128)(2,1)}, u32[]{:S(2)}, u32[]{:S(2)}) collective-permute-start(bf16[8,3,16,768]{3,2,1,0:T(8,128)(2,1)} %get-tuple-element.23), channel_id=1, source_target_pairs={{0,3},{1,0},{2,1},{3,2},{4,7},{5,4},{6,5},{7,6},{8,11},{9,8},{10,9... | collective-permute-start | bytes 1769480 | tf_op jit(solution)/shard_map/ppermute | solution.py:343
  21.5 0.0 copy-done.4
  21.5 0.0 collective-permute-done.3.moved
  21.5 0.0 copy-done.1
  21.5 0.0 copy-done.2
  21.5 0.0 copy-done.3
  21.5 3.7 %transform.5 = (bf16[6,3,16,768]{3,2,1,0:T(8,128)(2,1)S(1)}, bf16[6,3,16,768]{3,2,1,0:T(8,128)(2,1)}, bf16[6,3,16,768]{3,2,1,0:T(8,128)(2,1)}, bf16[6,3,16,768]{3,2,1,0:T(8,128)(2,1)}) custom-call(bf16[8,128,384]{2,1,0:T(8,128)(2,1)S(1)} %copy-done.3, bf16[3,512,768]{2,1,0:T(8,128)(2,1)S(1)} %bitcast.7, bf16[3,512,768]{2,1,0:T(8,128)(2,1)S(1)} %bitcast.8, ...), custom_call_target="tpu_custom_call" | custom-call | flops 999999995904 | tf_op jit(solution)/shard_map/transform/pallas_call | solution.py:98
  25.2 6.3 %collective-permute-start.7 = (bf16[6,3,16,768]{3,2,1,0:T(8,128)(2,1)}, bf16[6,3,16,768]{3,2,1,0:T(8,128)(2,1)}, u32[]{:S(2)}, u32[]{:S(2)}) collective-permute-start(bf16[6,3,16,768]{3,2,1,0:T(8,128)(2,1)} %get-tuple-element.29), channel_id=1, source_target_pairs={{0,1},{1,2},{2,3},{3,0},{4,5},{5,6},{6,7},{7,4},{8,9},{9,10},{10,1... | collective-permute-start | bytes 1327112 | tf_op jit(solution)/shard_map/ppermute | solution.py:343
  31.4 4.2 %collective-permute-start.8 = (bf16[6,3,16,768]{3,2,1,0:T(8,128)(2,1)}, bf16[6,3,16,768]{3,2,1,0:T(8,128)(2,1)}, u32[]{:S(2)}, u32[]{:S(2)}) collective-permute-start(bf16[6,3,16,768]{3,2,1,0:T(8,128)(2,1)} %get-tuple-element.30), channel_id=1, source_target_pairs={{0,2},{1,3},{2,0},{3,1},{4,6},{5,7},{6,4},{7,5},{8,10},{9,11},{10,... | collective-permute-start | bytes 1327112 | tf_op jit(solution)/shard_map/ppermute | solution.py:343
  35.6 11.7 %collective-permute-done.refs_1_ = bf16[8,3,16,768]{3,2,1,0:T(8,128)(2,1)} collective-permute-done((bf16[8,3,16,768]{3,2,1,0:T(8,128)(2,1)}, bf16[8,3,16,768]{3,2,1,0:T(8,128)(2,1)}, u32[]{:S(2)}, u32[]{:S(2)}) %collective-permute-start) | collective-permute-done | bytes 589856 | tf_op jit(solution)/shard_map/ppermute | solution.py:343
  47.3 0.0 collective-permute-start.9
  47.3 0.0 copy-start
  47.3 3.2 %transform.4 = (bf16[2,3,16,768]{3,2,1,0:T(8,128)(2,1)S(1)}, bf16[2,3,16,768]{3,2,1,0:T(8,128)(2,1)}, bf16[2,3,16,768]{3,2,1,0:T(8,128)(2,1)}, bf16[2,3,16,768]{3,2,1,0:T(8,128)(2,1)}) custom-call(bf16[8,128,384]{2,1,0:T(8,128)(2,1)S(1)} %copy-done.3, bf16[3,512,768]{2,1,0:T(8,128)(2,1)S(1)} %bitcast.9, bf16[3,512,768]{2,1,0:T(8,128)(2,1)S(1)} %bitcast.10, ...), custom_call_target="tpu_custom_call" | custom-call | flops 999999995904 | tf_op jit(solution)/shard_map/transform/pallas_call | solution.py:98
  50.5 23.7 %collective-permute-done.1.refs_2_ = bf16[8,3,16,768]{3,2,1,0:T(8,128)(2,1)} collective-permute-done((bf16[8,3,16,768]{3,2,1,0:T(8,128)(2,1)}, bf16[8,3,16,768]{3,2,1,0:T(8,128)(2,1)}, u32[]{:S(2)}, u32[]{:S(2)}) %collective-permute-start.1) | collective-permute-done | bytes 589856 | tf_op jit(solution)/shard_map/ppermute | solution.py:343
  74.1 10.4 %collective-permute-start.4 = (bf16[2,3,16,768]{3,2,1,0:T(8,128)(2,1)}, bf16[2,3,16,768]{3,2,1,0:T(8,128)(2,1)}, u32[]{:S(2)}, u32[]{:S(2)}) collective-permute-start(bf16[2,3,16,768]{3,2,1,0:T(8,128)(2,1)} %get-tuple-element.25), channel_id=1, source_target_pairs={{0,1},{1,2},{2,3},{3,0},{4,5},{5,6},{6,7},{7,4},{8,9},{9,10},{10,1... | collective-permute-start | bytes 442376 | tf_op jit(solution)/shard_map/ppermute | solution.py:343
  84.6 25.4 %collective-permute-done.2.refs_3_ = bf16[8,3,16,768]{3,2,1,0:T(8,128)(2,1)} collective-permute-done((bf16[8,3,16,768]{3,2,1,0:T(8,128)(2,1)}, bf16[8,3,16,768]{3,2,1,0:T(8,128)(2,1)}, u32[]{:S(2)}, u32[]{:S(2)}) %collective-permute-start.2) | collective-permute-done | bytes 589856 | tf_op jit(solution)/shard_map/ppermute | solution.py:343
  109.9 4.1 %collective-permute-start.5 = (bf16[2,3,16,768]{3,2,1,0:T(8,128)(2,1)}, bf16[2,3,16,768]{3,2,1,0:T(8,128)(2,1)}, u32[]{:S(2)}, u32[]{:S(2)}) collective-permute-start(bf16[2,3,16,768]{3,2,1,0:T(8,128)(2,1)} %get-tuple-element.26), channel_id=1, source_target_pairs={{0,2},{1,3},{2,0},{3,1},{4,6},{5,7},{6,4},{7,5},{8,10},{9,11},{10,... | collective-permute-start | bytes 442376 | tf_op jit(solution)/shard_map/ppermute | solution.py:343
  114.1 0.0 collective-permute-done.7.refs_5_
  114.1 1.0 collective-permute-start.6
  115.1 0.0 collective-permute-done.8.refs_6_
  115.1 4.3 %collective-permute-done.9.refs_7_ = bf16[6,3,16,768]{3,2,1,0:T(8,128)(2,1)} collective-permute-done((bf16[6,3,16,768]{3,2,1,0:T(8,128)(2,1)}, bf16[6,3,16,768]{3,2,1,0:T(8,128)(2,1)}, u32[]{:S(2)}, u32[]{:S(2)}) %collective-permute-start.9) | collective-permute-done | bytes 442400 | tf_op jit(solution)/shard_map/ppermute | solution.py:343
  119.4 0.0 copy-done
  119.4 4.5 %gram_terms.2 = (f32[136,128]{1,0:T(8,128)S(1)}, bf16[8,3,128,768]{3,2,1,0:T(8,128)(2,1)S(1)}) custom-call(bf16[8,3,16,768]{3,2,1,0:T(8,128)(2,1)S(1)} %copy-done, bf16[8,3,16,768]{3,2,1,0:T(8,128)(2,1)} %collective-permute-done.refs_1_, bf16[8,3,16,768]{3,2,1,0:T(8,128)(2,1)} %collective-permute-done.1.refs_2_, ...), custom_call_target="tpu_custom_call" | custom-call | flops 999999995904 | tf_op jit(solution)/shard_map/gram_terms/pallas_call | solution.py:216
  123.9 0.0 collective-permute-done.4.refs_5_
  123.9 0.0 collective-permute-done.5.refs_6_
  123.9 0.0 collective-permute-done.6.refs_7_
  123.9 2.2 %gram_terms.3 = (f32[136,128]{1,0:T(8,128)S(1)}, bf16[8,3,128,768]{3,2,1,0:T(8,128)(2,1)S(1)}) custom-call(bf16[8,3,16,768]{3,2,1,0:T(8,128)(2,1)S(1)} %copy-done, bf16[8,3,16,768]{3,2,1,0:T(8,128)(2,1)} %collective-permute-done.refs_1_, bf16[8,3,16,768]{3,2,1,0:T(8,128)(2,1)} %collective-permute-done.1.refs_2_, ...), custom_call_target="tpu_custom_call", output_to_operand_aliasing={{1}: (10, {})} | custom-call | tf_op jit(solution)/shard_map/gram_terms/pallas_call | solution.py:216
  126.2 0.1 collective-permute-start.12
  126.3 1.9 %collective-permute-start.11 = (f32[136,128]{1,0:T(8,128)S(1)}, f32[136,128]{1,0:T(8,128)S(1)}, u32[]{:S(2)}, u32[]{:S(2)}) collective-permute-start(f32[136,128]{1,0:T(8,128)S(1)} %get-tuple-element.34), channel_id=1, source_target_pairs={{0,8},{4,12},{8,0},{12,4},{16,24},{20,28},{24,16},{28,20},{32,40},... | collective-permute-start | bytes 208904 | tf_op jit(solution)/shard_map/ppermute | solution.py:327
  128.2 0.2 collective-permute-start.10
  128.4 2.4 %collective-permute-done.12 = f32[136,128]{1,0:T(8,128)S(1)} collective-permute-done((f32[136,128]{1,0:T(8,128)S(1)}, f32[136,128]{1,0:T(8,128)S(1)}, u32[]{:S(2)}, u32[]{:S(2)}) %collective-permute-start.12) | collective-permute-done | bytes 69664 | tf_op jit(solution)/shard_map/ppermute | solution.py:327
  130.8 1.5 collective-permute-done.11
  132.3 0.0 collective-permute-done.10
  132.3 2.6 %collective-permute-start.15 = (f32[136,128]{1,0:T(8,128)S(1)}, f32[136,128]{1,0:T(8,128)S(1)}, u32[]{:S(2)}, u32[]{:S(2)}) collective-permute-start(f32[136,128]{1,0:T(8,128)S(1)} %add_add_fusion.1), channel_id=1, source_target_pairs={{0,192},{4,196},{8,200},{12,204},{16,208},{20,212},{24,216},{28,22... | collective-permute-start | bytes 208904 | tf_op jit(solution)/shard_map/ppermute | solution.py:327
  134.9 0.5 collective-permute-start.14
  135.4 0.3 collective-permute-start.13
  135.7 1.1 collective-permute-done.15
  136.8 2.8 %collective-permute-done.14 = f32[136,128]{1,0:T(8,128)S(1)} collective-permute-done((f32[136,128]{1,0:T(8,128)S(1)}, f32[136,128]{1,0:T(8,128)S(1)}, u32[]{:S(2)}, u32[]{:S(2)}) %collective-permute-start.14) | collective-permute-done | bytes 69664 | tf_op jit(solution)/shard_map/ppermute | solution.py:327
  139.6 0.0 collective-permute-done.13
  139.6 2.8 %collective-permute-start.18 = (f32[136,128]{1,0:T(8,128)S(1)}, f32[136,128]{1,0:T(8,128)S(1)}, u32[]{:S(2)}, u32[]{:S(2)}) collective-permute-start(f32[136,128]{1,0:T(8,128)S(1)} %add_add_fusion.t0), channel_id=1, source_target_pairs={{0,48},{4,52},{8,56},{12,60},{16,32},{20,36},{24,40},{28,44},{32,1... | collective-permute-start | bytes 208904 | tf_op jit(solution)/shard_map/ppermute | solution.py:327
  142.4 0.4 collective-permute-start.17
  142.8 0.3 collective-permute-start.16
  143.1 1.3 collective-permute-done.18.t3
  144.4 2.8 %collective-permute-done.17.t2 = f32[136,128]{1,0:T(8,128)S(1)} collective-permute-done((f32[136,128]{1,0:T(8,128)S(1)}, f32[136,128]{1,0:T(8,128)S(1)}, u32[]{:S(2)}, u32[]{:S(2)}) %collective-permute-start.17) | collective-permute-done | bytes 69664 | tf_op jit(solution)/shard_map/ppermute | solution.py:327
  147.2 0.0 collective-permute-done.16.t1
  147.2 3.9 %modes.1 = (f32[16,2,32,32]{3,2,1,0:T(8,128)}, bf16[16,2,3,32,768]{4,3,2,1,0:T(8,128)(2,1)}) custom-call(f32[136,128]{1,0:T(8,128)S(1)} %add_add_fusion.t0, f32[136,128]{1,0:T(8,128)S(1)} %collective-permute-done.16.t1, f32[136,128]{1,0:T(8,128)S(1)} %collective-permute-done.17.t2, f32[136,128]{1,0:T(8,128)S(1)} %collective-permute-done.18.t3, ...), custom_call_target="tpu_custom_call" | custom-call | tf_op jit(solution)/shard_map/modes/pallas_call | solution.py:309
  (3 shorter events, 0.0 us)
Async XLA Ops:
  2.3 19.1 %collective-permute-start.3 = (bf16[3,64,768]{2,1,0:T(8,128)(2,1)}, bf16[3,64,768]{2,1,0:T(8,128)(2,1)}, u32[]{:S(2)}, u32[]{:S(2)}) collective-permute-start(bf16[3,64,768]{2,1,0:T(8,128)(2,1)} %dynamic-slice_bitcast_fusion), channel_id=1, source_target_pairs={{1,0},{2,1},{3,2},{4,5},{5,6},{6,7},{7,4},{9,8},{10,9},{11,10},{12... | collective-permute-start | bytes 884744 | tf_op jit(solution)/shard_map/ppermute | solution.py:365
  8.1 13.4 %copy-start.4 = (f32[768]{0:T(1024)S(1)}, f32[768]{0:T(1024)}, u32[]{:S(2)}) copy-start(f32[768]{0:T(1024)} %param.7) | copy-start | bytes 9220
  8.1 13.4 %copy-start.1 = (bf16[512,3,768]{2,0,1:T(8,128)(2,1)S(1)}, bf16[512,3,768]{2,0,1:T(8,128)(2,1)}, u32[]{:S(2)}) copy-start(bf16[512,3,768]{2,0,1:T(8,128)(2,1)} %param.5) | copy-start | bytes 7077892
  8.1 13.4 %copy-start.2 = (bf16[64,3,768]{2,0,1:T(8,128)(2,1)S(1)}, bf16[64,3,768]{2,0,1:T(8,128)(2,1)}, u32[]{:S(2)}) copy-start(bf16[64,3,768]{2,0,1:T(8,128)(2,1)} %param.6) | copy-start | bytes 884740
  8.1 13.4 %copy-start.3 = (bf16[8,128,384]{2,1,0:T(8,128)(2,1)S(1)}, bf16[8,128,384]{2,1,0:T(8,128)(2,1)}, u32[]{:S(2)}) copy-start(bf16[8,128,384]{2,1,0:T(8,128)(2,1)} %constant.31.clone.band) | copy-start | bytes 2359300
  12.8 34.5 %collective-permute-start = (bf16[8,3,16,768]{3,2,1,0:T(8,128)(2,1)}, bf16[8,3,16,768]{3,2,1,0:T(8,128)(2,1)}, u32[]{:S(2)}, u32[]{:S(2)}) collective-permute-start(bf16[8,3,16,768]{3,2,1,0:T(8,128)(2,1)} %get-tuple-element.21), channel_id=1, source_target_pairs={{0,1},{1,2},{2,3},{3,0},{4,5},{5,6},{6,7},{7,4},{8,9},{9,10},{10,1... | collective-permute-start | bytes 1769480 | tf_op jit(solution)/shard_map/ppermute | solution.py:343
  17.0 57.2 %collective-permute-start.1 = (bf16[8,3,16,768]{3,2,1,0:T(8,128)(2,1)}, bf16[8,3,16,768]{3,2,1,0:T(8,128)(2,1)}, u32[]{:S(2)}, u32[]{:S(2)}) collective-permute-start(bf16[8,3,16,768]{3,2,1,0:T(8,128)(2,1)} %get-tuple-element.22), channel_id=1, source_target_pairs={{0,2},{1,3},{2,0},{3,1},{4,6},{5,7},{6,4},{7,5},{8,10},{9,11},{10,... | collective-permute-start | bytes 1769480 | tf_op jit(solution)/shard_map/ppermute | solution.py:343
  18.0 92.0 %collective-permute-start.2 = (bf16[8,3,16,768]{3,2,1,0:T(8,128)(2,1)}, bf16[8,3,16,768]{3,2,1,0:T(8,128)(2,1)}, u32[]{:S(2)}, u32[]{:S(2)}) collective-permute-start(bf16[8,3,16,768]{3,2,1,0:T(8,128)(2,1)} %get-tuple-element.23), channel_id=1, source_target_pairs={{0,3},{1,0},{2,1},{3,2},{4,7},{5,4},{6,5},{7,6},{8,11},{9,8},{10,9... | collective-permute-start | bytes 1769480 | tf_op jit(solution)/shard_map/ppermute | solution.py:343
  25.2 88.9 %collective-permute-start.7 = (bf16[6,3,16,768]{3,2,1,0:T(8,128)(2,1)}, bf16[6,3,16,768]{3,2,1,0:T(8,128)(2,1)}, u32[]{:S(2)}, u32[]{:S(2)}) collective-permute-start(bf16[6,3,16,768]{3,2,1,0:T(8,128)(2,1)} %get-tuple-element.29), channel_id=1, source_target_pairs={{0,1},{1,2},{2,3},{3,0},{4,5},{5,6},{6,7},{7,4},{8,9},{9,10},{10,1... | collective-permute-start | bytes 1327112 | tf_op jit(solution)/shard_map/ppermute | solution.py:343
  31.4 83.7 %collective-permute-start.8 = (bf16[6,3,16,768]{3,2,1,0:T(8,128)(2,1)}, bf16[6,3,16,768]{3,2,1,0:T(8,128)(2,1)}, u32[]{:S(2)}, u32[]{:S(2)}) collective-permute-start(bf16[6,3,16,768]{3,2,1,0:T(8,128)(2,1)} %get-tuple-element.30), channel_id=1, source_target_pairs={{0,2},{1,3},{2,0},{3,1},{4,6},{5,7},{6,4},{7,5},{8,10},{9,11},{10,... | collective-permute-start | bytes 1327112 | tf_op jit(solution)/shard_map/ppermute | solution.py:343
  47.3 72.1 %collective-permute-start.9 = (bf16[6,3,16,768]{3,2,1,0:T(8,128)(2,1)}, bf16[6,3,16,768]{3,2,1,0:T(8,128)(2,1)}, u32[]{:S(2)}, u32[]{:S(2)}) collective-permute-start(bf16[6,3,16,768]{3,2,1,0:T(8,128)(2,1)} %get-tuple-element.31), channel_id=1, source_target_pairs={{0,3},{1,0},{2,1},{3,2},{4,7},{5,4},{6,5},{7,6},{8,11},{9,8},{10,9... | collective-permute-start | bytes 1327112 | tf_op jit(solution)/shard_map/ppermute | solution.py:343
  47.3 72.1 %copy-start = (bf16[8,3,16,768]{3,2,1,0:T(8,128)(2,1)S(1)}, bf16[8,3,16,768]{3,2,1,0:T(8,128)(2,1)}, u32[]{:S(2)}) copy-start(bf16[8,3,16,768]{3,2,1,0:T(8,128)(2,1)} %get-tuple-element.20.refs_0_) | copy-start | bytes 1769476
  74.1 49.8 %collective-permute-start.4 = (bf16[2,3,16,768]{3,2,1,0:T(8,128)(2,1)}, bf16[2,3,16,768]{3,2,1,0:T(8,128)(2,1)}, u32[]{:S(2)}, u32[]{:S(2)}) collective-permute-start(bf16[2,3,16,768]{3,2,1,0:T(8,128)(2,1)} %get-tuple-element.25), channel_id=1, source_target_pairs={{0,1},{1,2},{2,3},{3,0},{4,5},{5,6},{6,7},{7,4},{8,9},{9,10},{10,1... | collective-permute-start | bytes 442376 | tf_op jit(solution)/shard_map/ppermute | solution.py:343
  109.9 14.0 %collective-permute-start.5 = (bf16[2,3,16,768]{3,2,1,0:T(8,128)(2,1)}, bf16[2,3,16,768]{3,2,1,0:T(8,128)(2,1)}, u32[]{:S(2)}, u32[]{:S(2)}) collective-permute-start(bf16[2,3,16,768]{3,2,1,0:T(8,128)(2,1)} %get-tuple-element.26), channel_id=1, source_target_pairs={{0,2},{1,3},{2,0},{3,1},{4,6},{5,7},{6,4},{7,5},{8,10},{9,11},{10,... | collective-permute-start | bytes 442376 | tf_op jit(solution)/shard_map/ppermute | solution.py:343
  114.1 9.9 %collective-permute-start.6 = (bf16[2,3,16,768]{3,2,1,0:T(8,128)(2,1)}, bf16[2,3,16,768]{3,2,1,0:T(8,128)(2,1)}, u32[]{:S(2)}, u32[]{:S(2)}) collective-permute-start(bf16[2,3,16,768]{3,2,1,0:T(8,128)(2,1)} %get-tuple-element.27), channel_id=1, source_target_pairs={{0,3},{1,0},{2,1},{3,2},{4,7},{5,4},{6,5},{7,6},{8,11},{9,8},{10,9... | collective-permute-start | bytes 442376 | tf_op jit(solution)/shard_map/ppermute | solution.py:343
  126.2 4.7 %collective-permute-start.12 = (f32[136,128]{1,0:T(8,128)S(1)}, f32[136,128]{1,0:T(8,128)S(1)}, u32[]{:S(2)}, u32[]{:S(2)}) collective-permute-start(f32[136,128]{1,0:T(8,128)S(1)} %get-tuple-element.34), channel_id=1, source_target_pairs={{0,12},{4,8},{8,4},{12,0},{16,28},{20,24},{24,20},{28,16},{32,44},... | collective-permute-start | bytes 208904 | tf_op jit(solution)/shard_map/ppermute | solution.py:327
  126.3 6.0 %collective-permute-start.11 = (f32[136,128]{1,0:T(8,128)S(1)}, f32[136,128]{1,0:T(8,128)S(1)}, u32[]{:S(2)}, u32[]{:S(2)}) collective-permute-start(f32[136,128]{1,0:T(8,128)S(1)} %get-tuple-element.34), channel_id=1, source_target_pairs={{0,8},{4,12},{8,0},{12,4},{16,24},{20,28},{24,16},{28,20},{32,40},... | collective-permute-start | bytes 208904 | tf_op jit(solution)/shard_map/ppermute | solution.py:327
  128.2 4.1 %collective-permute-start.10 = (f32[136,128]{1,0:T(8,128)S(1)}, f32[136,128]{1,0:T(8,128)S(1)}, u32[]{:S(2)}, u32[]{:S(2)}) collective-permute-start(f32[136,128]{1,0:T(8,128)S(1)} %get-tuple-element.34), channel_id=1, source_target_pairs={{0,4},{4,0},{8,12},{12,8},{16,20},{20,16},{24,28},{28,24},{32,36},... | collective-permute-start | bytes 208904 | tf_op jit(solution)/shard_map/ppermute | solution.py:327
  132.3 4.5 %collective-permute-start.15 = (f32[136,128]{1,0:T(8,128)S(1)}, f32[136,128]{1,0:T(8,128)S(1)}, u32[]{:S(2)}, u32[]{:S(2)}) collective-permute-start(f32[136,128]{1,0:T(8,128)S(1)} %add_add_fusion.1), channel_id=1, source_target_pairs={{0,192},{4,196},{8,200},{12,204},{16,208},{20,212},{24,216},{28,22... | collective-permute-start | bytes 208904 | tf_op jit(solution)/shard_map/ppermute | solution.py:327
  134.9 4.7 %collective-permute-start.14 = (f32[136,128]{1,0:T(8,128)S(1)}, f32[136,128]{1,0:T(8,128)S(1)}, u32[]{:S(2)}, u32[]{:S(2)}) collective-permute-start(f32[136,128]{1,0:T(8,128)S(1)} %add_add_fusion.1), channel_id=1, source_target_pairs={{0,128},{4,132},{8,136},{12,140},{16,144},{20,148},{24,152},{28,15... | collective-permute-start | bytes 208904 | tf_op jit(solution)/shard_map/ppermute | solution.py:327
  135.4 4.1 %collective-permute-start.13 = (f32[136,128]{1,0:T(8,128)S(1)}, f32[136,128]{1,0:T(8,128)S(1)}, u32[]{:S(2)}, u32[]{:S(2)}) collective-permute-start(f32[136,128]{1,0:T(8,128)S(1)} %add_add_fusion.1), channel_id=1, source_target_pairs={{0,64},{4,68},{8,72},{12,76},{16,80},{20,84},{24,88},{28,92},{32,9... | collective-permute-start | bytes 208904 | tf_op jit(solution)/shard_map/ppermute | solution.py:327
  139.6 4.8 %collective-permute-start.18 = (f32[136,128]{1,0:T(8,128)S(1)}, f32[136,128]{1,0:T(8,128)S(1)}, u32[]{:S(2)}, u32[]{:S(2)}) collective-permute-start(f32[136,128]{1,0:T(8,128)S(1)} %add_add_fusion.t0), channel_id=1, source_target_pairs={{0,48},{4,52},{8,56},{12,60},{16,32},{20,36},{24,40},{28,44},{32,1... | collective-permute-start | bytes 208904 | tf_op jit(solution)/shard_map/ppermute | solution.py:327
  142.4 4.8 %collective-permute-start.17 = (f32[136,128]{1,0:T(8,128)S(1)}, f32[136,128]{1,0:T(8,128)S(1)}, u32[]{:S(2)}, u32[]{:S(2)}) collective-permute-start(f32[136,128]{1,0:T(8,128)S(1)} %add_add_fusion.t0), channel_id=1, source_target_pairs={{0,32},{4,36},{8,40},{12,44},{16,48},{20,52},{24,56},{28,60},{32,0... | collective-permute-start | bytes 208904 | tf_op jit(solution)/shard_map/ppermute | solution.py:327
  142.8 4.4 %collective-permute-start.16 = (f32[136,128]{1,0:T(8,128)S(1)}, f32[136,128]{1,0:T(8,128)S(1)}, u32[]{:S(2)}, u32[]{:S(2)}) collective-permute-start(f32[136,128]{1,0:T(8,128)S(1)} %add_add_fusion.t0), channel_id=1, source_target_pairs={{0,16},{4,20},{8,24},{12,28},{16,0},{20,4},{24,8},{28,12},{32,48},... | collective-permute-start | bytes 208904 | tf_op jit(solution)/shard_map/ppermute | solution.py:327
